TPU v7x, 32 devices: a whole 2x2x4 slice. The times are simulated.
32 devices in a mesh: section: 2 (over x), batch: 16 (over z, y, core).
Axes of the slice: x: 2, y: 2, z: 4, core: 2. Of those that a mesh axis runs over, the one named last changes fastest.
Arguments:
- tokens: bfloat16 [16384, 768], P('batch'), may hold values from -6 to 6
- cotangent: bfloat16 [16384, 768], P('batch'), may hold values from -6 to 6
- loss_weight: float32 [32], P('batch'), may hold values from 0.25 to 4
- timesteps: int32 [32], P('batch'), may hold values from 0 to 999, as said below
- owners: int32 [2, 432], P('section'), may hold values from 0 to 15, as said below
- master: float32 [2, 496, 32, 768], P('section', 'batch'), as said below
- first_moment: float32 [2, 496, 32, 768], P('section', 'batch'), as said below
- second_moment: float32 [2, 496, 32, 768], P('section', 'batch'), as said below
Outputs:
- block_outputs: bfloat16 [2, 16384, 768], P('section', 'batch')
- input_grads: float32 [2, 16384, 768], P('section', 'batch')
- master_new: float32 [2, 496, 32, 768], P('section', 'batch')
- first_new: float32 [2, 496, 32, 768], P('section', 'batch')
- second_new: float32 [2, 496, 32, 768], P('section', 'batch')
- copies_new: bfloat16 [2, 496, 32, 768], P('section', 'batch')
Inputs may be any that keep to these rules, and one draw needn't show every extreme that they name: `timesteps`: larger timestep indices are more common. `owners`: each owner holds at most 31 panels of a block; in every section some owner holds exactly 31. `master`: owner o's k-th panel (in panel order) sits in slot o * 31 + k; slots that hold no panel are zero. `first_moment`: same slots as master; slots that hold no panel are zero. `second_moment`: same slots as master; positive where a panel sits, zero elsewhere.
All inputs are finite; a program needn't handle non-finite values.
Results may differ from a plain program's by a relative error of at most 0.017.
The roundings to bfloat16 on the way count: a program that leaves them out, or rounds other values in their place, can miss the bound.
Values may be sent and summed in bfloat16 or wider, within the bound.
No kernel may reach another device: no remote copies, remote signals or barrier semaphores. Data moves between devices by JAX's collectives and lax.ppermute only.
A program may use at most 448 MiB of HBM per device.

v0:
```python
import math

import jax
import jax.numpy as jnp
from jax import lax
from jax.sharding import PartitionSpec as P

D = 768
HEADS = 12
HEAD_DIM = 64
FF = 3072
STEP = 10


norm_eps = 1e-06
adam_eps = 1e-08
learn_rate = 0.03
decay_rate = 0.1
beta_one = 0.5
beta_two = 0.5


def from_behind(value, axis, steps):
    count = lax.axis_size(axis)
    initial, last = (max(0, -steps), min(count, count - steps))
    return lax.ppermute(value, axis, [(source, source + steps) for source in range(initial, last)])


def panel_slots(owner_row, slot_count, owner_count):
    onehot = (owner_row[:, None] == jnp.arange(owner_count, dtype=jnp.int32)[None, :]).astype(
        jnp.int32
    )
    earlier = jnp.cumsum(onehot, axis=0) - onehot
    rank_in_owner = jnp.sum(earlier * onehot, axis=1)
    return owner_row * slot_count + rank_in_owner


def time_features(steps_in):
    half_width = D // 2
    freqs = jnp.exp(-math.log(10000.0) * jnp.arange(half_width, dtype=jnp.float32) / half_width)
    angles = steps_in.astype(jnp.float32)[:, None] * freqs[None, :]
    return jnp.concatenate([jnp.cos(angles), jnp.sin(angles)], axis=1)


def layer_norm(values_in):
    average = jnp.mean(values_in, axis=-1, keepdims=True)
    centred = values_in - average
    variance = jnp.mean(centred * centred, axis=-1, keepdims=True)
    return centred * lax.rsqrt(variance + norm_eps)


def modulate(values_in, shift_row, scale_row):
    return layer_norm(values_in) * (1.0 + scale_row) + shift_row


def split_parts(sheet):
    return (
        sheet[: 3 * D],
        sheet[3 * D : 4 * D],
        sheet[4 * D : 4 * D + FF],
        sheet[4 * D + FF : 4 * D + 2 * FF],
        sheet[4 * D + 2 * FF :],
    )


def attend(projected):
    length = projected.shape[0]
    shaped = projected.reshape(length, 3, HEADS, HEAD_DIM)
    query_heads = shaped[:, 0]
    key_heads = shaped[:, 1]
    value_heads = shaped[:, 2]
    score_scale = HEAD_DIM ** (-0.5)
    scores = (
        jnp.einsum("qhd,khd->hqk", query_heads, key_heads, preferred_element_type=jnp.float32)
        * score_scale
    )
    top_score = jnp.max(scores, axis=-1, keepdims=True)
    log_sum = top_score + jnp.log(jnp.sum(jnp.exp(scores - top_score), axis=-1, keepdims=True))
    soft_weights = jnp.exp(scores - log_sum).astype(jnp.bfloat16)
    results = jnp.einsum(
        "hqk,khd->qhd", soft_weights, value_heads, preferred_element_type=jnp.float32
    ).astype(jnp.bfloat16)
    mixed = results.reshape(length, HEADS * HEAD_DIM)
    return (mixed, log_sum)


def attend_back(projected, log_sums, grad_mixed):
    length = projected.shape[0]
    shaped = projected.reshape(length, 3, HEADS, HEAD_DIM)
    query_heads = shaped[:, 0]
    key_heads = shaped[:, 1]
    value_heads = shaped[:, 2]
    grad_heads = grad_mixed.reshape(length, HEADS, HEAD_DIM)
    score_scale = HEAD_DIM ** (-0.5)
    scores = (
        jnp.einsum("qhd,khd->hqk", query_heads, key_heads, preferred_element_type=jnp.float32)
        * score_scale
    )
    soft_weights = jnp.exp(scores - log_sums)
    grad_soft = jnp.einsum(
        "qhd,khd->hqk", grad_heads, value_heads, preferred_element_type=jnp.float32
    )
    grad_values = jnp.einsum(
        "hqk,qhd->khd",
        soft_weights.astype(jnp.bfloat16),
        grad_heads,
        preferred_element_type=jnp.float32,
    )
    grad_scores = soft_weights * (
        grad_soft - jnp.sum(grad_soft * soft_weights, axis=-1, keepdims=True)
    )
    grad_raw = (grad_scores * score_scale).astype(jnp.bfloat16)
    grad_queries = jnp.einsum(
        "hqk,khd->qhd", grad_raw, key_heads, preferred_element_type=jnp.float32
    )
    grad_keys = jnp.einsum(
        "hqk,qhd->khd", grad_raw, query_heads, preferred_element_type=jnp.float32
    )
    merged = jnp.concatenate([grad_queries, grad_keys, grad_values], axis=1)
    return merged.reshape(length, 3 * HEADS * HEAD_DIM).astype(jnp.bfloat16)


def forward_clip(inputs, cond_row, weight_parts):
    qkv_weight, proj_weight, up_weight, down_weight, mod_weight = weight_parts
    modulation = jnp.einsum("sd,ed->se", cond_row, mod_weight, preferred_element_type=jnp.float32)[
        0
    ]
    pieces = jnp.split(modulation, 6)
    hidden_one = modulate(inputs, pieces[0], pieces[1]).astype(jnp.bfloat16)
    projected = jnp.einsum(
        "td,ed->te", hidden_one, qkv_weight, preferred_element_type=jnp.float32
    ).astype(jnp.bfloat16)
    mixed, log_sums = attend(projected)
    branch = jnp.einsum("td,ed->te", mixed, proj_weight, preferred_element_type=jnp.float32)
    middle = inputs + pieces[2] * branch
    hidden_two = modulate(middle, pieces[3], pieces[4]).astype(jnp.bfloat16)
    upward = jnp.einsum("td,fd->tf", hidden_two, up_weight, preferred_element_type=jnp.float32)
    activated = jax.nn.gelu(upward).astype(jnp.bfloat16)
    branch_two = jnp.dot(activated, down_weight, preferred_element_type=jnp.float32)
    output = middle + pieces[5] * branch_two
    return (
        output,
        (
            inputs,
            modulation,
            hidden_one,
            projected,
            log_sums,
            mixed,
            branch,
            middle,
            hidden_two,
            upward,
            activated,
            branch_two,
        ),
    )


def backward_inputs(kept_state, upstream, cond_row, weight_parts):
    qkv_weight, proj_weight, up_weight, down_weight, mod_weight = weight_parts
    (
        inputs,
        modulation,
        hidden_one,
        projected,
        log_sums,
        mixed,
        branch,
        middle,
        hidden_two,
        upward,
        activated,
        branch_two,
    ) = kept_state
    pieces = jnp.split(modulation, 6)
    grad_branch_two = (pieces[5] * upstream).astype(jnp.bfloat16)
    grad_gate_two = jnp.sum(upstream * branch_two, axis=0)
    grad_activated = jnp.einsum(
        "td,fd->tf", grad_branch_two, down_weight, preferred_element_type=jnp.float32
    )
    unused_value, gelu_back = jax.vjp(jax.nn.gelu, upward)
    grad_upward = gelu_back(grad_activated)[0].astype(jnp.bfloat16)
    grad_hidden_two = jnp.einsum(
        "tf,fd->td", grad_upward, up_weight, preferred_element_type=jnp.float32
    )
    unused_second, modulate_two = jax.vjp(modulate, middle, pieces[3], pieces[4])
    grad_middle_norm, grad_shift_two, grad_scale_two = modulate_two(grad_hidden_two)
    grad_middle = upstream + grad_middle_norm
    grad_branch = (pieces[2] * grad_middle).astype(jnp.bfloat16)
    grad_gate_one = jnp.sum(grad_middle * branch, axis=0)
    grad_mixed = jnp.einsum(
        "te,ed->td", grad_branch, proj_weight, preferred_element_type=jnp.float32
    ).astype(jnp.bfloat16)
    grad_projected = attend_back(projected, log_sums, grad_mixed)
    grad_hidden_one = jnp.einsum(
        "te,ed->td", grad_projected, qkv_weight, preferred_element_type=jnp.float32
    )
    unused_first, modulate_one = jax.vjp(modulate, inputs, pieces[0], pieces[1])
    grad_inputs_norm, grad_shift_one, grad_scale_one = modulate_one(grad_hidden_one)
    grad_inputs = grad_middle + grad_inputs_norm
    grad_modulation = jnp.concatenate(
        [
            grad_shift_one,
            grad_scale_one,
            grad_gate_one,
            grad_shift_two,
            grad_scale_two,
            grad_gate_two,
        ]
    ).astype(jnp.bfloat16)[None, :]
    weight_inputs = (
        activated,
        grad_branch_two,
        grad_upward,
        hidden_two,
        grad_branch,
        mixed,
        grad_projected,
        hidden_one,
        grad_modulation,
        cond_row,
    )
    return (grad_inputs, weight_inputs)


def weight_grads(weight_inputs):
    (
        activated,
        grad_branch_two,
        grad_upward,
        hidden_two,
        grad_branch,
        mixed,
        grad_projected,
        hidden_one,
        grad_modulation,
        cond_row,
    ) = weight_inputs
    grad_down = jnp.einsum(
        "tf,td->fd", activated, grad_branch_two, preferred_element_type=jnp.float32
    )
    grad_up = jnp.einsum("tf,td->fd", grad_upward, hidden_two, preferred_element_type=jnp.float32)
    grad_proj = jnp.einsum("te,td->ed", grad_branch, mixed, preferred_element_type=jnp.float32)
    grad_qkv = jnp.einsum(
        "te,td->ed", grad_projected, hidden_one, preferred_element_type=jnp.float32
    )
    grad_mod = jnp.einsum(
        "se,sd->ed", grad_modulation, cond_row, preferred_element_type=jnp.float32
    )
    return jnp.concatenate([grad_qkv, grad_proj, grad_up, grad_down, grad_mod], axis=0)


def slot_terms(grad_sheet, slot_panel, panel_rows):
    grad_panels = grad_sheet.reshape(-1, panel_rows, grad_sheet.shape[1])
    picked = grad_panels[jnp.maximum(slot_panel, 0)]
    return jnp.where((slot_panel >= 0)[:, None, None], picked, 0.0)


def add_sheet(totals, grad_sheet):
    grad_total, share_total = totals
    grad_total = grad_total + grad_sheet
    return (grad_total, share_total)


def body(tokens, cotangent, loss_weight, timesteps, owners, master, first_moment, second_moment):
    section_index = lax.axis_index("section")
    owner_total = lax.axis_size("batch")
    slot_count = master.shape[1]
    panel_rows = master.shape[2]
    micro_count = timesteps.shape[0]
    clip_rows = tokens.shape[0] // micro_count
    slot_index = panel_slots(owners[0], slot_count, owner_total)
    everything = lax.all_gather(master[0].astype(jnp.bfloat16), "batch", axis=0, tiled=True)
    sheet = everything[slot_index].reshape(-1, D)
    weight_parts = split_parts(sheet)
    conditions = jax.nn.silu(time_features(timesteps)).astype(jnp.bfloat16)
    received = jnp.zeros((clip_rows, D), jnp.bfloat16)
    sent_list = []
    kept_list = []
    for tick_index in range(micro_count + 1):
        own_batch = min(tick_index, micro_count - 1)
        first_rows = tokens[own_batch * clip_rows : (own_batch + 1) * clip_rows]
        current = jnp.where(section_index == 0, first_rows, received)
        batch_index = jnp.clip(tick_index - section_index, 0, micro_count - 1)
        cond_row = lax.dynamic_slice_in_dim(conditions, batch_index, 1, 0)
        output, kept_state = forward_clip(current.astype(jnp.float32), cond_row, weight_parts)
        sent_rows = output.astype(jnp.bfloat16)
        sent_list.append(sent_rows)
        kept_list.append(kept_state + (cond_row,))
        if tick_index < micro_count:
            received = from_behind(sent_rows, "section", 1)
    kept_stack = jax.tree.map(lambda *leaves: jnp.stack(leaves), *kept_list)
    slot_panel = (
        jnp.full((owner_total * slot_count,), -1, jnp.int32)
        .at[slot_index]
        .set(jnp.arange(slot_index.shape[0], dtype=jnp.int32))
    )
    totals = (jnp.zeros((sheet.shape[0], D), jnp.float32), jnp.zeros(master.shape[1:], jnp.float32))
    received_grad = jnp.zeros((clip_rows, D), jnp.bfloat16)
    grad_list = []
    for tick_index in range(micro_count + 1):
        batch_raw = tick_index - 1 + section_index
        is_valid = (batch_raw >= 0) & (batch_raw < micro_count)
        own_batch = min(tick_index, micro_count - 1)
        last_rows = (
            cotangent[own_batch * clip_rows : (own_batch + 1) * clip_rows].astype(jnp.float32)
            * loss_weight[own_batch]
        )
        upstream = jnp.where(section_index == 1, last_rows, received_grad.astype(jnp.float32))
        forward_tick = jnp.clip(tick_index - 1 + 2 * section_index, 0, micro_count)
        picked_state = jax.tree.map(lambda stacked: stacked[forward_tick], kept_stack)
        cond_row = picked_state[-1]
        kept_state = picked_state[:-1]
        grad_inputs, weight_inputs = backward_inputs(kept_state, upstream, cond_row, weight_parts)
        grad_list.append(grad_inputs)
        totals = add_sheet(totals, jnp.where(is_valid, weight_grads(weight_inputs), 0.0))
        if tick_index < micro_count:
            received_grad = from_behind(grad_inputs.astype(jnp.bfloat16), "section", -1)
    grad_total, share_total = totals
    share_total = lax.psum_scatter(
        slot_terms(grad_total, slot_panel, panel_rows), "batch", scatter_dimension=0, tiled=True
    )
    block_rows = jnp.concatenate(
        [
            jnp.where(section_index == 0, sent_list[number], sent_list[number + 1])
            for number in range(micro_count)
        ],
        axis=0,
    )
    grad_rows = jnp.concatenate(
        [
            jnp.where(section_index == 0, grad_list[number + 1], grad_list[number])
            for number in range(micro_count)
        ],
        axis=0,
    )
    first_next = beta_one * first_moment[0] + (1.0 - beta_one) * share_total
    second_next = beta_two * second_moment[0] + (1.0 - beta_two) * share_total * share_total
    first_hat = first_next / (1.0 - beta_one**STEP)
    second_hat = second_next / (1.0 - beta_two**STEP)
    master_next = master[0] - learn_rate * (
        first_hat / (jnp.sqrt(second_hat) + adam_eps) + decay_rate * master[0]
    )
    return (
        block_rows[None],
        grad_rows[None],
        master_next[None],
        first_next[None],
        second_next[None],
        master_next.astype(jnp.bfloat16)[None],
    )


def solution(mesh):
    placed = (
        P("batch", None),
        P("batch", None),
        P("batch"),
        P("batch"),
        P("section", None),
        P("section", "batch", None, None),
        P("section", "batch", None, None),
        P("section", "batch", None, None),
    )
    return jax.shard_map(
        body,
        mesh=mesh,
        in_specs=placed,
        out_specs=(
            P("section", "batch", None),
            P("section", "batch", None),
            P("section", "batch", None, None),
            P("section", "batch", None, None),
            P("section", "batch", None, None),
            P("section", "batch", None, None),
        ),
        check_vma=False,
    )
```

profile of v0, /device:TPU:1, one launch (start us, length us, event | category | flops | bytes accessed | tf_op | source)
XLA Modules:
  0.0 1331.9 jit_solution(17373236587991073479)
XLA Ops:
  18.5 119.7 %all-gather.2.cloned.1.call-done = bf16[496,32,768]{2,1,0:T(8,128)(2,1)} async-done(((bf16[31,32,768]{2,1,0:T(8,128)(2,1)}), bf16[496,32,768]{2,1,0:T(8,128)(2,1)}) %all-gather.2.cloned.1.call-update) | async-done | bytes 24379408 | tf_op jit(solution)/shard_map/all_gather | solution.py:274
  138.1 23.3 %gather_fusion = bf16[432,32,768]{2,1,0:T(8,128)(2,1)} fusion(bf16[496,32,768]{2,1,0:T(8,128)(2,1)} %all-gather.2.cloned.1.call-done, s32[1024]{0:T(1024)S(1)} %pad_clamp_fusion.1), kind=kCustom, calls=%fused_computation | custom fusion | bytes 42469056 | tf_op jit(solution)/shard_map/gather | solution.py:275
  161.5 3.6 slice.172
  165.1 4.0 slice.173
  171.5 8.2 fusion.353
  189.2 4.5 copy.66
  199.1 3.7 fusion.182
  205.5 4.9 fusion.330
  210.4 3.7 fusion.342
  215.6 13.0 collective-permute-start
  229.5 6.1 collective-permute-done
  241.5 4.3 copy.68
  251.1 3.7 fusion.181
  258.1 5.0 fusion.332
  264.6 5.0 broadcast_select_fusion.3
  269.6 4.1 collective-permute-start.1
  273.8 5.8 fusion.338
  279.6 9.8 collective-permute-done.1
  295.9 4.3 copy.70
  305.6 4.1 fusion.180
  324.3 6.8 pad_maximum_fusion
  331.2 9.4 fusion.45
  350.3 3.9 pad_maximum_fusion.2
  357.3 4.3 copy.72
  365.6 8.0 fusion.224
  376.7 19.9 %fusion.201 = bf16[512,12,64]{0,2,1:T(8,128)(2,1)} fusion(f32[12,512,512]{1,2,0:T(8,128)} %fusion.224, f32[12,512,512]{1,2,0:T(8,128)} %copy-done.2, f32[12,512]{1,0:T(8,128)S(1)} %get-tuple-element.103, bf16[512,3,12,64]{0,3,2,1:T(8,128)(2,1)} %bitcast.501), kind=kOutput, calls=%fused_computation.300 | convolution fusion | flops 431364608 | bytes 51970048 | tf_op jit(solution)/shard_map/hqk,qhd->khd/dot_general | solution.py:116
  396.6 19.5 %fusion.204 = bf16[512,12,64]{0,2,1:T(8,128)(2,1)} fusion(f32[12,512,512]{1,2,0:T(8,128)} %fusion.224, f32[12,512,512]{1,2,0:T(8,128)} %copy-done.2, f32[12,512]{1,0:T(8,128)S(1)} %get-tuple-element.103, bf16[512,3,12,64]{0,3,2,1:T(8,128)(2,1)} %bitcast.502), kind=kOutput, calls=%fused_computation.301 | convolution fusion | flops 431364608 | bytes 51970048 | tf_op jit(solution)/shard_map/hqk,khd->qhd/dot_general | solution.py:113
  417.3 6.0 fusion.335
  423.4 7.7 fusion.221
  441.1 4.7 copy.77
  445.9 7.8 fusion.247
  453.6 4.4 copy.82
  460.0 4.9 convolution_dynamic-update-slice_fusion.2
  469.6 6.1 convolution_dynamic-update-slice_fusion.8
  478.9 6.4 convolution_dynamic-update-slice_fusion.7
  485.8 6.3 pad_maximum_fusion.5
  492.2 7.2 fusion.248
  499.5 9.6 fusion.52
  519.1 7.8 fusion.223
  526.8 7.7 fusion.195
  534.6 20.0 %fusion.207 = bf16[512,12,64]{0,2,1:T(8,128)(2,1)} fusion(f32[12,512,512]{1,2,0:T(8,128)} %fusion.223, f32[12,512,512]{1,2,0:T(8,128)} %fusion.247, f32[12,512]{1,0:T(8,128)S(1)} %get-tuple-element.102, bf16[512,3,12,64]{0,3,2,1:T(8,128)(2,1)} %bitcast.497), kind=kOutput, calls=%fused_computation.302 | convolution fusion | flops 431364608 | bytes 51970048 | tf_op jit(solution)/shard_map/hqk,qhd->khd/dot_general | solution.py:116
  554.5 19.5 %fusion.210 = bf16[512,12,64]{0,2,1:T(8,128)(2,1)} fusion(f32[12,512,512]{1,2,0:T(8,128)} %fusion.223, f32[12,512,512]{1,2,0:T(8,128)} %fusion.247, f32[12,512]{1,0:T(8,128)S(1)} %get-tuple-element.102, bf16[512,3,12,64]{0,3,2,1:T(8,128)(2,1)} %bitcast.498), kind=kOutput, calls=%fused_computation.303 | convolution fusion | flops 431364608 | bytes 51970048 | tf_op jit(solution)/shard_map/hqk,khd->qhd/dot_general | solution.py:113
  575.9 6.2 convolution_dynamic-update-slice_fusion.1
  582.1 3.8 multiply_reduce_fusion.9
  596.2 6.3 convolution_dynamic-update-slice_fusion.6
  602.9 10.0 convolution_dynamic-update-slice_fusion.5
  612.9 9.4 fusion.59
  627.1 4.5 fusion.160
  635.8 6.5 fusion.222
  642.3 7.7 fusion.192
  650.0 19.5 %fusion.213 = bf16[512,12,64]{0,2,1:T(8,128)(2,1)} fusion(f32[12,512,512]{1,2,0:T(8,128)} %fusion.222, f32[12,512,512]{1,2,0:T(8,128)} %fusion.248, f32[12,512]{1,0:T(8,128)S(1)} %copy-done.79, bf16[512,3,12,64]{0,3,2,1:T(8,128)(2,1)S(1)} %bitcast.491), kind=kOutput, calls=%fused_computation.304 | convolution fusion | flops 431364608 | bytes 51970048 | tf_op jit(solution)/shard_map/hqk,qhd->khd/dot_general | solution.py:116
  669.5 22.8 %fusion.216 = bf16[512,12,64]{0,2,1:T(8,128)(2,1)} fusion(f32[12,512,512]{1,2,0:T(8,128)} %fusion.222, f32[12,512,512]{1,2,0:T(8,128)} %fusion.248, f32[12,512]{1,0:T(8,128)S(1)} %copy-done.79, bf16[512,3,12,64]{0,3,2,1:T(8,128)(2,1)S(1)} %bitcast.492), kind=kOutput, calls=%fused_computation.305 | convolution fusion | flops 431364608 | bytes 51970048 | tf_op jit(solution)/shard_map/hqk,khd->qhd/dot_general | solution.py:113
  693.9 6.2 convolution_dynamic-update-slice_fusion
  703.7 6.4 convolution_dynamic-update-slice_fusion.4
  710.1 5.0 multiply_reduce_fusion.7
  718.2 9.0 convolution_dynamic-update-slice_fusion.3
  727.2 6.0 multiply_dynamic-update-slice_fusion
  733.2 5.9 multiply_dynamic-update-slice_fusion.1
  739.2 6.1 multiply_dynamic-update-slice_fusion.2
  745.2 41.7 %select_add_fusion = f32[13824,768]{1,0:T(8,128)} fusion(f32[13824,768]{1,0:T(8,128)} %multiply_dynamic-update-slice_fusion, f32[13824,768]{1,0:T(8,128)} %multiply_dynamic-update-slice_fusion.1, f32[13824,768]{1,0:T(8,128)} %multiply_dynamic-update-slice_fusion.2, pred[]{:T(512)S(6)} %and.12, pred[]{:T(512)S(6)} %and.11, pred[]{:T(512)S(6)} %and.10), kind=kLoop, calls=%fused_computation.6 | loop fusion | flops 53084160 | bytes 169869312 | tf_op jit(solution)/shard_map/add | solution.py:262
  786.9 36.9 %gather_fusion.1 = f32[496,32,768]{2,1,0:T(8,128)} fusion(f32[432,32,768]{2,1,0:T(8,128)} %bitcast.460, s32[1024]{0:T(1024)S(1)} %copy-done.94), kind=kCustom, calls=%fused_computation.1 | custom fusion | bytes 97519552 | tf_op jit(solution)/shard_map/gather | solution.py:256
  823.8 35.7 %broadcast_select_fusion = f32[496,32,768]{2,1,0:T(8,128)} fusion(f32[496,32,768]{2,1,0:T(8,128)} %gather_fusion.1, pred[496]{0:T(512)(128)(4,1)S(1)} %copy-done.106), kind=kLoop, calls=%fused_computation.7 | loop fusion | flops 12189696 | bytes 97518064 | tf_op jit(solution)/shard_map/jit(_where)/select_n | solution.py:257
  867.6 449.5 %reduce-scatter.4.cloned.1.call-done = f32[31,32,768]{2,1,0:T(8,128)} async-done(((f32[496,32,768]{2,1,0:T(8,128)}), f32[31,32,768]{2,1,0:T(8,128)}) %reduce-scatter.4.cloned.1.call-update) | async-done | bytes 3047440
  1317.1 7.5 convert_bitcast_fusion.3
  (478 shorter events, 164.0 us)
Async XLA Ops:
  7.2 9.5 copy-start.103
  7.2 10.1 copy-start.8
  7.2 130.9 %all-gather.2.cloned.1.call-start = ((), (), s32[]{:S(2)}) async-start(), calls=%async_computation.1 | async-start | bytes 25903104 | tf_op jit(solution)/shard_map/all_gather | solution.py:274
  10.6 1306.5 %reduce-scatter.4.cloned.1.call-start = ((), (), s32[]{:S(2)}) async-start(), calls=%async_computation.2 | async-start | bytes 51806208
  214.2 22.8 %copy-start.31 = (f32[512,768]{1,0:T(8,128)}, f32[512,768]{1,0:T(8,128)S(1)}, u32[]{:S(2)}) copy-start(f32[512,768]{1,0:T(8,128)S(1)} %fusion.342) | copy-start | bytes 4718596
  215.6 21.3 %copy-start.73 = (bf16[512,768]{1,0:T(8,128)(2,1)}, bf16[512,768]{1,0:T(8,128)(2,1)S(1)}, u32[]{:S(2)}) copy-start(bf16[512,768]{1,0:T(8,128)(2,1)S(1)} %get-tuple-element.96) | copy-start | bytes 2359300
  215.6 22.2 %copy-start.44 = (bf16[72,32,768]{2,1,0:T(8,128)(2,1)S(1)}, bf16[72,32,768]{2,1,0:T(8,128)(2,1)}, u32[]{:S(2)}) copy-start(bf16[72,32,768]{2,1,0:T(8,128)(2,1)} %slice.173) | copy-start | bytes 10616836
  215.6 20.0 %collective-permute-start = (bf16[512,768]{1,0:T(8,128)(2,1)S(1)}, bf16[512,768]{1,0:T(8,128)(2,1)S(1)}, u32[]{:S(2)}, u32[]{:S(2)}) collective-permute-start(bf16[512,768]{1,0:T(8,128)(2,1)S(1)} %get-tuple-element.96), channel_id=1, source_target_pairs={{0,16},{1,17},{2,18},{3,19},{4,20},{5,21},{6,22},{7,23},{8,24},{9,... | collective-permute-start | bytes 2359304 | tf_op jit(solution)/shard_map/ppermute | solution.py:26
  256.2 8.3 slice-start.26
  257.7 6.8 copy-start.6
  258.1 6.5 slice-start.27
  258.1 6.5 copy-start.74
  263.1 10.7 copy-start.4
  264.6 9.2 slice-start.6
  264.6 9.2 slice-start.7
  269.6 10.0 copy-start.107
  269.6 19.9 %collective-permute-start.1 = (bf16[512,768]{1,0:T(8,128)(2,1)S(1)}, bf16[512,768]{1,0:T(8,128)(2,1)S(1)}, u32[]{:S(2)}, u32[]{:S(2)}) collective-permute-start(bf16[512,768]{1,0:T(8,128)(2,1)S(1)} %get-tuple-element.77), channel_id=1, source_target_pairs={{0,16},{1,17},{2,18},{3,19},{4,20},{5,21},{6,22},{7,23},{8,24},{9,... | collective-permute-start | bytes 2359304 | tf_op jit(solution)/shard_map/ppermute | solution.py:26
  279.6 12.7 copy-start.45
  317.0 27.3 %copy-start.1 = (f32[3,512,768]{2,1,0:T(8,128)}, f32[3,512,768]{2,1,0:T(8,128)S(1)}, u32[]{:S(2)}) copy-start(f32[3,512,768]{2,1,0:T(8,128)S(1)} %pad_maximum_fusion.3) | copy-start | bytes 14155780
  317.9 22.8 %copy-start.97 = (f32[512]{0:T(512)}, f32[512]{0:T(512)S(1)}, u32[]{:S(2)}) copy-start(f32[512]{0:T(512)S(1)} %get-tuple-element.152) | copy-start | bytes 6148
  322.8 8.5 copy-start.5
  324.3 6.9 copy-start.38
  364.8 8.7 copy-start.2
  416.1 7.3 slice-start.12
  423.3 8.2 slice-start
  423.4 7.8 copy-start.57
  423.4 7.8 copy-start.75
  423.4 7.8 copy-start.76
  423.4 8.1 slice-start.1
  436.7 55.4 %copy-start.99 = (f32[512]{0:T(512)}, f32[512]{0:T(512)S(1)}, u32[]{:S(2)}) copy-start(f32[512]{0:T(512)S(1)} %get-tuple-element.26) | copy-start | bytes 6148
  439.8 59.6 %collective-permute-start.2 = (bf16[512,768]{1,0:T(8,128)(2,1)}, bf16[512,768]{1,0:T(8,128)(2,1)}, u32[]{:S(2)}, u32[]{:S(2)}) collective-permute-start(bf16[512,768]{1,0:T(8,128)(2,1)} %fusion.250), channel_id=1, source_target_pairs={{16,0},{17,1},{18,2},{19,3},{20,4},{21,5},{22,6},{23,7},{24,8},{25... | collective-permute-start | bytes 2359304 | tf_op jit(solution)/shard_map/ppermute | solution.py:26
  469.6 6.6 copy-start.16
  469.6 7.9 copy-start.17
  478.9 6.5 copy-start.25
  478.9 6.5 copy-start.93
  478.9 6.9 copy-start.30
  492.2 7.3 copy-start.40
  492.2 7.3 copy-start.102
  492.2 16.9 %slice-start.2 = ((s8[4718592]{0:T(1024)(128)(4,1)}), s8[4194304]{0:T(1024)(128)(4,1)S(1)}, s32[]{:S(2)}) async-start(s8[4718592]{0:T(1024)(128)(4,1)} %bitcast.466), calls=%async_computation.5 | async-start | bytes 8388608
  492.2 16.9 %slice-start.20 = ((s8[4718592]{0:T(1024)(128)(4,1)}), s8[4194304]{0:T(1024)(128)(4,1)S(1)}, s32[]{:S(2)}) async-start(s8[4718592]{0:T(1024)(128)(4,1)} %bitcast.525), calls=%async_computation.23 | async-start | bytes 8388608
  499.4 9.7 slice-start.3
  499.4 9.7 slice-start.21
  499.5 9.7 copy-start.86
  519.1 7.8 copy-start.28
  590.8 22.0 %collective-permute-start.3 = (bf16[512,768]{1,0:T(8,128)(2,1)}, bf16[512,768]{1,0:T(8,128)(2,1)}, u32[]{:S(2)}, u32[]{:S(2)}) collective-permute-start(bf16[512,768]{1,0:T(8,128)(2,1)} %convert_element_type.272), channel_id=1, source_target_pairs={{16,0},{17,1},{18,2},{19,3},{20,4},{21,5},{22,6},{23,7},{24,8},{25... | collective-permute-start | bytes 2359304 | tf_op jit(solution)/shard_map/ppermute | solution.py:26
  602.8 10.0 copy-start.41
  602.8 10.0 copy-start.101
  602.8 19.5 %slice-start.4 = ((s8[4718592]{0:T(1024)(128)(4,1)}), s8[4194304]{0:T(1024)(128)(4,1)S(1)}, s32[]{:S(2)}) async-start(s8[4718592]{0:T(1024)(128)(4,1)} %bitcast.468), calls=%async_computation.7 | async-start | bytes 8388608
  602.8 19.5 %slice-start.22 = ((s8[4718592]{0:T(1024)(128)(4,1)}), s8[4194304]{0:T(1024)(128)(4,1)S(1)}, s32[]{:S(2)}) async-start(s8[4718592]{0:T(1024)(128)(4,1)} %bitcast.528), calls=%async_computation.25 | async-start | bytes 8388608
  612.8 9.5 slice-start.5
  612.8 9.5 slice-start.23
  612.8 9.5 copy-start.83
  612.9 9.5 copy-start.98
  635.8 6.5 copy-start.79
  669.5 22.8 %copy-start.58 = (bf16[512,12,64]{0,2,1:T(8,128)(2,1)S(1)}, bf16[512,12,64]{0,2,1:T(8,128)(2,1)}, u32[]{:S(2)}) copy-start(bf16[512,12,64]{0,2,1:T(8,128)(2,1)} %fusion.192) | copy-start | bytes 2359300
  703.6 6.4 copy-start.81
  703.6 6.4 copy-start.96
  710.1 7.2 copy-start.105
  710.1 7.4 copy-start.104
  710.1 8.1 copy-start.42
  718.2 9.0 copy-start.90
  745.2 41.7 %copy-start.94 = (s32[1024]{0:T(1024)S(1)}, s32[1024]{0:T(1024)}, u32[]{:S(2)}) copy-start(s32[1024]{0:T(1024)} %pad_clamp_fusion) | copy-start | bytes 12292
  786.9 36.9 %copy-start.106 = (pred[496]{0:T(512)(128)(4,1)S(1)}, pred[496]{0:T(512)(128)(4,1)}, u32[]{:S(2)}) copy-start(pred[496]{0:T(512)(128)(4,1)} %broadcast_compare_fusion) | copy-start | bytes 1492
  865.7 451.4 %copy-start.22 = (f32[1,31,32,768]{3,2,1,0:T(8,128)S(1)}, f32[1,31,32,768]{3,2,1,0:T(8,128)}, u32[]{:S(2)}) copy-start(f32[1,31,32,768]{3,2,1,0:T(8,128)} %param.13) | copy-start | bytes 9142276
  (86 other events, 319.5 us)
Sparse Core Ops, SparseCore 0:
  10.7 127.3 all-gather.1
  859.7 457.3 reduce-scatter.3
where the time goes:
time: 1340 us; the launch traced here: 1330 us
  waiting for transfers between devices  585 us (44%)
  matrix products  375 us (28%)
  other arithmetic  191 us (14%)
  local copies, waits for them, and re-layouts  144 us (11%)
  starting transfers between devices  20.5 us (2%)
  between operations  16.4 us (1%)
    unnamed x3, waiting for transfers between devices  450 us
    all_gather x1, waiting for transfers between devices, body(): lax.all_gather(master[0].astype(jnp.bfloat16), 'batch', axis=0, tiled=True)  120 us
    dot_general x3, matrix products, attend_back(): jnp.einsum('hqk,khd->qhd', grad_raw, key_heads, preferred_element_type=jn...  61.8 us
    dot_general x3, matrix products, attend_back(): jnp.einsum('hqk,qhd->khd', grad_raw, query_heads, preferred_element_type=...  59.3 us
    add x1, other arithmetic, add_sheet(): grad_total = grad_total + grad_sheet  41.7 us
    another operation x19, other arithmetic, body(): kept_stack = jax.tree.map(lambda *leaves: jnp.stack(leaves), *kept_list)  40.1 us
    gather x1, local copies, waits for them, and re-layouts, slot_terms(): picked = grad_panels[jnp.maximum(slot_panel, 0)]  36.9 us
    select_n x1, other arithmetic, slot_terms(): return jnp.where((slot_panel >= 0)[:, None, None], picked, 0.0)  35.7 us
  transfers between devices with their start and end apart: 6, of which 4 were waited for; matrix products, arithmetic and copies ran while one was open for 7% of the time, Pallas kernels for 0%

commit v1 on v0

v1 whole, which is shorter than its diff:
```python
import functools
import math

import jax
import jax.numpy as jnp
from jax import lax
from jax.experimental import pallas as pl
from jax.experimental.pallas import tpu as pltpu
from jax.sharding import PartitionSpec as P

D = 768
HEADS = 12
HEAD_DIM = 64
FF = 3072
STEP = 10
QKV_END = 3 * D
PROJ_END = 4 * D
UP_END = 4 * D + FF
DOWN_END = 4 * D + 2 * FF

norm_eps = 1e-06
adam_eps = 1e-08
learn_rate = 0.03
decay_rate = 0.1
beta_one = 0.5
beta_two = 0.5

bf16 = jnp.bfloat16
f32 = jnp.float32
VMEM_LIMIT = 60 * 1024 * 1024
ROWS = 128
GELU_C = math.sqrt(2.0 / math.pi)


def dot_nn(a, b):
    return lax.dot_general(a, b, (((1,), (0,)), ((), ())), preferred_element_type=f32)


def dot_nt(a, b):
    return lax.dot_general(a, b, (((1,), (1,)), ((), ())), preferred_element_type=f32)


def dot_tn(a, b):
    return lax.dot_general(a, b, (((0,), (0,)), ((), ())), preferred_element_type=f32)


def start(src, dst, sem):
    copy = pltpu.make_async_copy(src, dst, sem)
    copy.start()
    return copy


def norm(values):
    average = jnp.mean(values, axis=-1, keepdims=True)
    centred = values - average
    variance = jnp.mean(centred * centred, axis=-1, keepdims=True)
    inverse = lax.rsqrt(variance + norm_eps)
    return centred * inverse, inverse


def norm_back(grad, values, scale_row):
    normed, inverse = norm(values)
    dn = grad * (1.0 + scale_row)
    mean_one = jnp.mean(dn, axis=-1, keepdims=True)
    mean_two = jnp.mean(dn * normed, axis=-1, keepdims=True)
    dx = inverse * (dn - mean_one - normed * mean_two)
    return dx, jnp.sum(grad, axis=0, keepdims=True), jnp.sum(grad * normed, axis=0, keepdims=True)


def gelu(u):
    return 0.5 * u * (1.0 + jnp.tanh(GELU_C * (u + 0.044715 * (u * u * u))))


def gelu_slope(u):
    square = u * u
    t = jnp.tanh(GELU_C * (u + 0.044715 * (square * u)))
    return 0.5 * (1.0 + t) + 0.5 * u * (1.0 - t * t) * (GELU_C * (1.0 + 3.0 * 0.044715 * square))


def assemble_kernel(panels, first_size, index_ref, *refs):
    sources, sheet, sem = refs[:-2], refs[-2], refs[-1]
    rows = sheet.shape[1]

    @pl.loop(0, panels)
    def _(p):
        where = index_ref[p]
        if len(sources) == 1:
            pltpu.make_async_copy(sources[0].at[where], sheet.at[p], sem).start()
        else:

            @pl.when(where < first_size)
            def _():
                pltpu.make_async_copy(sources[0].at[where], sheet.at[p], sem).start()

            @pl.when(where >= first_size)
            def _():
                pltpu.make_async_copy(sources[1].at[where - first_size], sheet.at[p], sem).start()

    pltpu.make_async_copy(sheet, sheet, sem).wait()


def assemble(index, sources, panels):
    first_size = sources[0].shape[0]
    rows = sources[0].shape[1]
    return pl.pallas_call(
        functools.partial(assemble_kernel, panels, first_size),
        out_shape=jax.ShapeDtypeStruct((panels, rows, D), bf16),
        in_specs=[pl.BlockSpec(memory_space=pltpu.SMEM)]
        + [pl.BlockSpec(memory_space=pl.ANY)] * len(sources),
        out_specs=pl.BlockSpec(memory_space=pl.ANY),
        scratch_shapes=[pltpu.SemaphoreType.DMA],
        cost_estimate=pl.CostEstimate(flops=0, bytes_accessed=4 * panels * rows * D, transcendentals=0),
        name="assemble",
    )(index, *sources)


FORWARD_STATE = ("xin", "h1", "qkv", "lse", "o", "a", "x1", "h2", "u", "z", "b")


def forward_shapes(length):
    return {
        "xin": ((length, D), bf16),
        "h1": ((length, D), bf16),
        "qkv": ((length, 3 * D), bf16),
        "lse": ((16, length), f32),
        "o": ((length, D), bf16),
        "a": ((length, D), bf16),
        "x1": ((length, D), f32),
        "h2": ((length, D), bf16),
        "u": ((length, FF), f32),
        "z": ((length, FF), bf16),
        "b": ((length, D), bf16),
    }


def forward_kernel(want, clip, x_offset, length, chained, *refs):
    n_state = len(FORWARD_STATE)
    sec_ref, mod_ref, x_hbm, w_hbm = refs[:4]
    refs = refs[4 + 1 :]
    refs = refs[(n_state if chained else 0) + (1 if clip or chained else 0) :]
    state = dict(zip(FORWARD_STATE, refs[:n_state]))
    outs_hbm, sent_hbm = refs[n_state : n_state + 2]
    scratch = refs[n_state + 2 :]
    w, keep, out_v, acc, score, soft, lse_cols, w_sem, x_sem, o_sem = (
        scratch[0],
        dict(zip(FORWARD_STATE, scratch[1 : 1 + n_state])),
        *scratch[1 + n_state :],
    )

    @pl.when(sec_ref[0] == want)
    def _():
        get_x = start(x_hbm.at[pl.ds(x_offset, length)], keep["xin"], x_sem)
        bounds = (0, QKV_END, PROJ_END, UP_END, DOWN_END)
        get_w = [
            start(
                w_hbm.at[pl.ds(bounds[i], bounds[i + 1] - bounds[i])],
                w.at[pl.ds(bounds[i], bounds[i + 1] - bounds[i])],
                w_sem.at[i],
            )
            for i in range(4)
        ]
        row = lambda n: mod_ref[clip, n : n + 1, :]
        put = []

        def save(name):
            put.append(start(keep[name], state[name], o_sem.at[len(put)]))

        get_x.wait()
        save("xin")
        for r in range(0, length, ROWS):
            block = pl.ds(r, ROWS)
            normed, _ = norm(keep["xin"][block, :].astype(f32))
            keep["h1"][block, :] = (normed * (1.0 + row(1)) + row(0)).astype(bf16)
        save("h1")
        get_w[0].wait()
        for n in range(3):
            part = dot_nt(keep["h1"][...], w[n * D : (n + 1) * D, :])
            keep["qkv"][:, n * D : (n + 1) * D] = part.astype(bf16)
        save("qkv")
        lse_cols[...] = jnp.zeros_like(lse_cols)
        low_lanes = lax.broadcasted_iota(jnp.int32, (1, 128), 1) < HEAD_DIM

        @pl.loop(0, HEADS // 2)
        def _(pair):
            at = lambda n: pl.ds(pl.multiple_of(n * D + pair * 128, 128), 128)
            q = keep["qkv"][:, at(0)] * jnp.asarray(HEAD_DIM ** (-0.5), bf16)
            k = keep["qkv"][:, at(1)]
            v = keep["qkv"][:, at(2)]
            mixed = []
            for h in range(2):
                qh = jnp.where(low_lanes if h == 0 else ~low_lanes, q, jnp.zeros_like(q))
                score[h, :, :] = dot_nt(qh, k)
                lane = lax.broadcasted_iota(jnp.int32, (1, 128), 1) == pair * 2 + h
                for r in range(0, length, ROWS):
                    block = pl.ds(r, ROWS)
                    s = score[h, block, :]
                    top = jnp.max(s, axis=-1, keepdims=True)
                    e = jnp.exp(s - top)
                    total = jnp.sum(e, axis=-1, keepdims=True)
                    soft[h, block, :] = (e * (1.0 / total)).astype(bf16)
                    lse_cols[block, :] = jnp.where(lane, top + jnp.log(total), lse_cols[block, :])
                mixed.append(dot_nn(soft[h, :, :], v))
            keep["o"][:, at(0)] = jnp.where(low_lanes, mixed[0], mixed[1]).astype(bf16)

        keep["lse"][...] = lse_cols[...].T[:16, :]
        save("lse")
        save("o")
        get_w[1].wait()
        acc[...] = dot_nt(keep["o"][...], w[QKV_END:PROJ_END, :])
        for r in range(0, length, ROWS):
            block = pl.ds(r, ROWS)
            branch = acc[block, :]
            keep["a"][block, :] = branch.astype(bf16)
            middle = keep["xin"][block, :].astype(f32) + row(2) * branch
            keep["x1"][block, :] = middle
            normed, _ = norm(middle)
            keep["h2"][block, :] = (normed * (1.0 + row(4)) + row(3)).astype(bf16)
        save("a")
        save("x1")
        save("h2")
        get_w[2].wait()
        get_w[3].wait()
        tile = D
        for n in range(FF // tile):
            span = slice(n * tile, (n + 1) * tile)
            keep["u"][:, span] = dot_nt(keep["h2"][...], w[PROJ_END + n * tile : PROJ_END + (n + 1) * tile, :])
            for r in range(0, length, ROWS):
                block = pl.ds(r, ROWS)
                keep["z"][block, span] = gelu(keep["u"][block, span]).astype(bf16)
            part = dot_nn(keep["z"][:, span], w[UP_END + n * tile : UP_END + (n + 1) * tile, :])
            if n:
                acc[...] += part
            else:
                acc[...] = part
        save("u")
        save("z")
        for r in range(0, length, ROWS):
            block = pl.ds(r, ROWS)
            branch = acc[block, :]
            keep["b"][block, :] = branch.astype(bf16)
            out_v[block, :] = (keep["x1"][block, :] + row(5) * branch).astype(bf16)
        save("b")
        put.append(start(out_v, outs_hbm.at[pl.ds(clip * length, length)], o_sem.at[len(put)]))
        put.append(start(out_v, sent_hbm, o_sem.at[len(put)]))
        for copy in put:
            copy.wait()


def forward(want, clip, clips, length, section, mod, x, x_offset, sheet, token, state, outs):
    shapes = forward_shapes(length)
    any_spec = pl.BlockSpec(memory_space=pl.ANY)
    chained = state is not None
    operands = [section, mod, x, sheet, token]
    aliases = {}
    if chained:
        for n, name in enumerate(FORWARD_STATE):
            aliases[len(operands)] = n
            operands.append(state[name])
    if outs is not None:
        aliases[len(operands)] = len(FORWARD_STATE)
        operands.append(outs)
    out_shape = [jax.ShapeDtypeStruct(*shapes[name]) for name in FORWARD_STATE]
    out_shape += [
        jax.ShapeDtypeStruct((clips * length, D), bf16),
        jax.ShapeDtypeStruct((length, D), bf16),
    ]
    results = pl.pallas_call(
        functools.partial(forward_kernel, want, clip, x_offset, length, chained),
        out_shape=out_shape,
        in_specs=[
            pl.BlockSpec(memory_space=pltpu.SMEM),
            pl.BlockSpec(memory_space=pltpu.VMEM),
        ]
        + [any_spec] * (len(operands) - 2),
        out_specs=[any_spec] * len(out_shape),
        scratch_shapes=[pltpu.VMEM((DOWN_END, D), bf16)]
        + [pltpu.VMEM(*shapes[name]) for name in FORWARD_STATE]
        + [
            pltpu.VMEM((length, D), bf16),
            pltpu.VMEM((length, D), f32),
            pltpu.VMEM((2, length, length), f32),
            pltpu.VMEM((2, length, length), bf16),
            pltpu.VMEM((length, 128), f32),
            pltpu.SemaphoreType.DMA((4,)),
            pltpu.SemaphoreType.DMA,
            pltpu.SemaphoreType.DMA((len(FORWARD_STATE) + 2,)),
        ],
        input_output_aliases=aliases,
        compiler_params=pltpu.CompilerParams(vmem_limit_bytes=VMEM_LIMIT),
        cost_estimate=pl.CostEstimate(
            flops=2 * length * DOWN_END * D * 2, bytes_accessed=20 << 20, transcendentals=length * length * HEADS
        ),
        name=f"block_forward_{want}_{clip}",
    )(*operands)
    return dict(zip(FORWARD_STATE, results)), results[-2], results[-1]


BACK_NEEDS = ("xin", "qkv", "lse", "a", "x1", "u", "b")
BACK_STATE = ("db", "du", "da", "dqkv", "dmod")


def back_shapes(length):
    return {
        "db": ((length, D), bf16),
        "du": ((length, FF), bf16),
        "da": ((length, D), bf16),
        "dqkv": ((length, 3 * D), bf16),
        "dmod": ((6, D), f32),
    }


def back_kernel(want, clip, g_offset, length, chained, *refs):
    n_need, n_state = len(BACK_NEEDS), len(BACK_STATE)
    sec_ref, loss_ref, mod_ref, g_hbm, w_hbm = refs[:5]
    needs = dict(zip(BACK_NEEDS, refs[5 : 5 + n_need]))
    refs = refs[5 + n_need :]
    refs = refs[(n_state if chained else 0) + (1 if clip or chained else 0) :]
    state = dict(zip(BACK_STATE, refs[:n_state]))
    gin_hbm, sent_hbm, token_hbm = refs[n_state : n_state + 3]
    scratch = refs[n_state + 3 :]
    w = scratch[0]
    have = dict(zip(BACK_NEEDS, scratch[1 : 1 + n_need]))
    keep = dict(zip(BACK_STATE, scratch[1 + n_need : 1 + n_need + n_state]))
    g_low, dx1, acc, do, sent_v, w_sem, g_sem, h_sem, o_sem = scratch[1 + n_need + n_state :]

    @pl.when(sec_ref[0] == want)
    def _():
        get_g = start(g_hbm.at[pl.ds(g_offset, length)], g_low, g_sem)
        get = {}
        bounds = (0, QKV_END, PROJ_END, UP_END, DOWN_END)

        def fetch(name):
            get[name] = start(needs[name], have[name], h_sem.at[BACK_NEEDS.index(name)])

        def fetch_w(i):
            span = pl.ds(bounds[i], bounds[i + 1] - bounds[i])
            get[i] = start(w_hbm.at[span], w.at[span], w_sem.at[i])

        fetch("b")
        fetch_w(3)
        fetch("u")
        fetch_w(2)
        fetch("x1")
        fetch("a")
        fetch_w(1)
        fetch("qkv")
        fetch("lse")
        fetch_w(0)
        fetch("xin")
        row = lambda n: mod_ref[clip, n : n + 1, :]
        put = []

        def save(name):
            put.append(start(keep[name], state[name], o_sem.at[len(put)]))

        get_g.wait()
        get["b"].wait()
        gate_two = jnp.zeros((1, D), f32)
        for r in range(0, length, ROWS):
            block = pl.ds(r, ROWS)
            g = g_low[block, :].astype(f32)
            if want:
                g = g * loss_ref[clip]
            dx1[block, :] = g
            keep["db"][block, :] = (row(5) * g).astype(bf16)
            gate_two += jnp.sum(g * have["b"][block, :].astype(f32), axis=0, keepdims=True)
        keep["dmod"][5:6, :] = gate_two
        save("db")
        get[3].wait()
        get["u"].wait()
        get[2].wait()
        tile = D
        for n in range(FF // tile):
            span = slice(n * tile, (n + 1) * tile)
            dz = dot_nt(keep["db"][...], w[UP_END + n * tile : UP_END + (n + 1) * tile, :])
            keep["du"][:, span] = (dz * gelu_slope(have["u"][:, span])).astype(bf16)
            part = dot_nn(keep["du"][:, span], w[PROJ_END + n * tile : PROJ_END + (n + 1) * tile, :])
            if n:
                acc[...] += part
            else:
                acc[...] = part
        save("du")
        get["x1"].wait()
        get["a"].wait()
        shift_two = jnp.zeros((1, D), f32)
        scale_two = jnp.zeros((1, D), f32)
        gate_one = jnp.zeros((1, D), f32)
        for r in range(0, length, ROWS):
            block = pl.ds(r, ROWS)
            dx, shift_part, scale_part = norm_back(acc[block, :], have["x1"][block, :], row(4))
            total = dx1[block, :] + dx
            dx1[block, :] = total
            shift_two += shift_part
            scale_two += scale_part
            gate_one += jnp.sum(total * have["a"][block, :].astype(f32), axis=0, keepdims=True)
            keep["da"][block, :] = (row(2) * total).astype(bf16)
        keep["dmod"][2:3, :] = gate_one
        keep["dmod"][3:4, :] = shift_two
        keep["dmod"][4:5, :] = scale_two
        save("da")
        get[1].wait()
        do[...] = dot_nn(keep["da"][...], w[QKV_END:PROJ_END, :]).astype(bf16)
        get["qkv"].wait()
        get["lse"].wait()
        low_lanes = lax.broadcasted_iota(jnp.int32, (1, 128), 1) < HEAD_DIM
        scale = HEAD_DIM ** (-0.5)

        @pl.loop(0, HEADS // 2)
        def _(pair):
            at = lambda n: pl.ds(pl.multiple_of(n * D + pair * 128, 128), 128)
            q = have["qkv"][:, at(0)]
            k = have["qkv"][:, at(1)]
            v = have["qkv"][:, at(2)]
            dop = do[:, at(0)]
            zero = jnp.zeros_like(q)
            dq = dk = dv = None
            for h in range(2):
                lanes = low_lanes if h == 0 else ~low_lanes
                qh = jnp.where(lanes, q, zero)
                kh = jnp.where(lanes, k, zero)
                doh = jnp.where(lanes, dop, zero)
                st = dot_nt(k, qh * jnp.asarray(scale, bf16))
                pt = jnp.exp(st - have["lse"][pl.ds(pair * 2 + h, 1), :])
                dpt = dot_nt(v, doh)
                dv_part = dot_nn(pt.astype(bf16), doh)
                inner = jnp.sum(dpt * pt, axis=0, keepdims=True)
                drt = (pt * (dpt - inner) * scale).astype(bf16)
                dk_part = dot_nn(drt, qh)
                dq_part = dot_tn(drt, kh)
                dq = dq_part if h == 0 else dq + dq_part
                dk = dk_part if h == 0 else dk + dk_part
                dv = dv_part if h == 0 else dv + dv_part
            keep["dqkv"][:, at(0)] = dq.astype(bf16)
            keep["dqkv"][:, at(1)] = dk.astype(bf16)
            keep["dqkv"][:, at(2)] = dv.astype(bf16)

        save("dqkv")
        get[0].wait()
        acc[...] = dot_nn(keep["dqkv"][...], w[0:QKV_END, :])
        get["xin"].wait()
        shift_one = jnp.zeros((1, D), f32)
        scale_one = jnp.zeros((1, D), f32)
        for r in range(0, length, ROWS):
            block = pl.ds(r, ROWS)
            dx, shift_part, scale_part = norm_back(acc[block, :], have["xin"][block, :].astype(f32), row(1))
            total = dx1[block, :] + dx
            dx1[block, :] = total
            sent_v[block, :] = total.astype(bf16)
            shift_one += shift_part
            scale_one += scale_part
        keep["dmod"][0:1, :] = shift_one
        keep["dmod"][1:2, :] = scale_one
        save("dmod")
        put.append(start(sent_v, sent_hbm, o_sem.at[len(put)]))
        put.append(start(dx1, gin_hbm.at[pl.ds(clip * length, length)], o_sem.at[len(put)]))
        for copy in put:
            copy.wait()


def back(want, clip, clips, length, section, loss_weight, mod, g, g_offset, sheet, kept, state, gin):
    shapes, kept_shapes = back_shapes(length), forward_shapes(length)
    any_spec = pl.BlockSpec(memory_space=pl.ANY)
    chained = state is not None
    operands = [section, loss_weight, mod, g, sheet] + [kept[name] for name in BACK_NEEDS]
    aliases = {}
    if chained:
        for n, name in enumerate(BACK_STATE):
            aliases[len(operands)] = n
            operands.append(state[name])
    if gin is not None:
        aliases[len(operands)] = len(BACK_STATE)
        operands.append(gin)
    out_shape = [jax.ShapeDtypeStruct(*shapes[name]) for name in BACK_STATE]
    out_shape += [
        jax.ShapeDtypeStruct((clips * length, D), f32),
        jax.ShapeDtypeStruct((length, D), bf16),
        jax.ShapeDtypeStruct((8, 128), f32),
    ]
    results = pl.pallas_call(
        functools.partial(back_kernel, want, clip, g_offset, length, chained),
        out_shape=out_shape,
        in_specs=[
            pl.BlockSpec(memory_space=pltpu.SMEM),
            pl.BlockSpec(memory_space=pltpu.SMEM),
            pl.BlockSpec(memory_space=pltpu.VMEM),
        ]
        + [any_spec] * (len(operands) - 3),
        out_specs=[any_spec] * len(out_shape),
        scratch_shapes=[pltpu.VMEM((DOWN_END, D), bf16)]
        + [pltpu.VMEM(*kept_shapes[name]) for name in BACK_NEEDS]
        + [pltpu.VMEM(*shapes[name]) for name in BACK_STATE]
        + [
            pltpu.VMEM((length, D), bf16),
            pltpu.VMEM((length, D), f32),
            pltpu.VMEM((length, D), f32),
            pltpu.VMEM((length, D), bf16),
            pltpu.VMEM((length, D), bf16),
            pltpu.SemaphoreType.DMA((4,)),
            pltpu.SemaphoreType.DMA,
            pltpu.SemaphoreType.DMA((len(BACK_NEEDS),)),
            pltpu.SemaphoreType.DMA((len(BACK_STATE) + 2,)),
        ],
        input_output_aliases=aliases,
        compiler_params=pltpu.CompilerParams(vmem_limit_bytes=VMEM_LIMIT),
        cost_estimate=pl.CostEstimate(
            flops=2 * length * DOWN_END * D * 2, bytes_accessed=30 << 20, transcendentals=length * length * HEADS
        ),
        name=f"block_back_{want}_{clip}",
    )(*operands)
    return dict(zip(BACK_STATE, results)), results[-3], results[-2], results[-1]


GRAD_PAIRS = (("z", "db", UP_END), ("du", "h2", PROJ_END), ("da", "o", QKV_END), ("dqkv", "h1", 0))


def grads_kernel(clips, length, panel_rows, first_size, two, dest_ref, *refs):
    count = 2 * len(GRAD_PAIRS) * clips
    sources = refs[:count]
    outs = refs[count : count + (2 if two else 1)]
    scratch = refs[count + (2 if two else 1) :]
    values = scratch[: 2 * len(GRAD_PAIRS)]
    tile_v, in_sem, out_sem = scratch[2 * len(GRAD_PAIRS) :]
    get = []
    for n in range(2 * len(GRAD_PAIRS)):
        get.append(
            [
                start(sources[n * clips + c], values[n].at[pl.ds(c * length, length)], in_sem.at[n, c])
                for c in range(clips)
            ]
        )
    tiles = []
    for n, (left, right, base) in enumerate(GRAD_PAIRS):
        width = values[2 * n].shape[1]
        tiles += [(n, column, base + column) for column in range(0, width, D)]
    per_tile = D // panel_rows
    seen = set()

    def drain(slot):
        pltpu.make_async_copy(outs[0].at[pl.ds(0, per_tile)], tile_v.at[slot], out_sem.at[slot]).wait()

    for t, (n, column, first_row) in enumerate(tiles):
        slot = t % 2
        if n not in seen:
            seen.add(n)
            for copy in get[2 * n] + get[2 * n + 1]:
                copy.wait()
        if t >= 2:
            drain(slot)
        part = dot_tn(values[2 * n][:, column : column + D], values[2 * n + 1][...])
        tile_v[slot, :, :, :] = part.astype(bf16).reshape(per_tile, panel_rows, D)

        @pl.loop(0, per_tile)
        def _(p):
            where = dest_ref[first_row // panel_rows + p]
            if not two:
                pltpu.make_async_copy(tile_v.at[slot, p], outs[0].at[where], out_sem.at[slot]).start()
            else:

                @pl.when(where < first_size)
                def _():
                    pltpu.make_async_copy(tile_v.at[slot, p], outs[0].at[where], out_sem.at[slot]).start()

                @pl.when(where >= first_size)
                def _():
                    pltpu.make_async_copy(
                        tile_v.at[slot, p], outs[1].at[where - first_size], out_sem.at[slot]
                    ).start()

    drain(0)
    drain(1)


def weight_grads(dest, kept, backs, length, panel_rows, sizes):
    clips = len(kept)
    any_spec = pl.BlockSpec(memory_space=pl.ANY)
    operands, scratch = [], []
    for left, right, _ in GRAD_PAIRS:
        for name in (left, right):
            arrays = [{**kept[c], **backs[c]}[name] for c in range(clips)]
            operands += arrays
            scratch.append(pltpu.VMEM((clips * length, arrays[0].shape[1]), bf16))
    two = len(sizes) == 2
    return pl.pallas_call(
        functools.partial(grads_kernel, clips, length, panel_rows, sizes[0], two),
        out_shape=[jax.ShapeDtypeStruct((size, panel_rows, D), bf16) for size in sizes],
        in_specs=[pl.BlockSpec(memory_space=pltpu.SMEM)] + [any_spec] * len(operands),
        out_specs=[any_spec] * len(sizes),
        scratch_shapes=scratch
        + [
            pltpu.VMEM((2, D // panel_rows, panel_rows, D), bf16),
            pltpu.SemaphoreType.DMA((2 * len(GRAD_PAIRS), clips)),
            pltpu.SemaphoreType.DMA((2,)),
        ],
        compiler_params=pltpu.CompilerParams(vmem_limit_bytes=VMEM_LIMIT),
        cost_estimate=pl.CostEstimate(
            flops=2 * clips * length * DOWN_END * D, bytes_accessed=40 << 20, transcendentals=0
        ),
        name="weight_grads",
    )(dest, *operands)


def adam_kernel(kind_ref, row_ref, master, first, second, sums, dmod, cond, master_o, first_o, second_o, copy_o):
    slot = pl.program_id(0)
    rows = master.shape[1]
    kind = kind_ref[slot]

    def update(grad):
        first_next = beta_one * first[0] + (1.0 - beta_one) * grad
        second_next = beta_two * second[0] + (1.0 - beta_two) * grad * grad
        first_hat = first_next / (1.0 - beta_one**STEP)
        second_hat = second_next / (1.0 - beta_two**STEP)
        value = master[0] - learn_rate * (
            first_hat / (jnp.sqrt(second_hat) + adam_eps) + decay_rate * master[0]
        )
        master_o[0] = value
        first_o[0] = first_next
        second_o[0] = second_next
        copy_o[0] = value.astype(bf16)

    @pl.when(kind == 0)
    def _():
        update(jnp.zeros((rows, D), f32))

    @pl.when(kind == 1)
    def _():
        update(sums[0].astype(f32))

    @pl.when(kind == 2)
    def _():
        at = pl.multiple_of(row_ref[slot], rows)
        update(dot_nn(dmod[pl.ds(at, rows), :], cond[...]))


def adam(kind, row, master, first, second, sums, dmod, cond):
    slots, rows = master.shape[0], master.shape[1]
    block = pl.BlockSpec((1, rows, D), lambda s, *_: (s, 0, 0))
    return pl.pallas_call(
        adam_kernel,
        grid_spec=pltpu.PrefetchScalarGridSpec(
            num_scalar_prefetch=2,
            grid=(slots,),
            in_specs=[block] * 4
            + [
                pl.BlockSpec(dmod.shape, lambda s, *_: (0, 0)),
                pl.BlockSpec(cond.shape, lambda s, *_: (0, 0)),
            ],
            out_specs=[block] * 4,
        ),
        out_shape=[jax.ShapeDtypeStruct(master.shape, f32)] * 3 + [jax.ShapeDtypeStruct(master.shape, bf16)],
        cost_estimate=pl.CostEstimate(flops=0, bytes_accessed=slots * rows * D * 30, transcendentals=0),
        name="adam",
    )(kind, row, master, first, second, sums, dmod, cond)


def time_features(steps_in):
    half_width = D // 2
    freqs = jnp.exp(-math.log(10000.0) * jnp.arange(half_width, dtype=f32) / half_width)
    angles = steps_in.astype(f32)[:, None] * freqs[None, :]
    return jnp.concatenate([jnp.cos(angles), jnp.sin(angles)], axis=1)


def body(tokens, cotangent, loss_weight, timesteps, owners, master, first_moment, second_moment):
    section_index = lax.axis_index("section")
    me = lax.axis_index("batch")
    owner_total = lax.axis_size("batch")
    slots, panel_rows = master.shape[1], master.shape[2]
    clips = timesteps.shape[0]
    length = tokens.shape[0] // clips
    owner = owners[0]
    panels = owner.shape[0]
    moved = DOWN_END // panel_rows
    cap = min(slots, max(4, (slots * 27 + 30) // 31))
    section = jnp.reshape(section_index, (1,)).astype(jnp.int32)

    number = jnp.arange(panels, dtype=jnp.int32)
    same = (owner[:, None] == owner[None, :]) & (number[None, :] < number[:, None])
    rank = jnp.sum(same.astype(jnp.int32), axis=1)
    first_size = owner_total * cap
    place = jnp.where(
        rank < cap, owner * cap + rank, first_size + owner * (slots - cap) + rank - cap
    )[:moved]
    mine = (owner[None, :] == me) & (
        rank[None, :] == jnp.arange(slots, dtype=jnp.int32)[:, None]
    )
    slot_panel = jnp.sum(jnp.where(mine, number[None, :] + 1, 0), axis=1) - 1
    kind = jnp.where(slot_panel < 0, 0, jnp.where(slot_panel < moved, 1, 2)).astype(jnp.int32)
    mod_row = jnp.where(kind == 2, (slot_panel - moved) * panel_rows, 0).astype(jnp.int32)

    low = master[0].astype(bf16)
    sources = [lax.all_gather(low[:cap], "batch", axis=0, tiled=True)]
    over = None
    if cap < slots:
        beyond = jnp.max(jnp.where(number < moved, rank, 0)) >= cap
        over = lax.pmax(beyond.astype(f32), "section") > 0.5
        rest = low[cap:]
        rest_shape = (owner_total * (slots - cap), panel_rows, D)
        sources.append(
            lax.cond(
                over,
                lambda part: lax.all_gather(part, "batch", axis=0, tiled=True),
                lambda part: jnp.zeros(rest_shape, bf16),
                rest,
            )
        )
    sheet = assemble(place, sources, moved).reshape(moved * panel_rows, D)

    all_steps = lax.all_gather(timesteps, "batch", axis=0, tiled=True)
    cond = jax.nn.silu(time_features(all_steps)).astype(bf16)
    clip_total = cond.shape[0]
    share = jnp.einsum("cd,sd->cs", cond, low.reshape(slots * panel_rows, D), preferred_element_type=f32)
    share = lax.all_to_all(
        share.reshape(owner_total, clips, slots * panel_rows), "batch", split_axis=0, concat_axis=0, tiled=True
    )
    share = share.reshape(owner_total, clips, slots, panel_rows).transpose(1, 0, 2, 3)
    share = share.reshape(clips, owner_total * slots, panel_rows)
    pick = (
        (owner * slots + rank)[moved:, None] == jnp.arange(owner_total * slots, dtype=jnp.int32)[None, :]
    ).astype(f32)
    mod = jnp.einsum("ps,csr->cpr", pick, share, precision=lax.Precision.HIGHEST)
    mod = mod.reshape(clips, 6, D)

    run = functools.partial
    fwd = run(forward, clips=clips, length=length, section=section, mod=mod, sheet=sheet)
    bwd = run(back, clips=clips, length=length, section=section, loss_weight=loss_weight, mod=mod, sheet=sheet)
    token = jnp.zeros((8, 128), f32)
    kept, sent, outs = [None] * clips, [None] * clips, None
    for c in range(clips):
        kept[c], outs, sent[c] = fwd(0, c, x=tokens, x_offset=c * length, token=token, state=None, outs=outs)
    received = [lax.ppermute(rows, "section", [(0, 1)]) for rows in sent]
    backs, gin = [None] * clips, None
    for c in range(clips):
        kept[c], outs, _ = fwd(1, c, x=received[c], x_offset=0, token=token, state=kept[c], outs=outs)
        backs[c], gin, sent[c], token = bwd(1, c, g=cotangent, g_offset=c * length, kept=kept[c], state=None, gin=gin)
    received = [lax.ppermute(rows, "section", [(1, 0)]) for rows in sent]
    for c in range(clips):
        backs[c], gin, _, token = bwd(0, c, g=received[c], g_offset=0, kept=kept[c], state=backs[c], gin=gin)

    sizes = [first_size] + ([owner_total * (slots - cap)] if cap < slots else [])
    grads = weight_grads(place, kept, backs, length, panel_rows, sizes)
    sums = lax.psum_scatter(grads[0], "batch", scatter_dimension=0, tiled=True)
    if cap < slots:
        more = lax.cond(
            over,
            lambda part: lax.psum_scatter(part, "batch", scatter_dimension=0, tiled=True),
            lambda part: jnp.zeros((slots - cap, panel_rows, D), bf16),
            grads[1],
        )
        sums = jnp.concatenate([sums, more], axis=0)
    dmod = jnp.stack([b["dmod"] for b in backs]).reshape(clips, 6 * D).astype(bf16)
    dmod = lax.all_gather(dmod, "batch", axis=0, tiled=True).T
    results = adam(kind, mod_row, master[0], first_moment[0], second_moment[0], sums, dmod, cond)
    return (outs[None], gin[None], *(r[None] for r in results))


def solution(mesh):
    placed = (
        P("batch", None),
        P("batch", None),
        P("batch"),
        P("batch"),
        P("section", None),
        P("section", "batch", None, None),
        P("section", "batch", None, None),
        P("section", "batch", None, None),
    )
    return jax.shard_map(
        body,
        mesh=mesh,
        in_specs=placed,
        out_specs=(
            P("section", "batch", None),
            P("section", "batch", None),
            P("section", "batch", None, None),
            P("section", "batch", None, None),
            P("section", "batch", None, None),
            P("section", "batch", None, None),
        ),
        check_vma=False,
    )
```

time: 1340 us -> 1090 us (0.81)
  Pallas kernels: 0 us -> 625 us
  matrix products: 375 us -> 1.11 us
  waiting for transfers between devices: 585 us -> 366 us
  other arithmetic: 191 us -> 10.8 us
  local copies, waits for them, and re-layouts: 144 us -> 14.1 us
  blocking collectives: 0 us -> 38.4 us
    pallas_call x0 -> x11, Pallas kernels: none -> 625 us  [the longest x1 431 us: assemble(): pl.pallas_call(functools.partial(assemble_kernel, panels, first_size), ou...]
    unnamed x3 -> x2, waiting for transfers between devices: 450 us -> 1.08 us
    dot_general x60 -> x2, matrix products: 375 us -> 1.11 us  [the longest x1 0.59 us: body(): jnp.einsum('ps,csr->cpr', pick, share, precision=lax.Precision.HIGHEST)]
    reduce_scatter x0 -> x1, waiting for transfers between devices: none -> 190 us  [body(): sums = lax.psum_scatter(grads[0], 'batch', scatter_dimension=0, tiled=True)]
    ppermute x4, waiting for transfers between devices: 16 us -> 81 us  [the longest x2 74 us: body(): received = [lax.ppermute(rows, 'section', [(1, 0)]) for rows in sent]]
    gather x2 -> x0, local copies, waits for them, and re-layouts: 60.3 us -> none  [the longest x1 36.9 us: slot_terms(): picked = grad_panels[jnp.maximum(slot_panel, 0)]]
    add x7 -> x1, other arithmetic: 45.7 us -> 0.01 us  [body(): slot_panel = jnp.sum(jnp.where(mine, number[None, :] + 1, 0), axis=1) - 1]
    another operation x27 -> x0, other arithmetic: 42 us -> none  [the longest x19 40.1 us: body(): kept_stack = jax.tree.map(lambda *leaves: jnp.stack(leaves), *kept_list)]
  transfers between devices with their start and end apart: 6 -> 7, of which waited for: 4 -> 6; matrix products, arithmetic and copies ran while one was open for 7% -> 1% of each run, Pallas kernels for 0% -> 7%
where the time goes in v1:
time: 1090 us
  Pallas kernels  625 us (57%)
  waiting for transfers between devices  366 us (34%)
  blocking collectives  38.4 us (4%)
  between operations  18 us (2%)
  local copies, waits for them, and re-layouts  14.1 us (1%)
  starting transfers between devices  11.8 us (1%)
    pallas_call x1, Pallas kernels, assemble(): pl.pallas_call(functools.partial(assemble_kernel, panels, first_size), ou...  431 us
    reduce_scatter x1, waiting for transfers between devices, body(): sums = lax.psum_scatter(grads[0], 'batch', scatter_dimension=0, tiled=True)  190 us
    pallas_call x4, Pallas kernels, back(): pl.pallas_call(functools.partial(back_kernel, want, clip, g_offset, lengt...  88.9 us
    all_gather x1, waiting for transfers between devices, body(): sources = [lax.all_gather(low[:cap], 'batch', axis=0, tiled=True)]  84.4 us
    ppermute x2, waiting for transfers between devices, body(): received = [lax.ppermute(rows, 'section', [(1, 0)]) for rows in sent]  74 us
    pallas_call x4, Pallas kernels, forward(): pl.pallas_call(functools.partial(forward_kernel, want, clip, x_offset, le...  54.2 us
    pallas_call x1, Pallas kernels, weight_grads(): pl.pallas_call(functools.partial(grads_kernel, clips, length, panel_rows,...  29 us
    pallas_call x1, Pallas kernels, adam(): pl.pallas_call(adam_kernel, grid_spec=pltpu.PrefetchScalarGridSpec(num_sc...  22.4 us
  transfers between devices with their start and end apart: 7, of which 6 were waited for; matrix products, arithmetic and copies ran while one was open for 1% of the time, Pallas kernels for 7%

profile of v1, /device:TPU:1, one launch (start us, length us, event | category | flops | bytes accessed | tf_op | source)
XLA Modules:
  0.0 1085.5 jit_solution(5130691482728880311)
XLA Ops:
  8.0 1.0 convert_reduce_fusion
  9.0 0.6 copy-done.3
  9.6 1.9 add_select_fusion
  12.1 4.9 pmax.7
  17.6 3.2 bitcast_convert_fusion
  20.9 1.2 slice.18
  22.0 2.1 conditional.2
  22.0 2.1 broadcast.54
  24.1 0.6 all-gather.6.cloned.1.call-update
  24.7 0.6 dynamic-slice
  26.0 0.2 dynamic-update-slice
  26.2 11.3 %all-reduce = s32[32]{0:T(128)S(1)} all-reduce(s32[32]{0:T(128)S(1)} %dynamic-update-slice), channel_id=1, replica_groups=mesh['section'=2,'batch'=16] {'batch'}, use_global_device_ids=true, to_apply=%add | all-reduce | flops 32 | bytes 256
  37.5 0.5 copy-done.7
  38.0 0.1 mul.51
  38.1 0.1 copy.67
  38.2 0.3 multiply_cosine_fusion.1
  38.5 0.3 copy-done.5
  38.8 0.5 fusion.5
  39.3 0.8 copy.68
  40.1 6.5 all-to-all-start
  46.6 0.1 slice.15
  46.7 9.3 all-to-all-done
  56.0 0.2 reshape.72
  56.3 0.6 convolution_bitcast_fusion
  56.8 0.1 copy.71
  57.0 0.7 reshape.74.refs_1_.refs_2_
  57.7 84.4 %all-gather.6.cloned.1.call-done.refs_0_ = bf16[432,32,768]{2,1,0:T(8,128)(2,1)} async-done(((bf16[27,32,768]{2,1,0:T(8,128)(2,1)}), bf16[432,32,768]{2,1,0:T(8,128)(2,1)}) %all-gather.6.cloned.1.call-update) | async-done | bytes 21233680 | tf_op jit(solution)/shard_map/all_gather | solution.py:690
  142.1 430.6 %assemble.1 = bf16[288,32,768]{2,1,0:T(8,128)(2,1)} custom-call(s32[288]{0:T(512)} %bitcast.57, bf16[432,32,768]{2,1,0:T(8,128)(2,1)} %all-gather.6.cloned.1.call-done.refs_0_, bf16[64,32,768]{2,1,0:T(8,128)(2,1)} %get-tuple-element.192.refs_1_), custom_call_target="tpu_custom_call" | custom-call | bytes 28311552 | tf_op jit(solution)/shard_map/assemble/pallas_call | solution.py:105
  572.7 0.6 broadcast_in_dim.57.refs_4_
  573.3 25.9 %block_forward_0_0.1 = (bf16[512,768]{1,0:T(8,128)(2,1)}, bf16[512,768]{1,0:T(8,128)(2,1)}, bf16[512,2304]{1,0:T(8,128)(2,1)}, f32[16,512]{1,0:T(8,128)}, bf16[5...) custom-call(s32[1]{0:T(128)} %bitcast.refs_0_, ...), custom_call_target="tpu_custom_call" | custom-call | flops 14495514624 | bytes 20971520 | tf_op jit(solution)/shard_map/block_forward_0_0/pallas_call | solution.py:267
  599.2 1.3 collective-permute-start.1
  600.5 26.2 %block_forward_0_1.1 = (bf16[512,768]{1,0:T(8,128)(2,1)}, bf16[512,768]{1,0:T(8,128)(2,1)}, bf16[512,2304]{1,0:T(8,128)(2,1)}, f32[16,512]{1,0:T(8,128)}, bf16[5...) custom-call(s32[1]{0:T(128)} %bitcast.refs_0_, ...), custom_call_target="tpu_custom_call", output_to_operand_aliasing={{11}: (5, {})} | custom-call | flops 14495514624 | bytes 20971520 | tf_op jit(solution)/shard_map/block_forward_0_1/pallas_call | solution.py:267
  626.7 1.3 collective-permute-start
  628.1 0.0 copy-start.12
  628.1 0.9 copy-done.12
  629.0 1.1 block_forward_1_0.1
  630.1 6.9 block_back_1_0.1
  637.0 1.3 collective-permute-start.3
  638.3 7.0 collective-permute-done.refs_2_
  645.3 0.9 copy-done.9
  646.2 1.0 block_forward_1_1.1
  647.2 7.4 block_back_1_1.1
  654.7 1.3 collective-permute-start.2
  656.0 46.9 %collective-permute-done.3.refs_3_ = bf16[512,768]{1,0:T(8,128)(2,1)S(1)} collective-permute-done((bf16[512,768]{1,0:T(8,128)(2,1)}, bf16[512,768]{1,0:T(8,128)(2,1)S(1)}, u32[]{:S(2)}, u32[]{:S(2)}) %collective-permute-start.3) | collective-permute-done | bytes 786464 | tf_op jit(solution)/shard_map/ppermute | solution.py:734
  702.8 0.9 copy-done.10
  703.7 37.5 %block_back_0_0.1 = (bf16[512,768]{1,0:T(8,128)(2,1)}, bf16[512,3072]{1,0:T(8,128)(2,1)}, bf16[512,768]{1,0:T(8,128)(2,1)}, bf16[512,2304]{1,0:T(8,128)(2,1)}, f...) custom-call(s32[1]{0:T(128)} %bitcast.refs_0_, ...), custom_call_target="tpu_custom_call", output_to_operand_aliasing={{0}: (12, {}), {1}: (13, {}), {2}: (14, {}), {3}: (15, {}),... | custom-call | flops 14495514624 | bytes 31457280 | tf_op jit(solution)/shard_map/block_back_0_0/pallas_call | solution.py:479
  741.2 27.2 %collective-permute-done.2.refs_3_ = bf16[512,768]{1,0:T(8,128)(2,1)S(1)} collective-permute-done((bf16[512,768]{1,0:T(8,128)(2,1)}, bf16[512,768]{1,0:T(8,128)(2,1)S(1)}, u32[]{:S(2)}, u32[]{:S(2)}) %collective-permute-start.2) | collective-permute-done | bytes 786464 | tf_op jit(solution)/shard_map/ppermute | solution.py:734
  768.3 0.9 copy-done.11
  769.2 37.0 %block_back_0_1.1 = (bf16[512,768]{1,0:T(8,128)(2,1)}, bf16[512,3072]{1,0:T(8,128)(2,1)}, bf16[512,768]{1,0:T(8,128)(2,1)}, bf16[512,2304]{1,0:T(8,128)(2,1)}, f...) custom-call(s32[1]{0:T(128)} %bitcast.refs_0_, ...), custom_call_target="tpu_custom_call", output_to_operand_aliasing={{0}: (12, {}), {1}: (13, {}), {2}: (14, {}), {3}: (15, {}),... | custom-call | flops 14495514624 | bytes 31457280 | tf_op jit(solution)/shard_map/block_back_0_1/pallas_call | solution.py:479
  806.3 29.0 %weight_grads.1 = (bf16[432,32,768]{2,1,0:T(8,128)(2,1)}, bf16[64,32,768]{2,1,0:T(8,128)(2,1)}) custom-call(s32[288]{0:T(512)} %bitcast.58, bf16[512,3072]{1,0:T(8,128)(2,1)} %get-tuple-element.157.refs_0_, bf16[512,3072]{1,0:T(8,128)(2,1)} %get-tuple-element.158.refs_1_, bf16[512,768]{1,0:T(8,128)(2,1)} %get-tuple-element.159.refs_2_, ...), custom_call_target="tpu_custom_call" | custom-call | flops 14495514624 | bytes 41943040 | tf_op jit(solution)/shard_map/weight_grads/pallas_call | solution.py:583
  835.2 0.7 conditional.3
  835.2 0.7 broadcast.55
  836.0 0.5 reduce-scatter.5.cloned.1.call-update
  836.5 0.1 copy-done
  836.6 0.3 multiply_cosine_fusion
  836.9 0.7 multiply_convert_fusion.cond
  837.6 0.1 select_reduce_fusion
  837.7 0.6 compare_select_fusion
  838.4 22.3 %all-gather = bf16[16,2,4608]{2,1,0:T(2,128)(2,1)S(1)} all-gather(bf16[1,2,4608]{2,1,0:T(2,128)(2,1)S(1)} %maximum_bitcast_fusion), channel_id=1, replica_groups=mesh['section'=2,'batch'=16] {'batch'}, dimensions={0}, use_global_device_ids=true | all-gather | bytes 313344 | tf_op jit(solution)/shard_map/all_gather | solution.py:750
  860.7 0.1 reshape.80
  860.8 1.4 copy.72
  862.2 190.4 %reduce-scatter.5.cloned.1.call-done = bf16[27,32,768]{2,1,0:T(8,128)(2,1)} async-done(((bf16[432,32,768]{2,1,0:T(8,128)(2,1)}), bf16[27,32,768]{2,1,0:T(8,128)(2,1)}) %reduce-scatter.5.cloned.1.call-update) | async-done | bytes 1327120 | tf_op jit(solution)/shard_map/reduce_scatter | solution.py:740
  1052.7 2.7 pad_maximum_fusion.sums
  1055.4 22.4 %adam.1 = (f32[31,32,768]{2,1,0:T(8,128)}, f32[31,32,768]{2,1,0:T(8,128)}, f32[31,32,768]{2,1,0:T(8,128)}, bf16[31,32,768]{2,1,0:T(8,128)(2,1)}) custom-call(s32[31]{0:T(128)} %get-tuple-element.191.kind_ref, s32[31]{0:T(128)} %get-tuple-element.190.row_ref, f32[31,32,768]{2,1,0:T(8,128)} %bitcast.47, f32[31,32,768]{2,1,0:T(8,128)} %bitcast.50, ...), custom_call_target="tpu_custom_call" | custom-call | bytes 22855680 | tf_op jit(solution)/shard_map/adam/pallas_call | solution.py:637
  (36 shorter events, 0.3 us)
Async XLA Ops:
  9.0 0.6 copy-start.3
  22.0 2.7 copy-start.14
  22.0 3.9 copy-start.13
  24.1 117.9 %all-gather.6.cloned.1.call-start = ((), (), s32[]{:S(2)}) async-start(), calls=%async_computation.5 | async-start | bytes 22560768 | tf_op jit(solution)/shard_map/all_gather | solution.py:690
  37.5 0.5 copy-start.7
  38.2 0.6 copy-start.5
  40.1 15.8 %all-to-all-start = ((f32[16,2,992]{2,1,0:T(2,128)}), f32[16,2,992]{2,1,0:T(2,128)S(1)}, u32[]{:S(2)}, u32[]{:S(2)}) async-start(f32[16,2,992]{2,1,0:T(2,128)} %copy.68), calls=%async_computation.1 | async-start | bytes 262144 | tf_op jit(solution)/shard_map/all_to_all | solution.py:711
  599.2 28.9 %collective-permute-start.1 = (bf16[512,768]{1,0:T(8,128)(2,1)}, bf16[512,768]{1,0:T(8,128)(2,1)S(1)}, u32[]{:S(2)}, u32[]{:S(2)}) collective-permute-start(bf16[512,768]{1,0:T(8,128)(2,1)} %get-tuple-element.100), channel_id=1, source_target_pairs={{0,16},{1,17},{2,18},{3,19},{4,20},{5,21},{6,22},{7,23},{8,24},{9,... | collective-permute-start | bytes 2359304 | tf_op jit(solution)/shard_map/ppermute | solution.py:729
  626.7 18.6 %collective-permute-start = (bf16[512,768]{1,0:T(8,128)(2,1)}, bf16[512,768]{1,0:T(8,128)(2,1)S(1)}, u32[]{:S(2)}, u32[]{:S(2)}) collective-permute-start(bf16[512,768]{1,0:T(8,128)(2,1)} %get-tuple-element.99), channel_id=1, source_target_pairs={{0,16},{1,17},{2,18},{3,19},{4,20},{5,21},{6,22},{7,23},{8,24},{9,... | collective-permute-start | bytes 2359304 | tf_op jit(solution)/shard_map/ppermute | solution.py:729
  628.1 0.9 copy-start.12
  637.0 65.8 %collective-permute-start.3 = (bf16[512,768]{1,0:T(8,128)(2,1)}, bf16[512,768]{1,0:T(8,128)(2,1)S(1)}, u32[]{:S(2)}, u32[]{:S(2)}) collective-permute-start(bf16[512,768]{1,0:T(8,128)(2,1)} %get-tuple-element.148), channel_id=1, source_target_pairs={{16,0},{17,1},{18,2},{19,3},{20,4},{21,5},{22,6},{23,7},{24,8},{25... | collective-permute-start | bytes 2359304 | tf_op jit(solution)/shard_map/ppermute | solution.py:734
  645.3 0.9 copy-start.9
  654.7 113.7 %collective-permute-start.2 = (bf16[512,768]{1,0:T(8,128)(2,1)}, bf16[512,768]{1,0:T(8,128)(2,1)S(1)}, u32[]{:S(2)}, u32[]{:S(2)}) collective-permute-start(bf16[512,768]{1,0:T(8,128)(2,1)} %get-tuple-element.142), channel_id=1, source_target_pairs={{16,0},{17,1},{18,2},{19,3},{20,4},{21,5},{22,6},{23,7},{24,8},{25... | collective-permute-start | bytes 2359304 | tf_op jit(solution)/shard_map/ppermute | solution.py:734
  702.8 0.9 copy-start.10
  768.3 0.9 copy-start.11
  835.9 216.7 %reduce-scatter.5.cloned.1.call-start = ((), (), s32[]{:S(2)}) async-start(), calls=%async_computation.6 | async-start | bytes 22560768 | tf_op jit(solution)/shard_map/reduce_scatter | solution.py:740
  835.9 0.7 copy-start
  835.9 0.7 copy-start.6
  835.9 0.7 copy-start.8
  835.9 1.6 copy-start.4
  835.9 2.3 copy-start.2
  836.0 2.4 copy-start.1
Sparse Core Ops, SparseCore 1:
  26.8 115.2 all-gather.5
  840.5 212.1 reduce-scatter.4

commit v2 on v1

--- a/solution.py
+++ b/solution.py
@@ -77,26 +77,36 @@
     return 0.5 * (1.0 + t) + 0.5 * u * (1.0 - t * t) * (GELU_C * (1.0 + 3.0 * 0.044715 * square))
 
 
+PARTS = 4
+
+
 def assemble_kernel(panels, first_size, index_ref, *refs):
-    sources, sheet, sem = refs[:-2], refs[-2], refs[-1]
-    rows = sheet.shape[1]
-
-    @pl.loop(0, panels)
-    def _(p):
-        where = index_ref[p]
-        if len(sources) == 1:
-            pltpu.make_async_copy(sources[0].at[where], sheet.at[p], sem).start()
-        else:
-
-            @pl.when(where < first_size)
-            def _():
-                pltpu.make_async_copy(sources[0].at[where], sheet.at[p], sem).start()
-
-            @pl.when(where >= first_size)
-            def _():
-                pltpu.make_async_copy(sources[1].at[where - first_size], sheet.at[p], sem).start()
-
-    pltpu.make_async_copy(sheet, sheet, sem).wait()
+    sources, sheet, held, in_sem, out_sem = refs[:-4], refs[-4], refs[-3], refs[-2], refs[-1]
+    size = panels // PARTS
+    for part in range(PARTS):
+
+        @pl.loop(part * size, (part + 1) * size)
+        def _(p):
+            where = index_ref[p]
+            if len(sources) == 1:
+                pltpu.make_async_copy(sources[0].at[where], held.at[p], in_sem.at[part]).start()
+            else:
+
+                @pl.when(where < first_size)
+                def _():
+                    pltpu.make_async_copy(sources[0].at[where], held.at[p], in_sem.at[part]).start()
+
+                @pl.when(where >= first_size)
+                def _():
+                    pltpu.make_async_copy(sources[1].at[where - first_size], held.at[p], in_sem.at[part]).start()
+
+    for part in range(PARTS):
+        span = pl.ds(part * size, size)
+        pltpu.make_async_copy(sheet.at[span], held.at[span], in_sem.at[part]).wait()
+        pltpu.make_async_copy(held.at[span], sheet.at[span], out_sem.at[part]).start()
+    for part in range(PARTS):
+        span = pl.ds(part * size, size)
+        pltpu.make_async_copy(held.at[span], sheet.at[span], out_sem.at[part]).wait()
 
 
 def assemble(index, sources, panels):
@@ -108,7 +118,12 @@
         in_specs=[pl.BlockSpec(memory_space=pltpu.SMEM)]
         + [pl.BlockSpec(memory_space=pl.ANY)] * len(sources),
         out_specs=pl.BlockSpec(memory_space=pl.ANY),
-        scratch_shapes=[pltpu.SemaphoreType.DMA],
+        scratch_shapes=[
+            pltpu.VMEM((panels, rows, D), bf16),
+            pltpu.SemaphoreType.DMA((PARTS,)),
+            pltpu.SemaphoreType.DMA((PARTS,)),
+        ],
+        compiler_params=pltpu.CompilerParams(vmem_limit_bytes=VMEM_LIMIT),
         cost_estimate=pl.CostEstimate(flops=0, bytes_accessed=4 * panels * rows * D, transcendentals=0),
         name="assemble",
     )(index, *sources)
@@ -295,8 +310,10 @@
     return dict(zip(FORWARD_STATE, results)), results[-2], results[-1]
 
 
-BACK_NEEDS = ("xin", "qkv", "lse", "a", "x1", "u", "b")
-BACK_STATE = ("db", "du", "da", "dqkv", "dmod")
+FFN_NEEDS = ("b", "u", "x1", "a")
+FFN_STATE = ("db", "du", "da", "dx1", "dmod_ffn")
+ATT_NEEDS = ("da", "qkv", "lse", "dx1", "xin")
+ATT_STATE = ("dqkv", "dmod_att")
 
 
 def back_shapes(length):
@@ -304,49 +321,39 @@
         "db": ((length, D), bf16),
         "du": ((length, FF), bf16),
         "da": ((length, D), bf16),
+        "dx1": ((length, D), f32),
+        "dmod_ffn": ((4, D), f32),
         "dqkv": ((length, 3 * D), bf16),
-        "dmod": ((6, D), f32),
+        "dmod_att": ((2, D), f32),
     }
 
 
-def back_kernel(want, clip, g_offset, length, chained, *refs):
-    n_need, n_state = len(BACK_NEEDS), len(BACK_STATE)
+def back_ffn_kernel(want, clip, g_offset, length, chained, *refs):
+    n_need, n_state = len(FFN_NEEDS), len(FFN_STATE)
     sec_ref, loss_ref, mod_ref, g_hbm, w_hbm = refs[:5]
-    needs = dict(zip(BACK_NEEDS, refs[5 : 5 + n_need]))
-    refs = refs[5 + n_need :]
-    refs = refs[(n_state if chained else 0) + (1 if clip or chained else 0) :]
-    state = dict(zip(BACK_STATE, refs[:n_state]))
-    gin_hbm, sent_hbm, token_hbm = refs[n_state : n_state + 3]
-    scratch = refs[n_state + 3 :]
+    needs = dict(zip(FFN_NEEDS, refs[5 : 5 + n_need]))
+    refs = refs[5 + n_need + (n_state if chained else 0) :]
+    state = dict(zip(FFN_STATE, refs[:n_state]))
+    scratch = refs[n_state:]
     w = scratch[0]
-    have = dict(zip(BACK_NEEDS, scratch[1 : 1 + n_need]))
-    keep = dict(zip(BACK_STATE, scratch[1 + n_need : 1 + n_need + n_state]))
-    g_low, dx1, acc, do, sent_v, w_sem, g_sem, h_sem, o_sem = scratch[1 + n_need + n_state :]
+    have = dict(zip(FFN_NEEDS, scratch[1 : 1 + n_need]))
+    keep = dict(zip(FFN_STATE, scratch[1 + n_need : 1 + n_need + n_state]))
+    g_low, acc, w_sem, g_sem, h_sem, o_sem = scratch[1 + n_need + n_state :]
 
     @pl.when(sec_ref[0] == want)
     def _():
         get_g = start(g_hbm.at[pl.ds(g_offset, length)], g_low, g_sem)
         get = {}
-        bounds = (0, QKV_END, PROJ_END, UP_END, DOWN_END)
 
         def fetch(name):
-            get[name] = start(needs[name], have[name], h_sem.at[BACK_NEEDS.index(name)])
-
-        def fetch_w(i):
-            span = pl.ds(bounds[i], bounds[i + 1] - bounds[i])
-            get[i] = start(w_hbm.at[span], w.at[span], w_sem.at[i])
+            get[name] = start(needs[name], have[name], h_sem.at[FFN_NEEDS.index(name)])
 
         fetch("b")
-        fetch_w(3)
+        get_down = start(w_hbm.at[pl.ds(UP_END, FF)], w.at[pl.ds(FF, FF)], w_sem.at[0])
         fetch("u")
-        fetch_w(2)
+        get_up = start(w_hbm.at[pl.ds(PROJ_END, FF)], w.at[pl.ds(0, FF)], w_sem.at[1])
         fetch("x1")
         fetch("a")
-        fetch_w(1)
-        fetch("qkv")
-        fetch("lse")
-        fetch_w(0)
-        fetch("xin")
         row = lambda n: mod_ref[clip, n : n + 1, :]
         put = []
 
@@ -355,6 +362,7 @@
 
         get_g.wait()
         get["b"].wait()
+        dx1 = keep["dx1"]
         gate_two = jnp.zeros((1, D), f32)
         for r in range(0, length, ROWS):
             block = pl.ds(r, ROWS)
@@ -364,17 +372,17 @@
             dx1[block, :] = g
             keep["db"][block, :] = (row(5) * g).astype(bf16)
             gate_two += jnp.sum(g * have["b"][block, :].astype(f32), axis=0, keepdims=True)
-        keep["dmod"][5:6, :] = gate_two
+        keep["dmod_ffn"][3:4, :] = gate_two
         save("db")
-        get[3].wait()
+        get_down.wait()
         get["u"].wait()
-        get[2].wait()
+        get_up.wait()
         tile = D
         for n in range(FF // tile):
             span = slice(n * tile, (n + 1) * tile)
-            dz = dot_nt(keep["db"][...], w[UP_END + n * tile : UP_END + (n + 1) * tile, :])
+            dz = dot_nt(keep["db"][...], w[FF + n * tile : FF + (n + 1) * tile, :])
             keep["du"][:, span] = (dz * gelu_slope(have["u"][:, span])).astype(bf16)
-            part = dot_nn(keep["du"][:, span], w[PROJ_END + n * tile : PROJ_END + (n + 1) * tile, :])
+            part = dot_nn(keep["du"][:, span], w[n * tile : (n + 1) * tile, :])
             if n:
                 acc[...] += part
             else:
@@ -394,12 +402,53 @@
             scale_two += scale_part
             gate_one += jnp.sum(total * have["a"][block, :].astype(f32), axis=0, keepdims=True)
             keep["da"][block, :] = (row(2) * total).astype(bf16)
-        keep["dmod"][2:3, :] = gate_one
-        keep["dmod"][3:4, :] = shift_two
-        keep["dmod"][4:5, :] = scale_two
+        keep["dmod_ffn"][0:1, :] = gate_one
+        keep["dmod_ffn"][1:2, :] = shift_two
+        keep["dmod_ffn"][2:3, :] = scale_two
         save("da")
-        get[1].wait()
-        do[...] = dot_nn(keep["da"][...], w[QKV_END:PROJ_END, :]).astype(bf16)
+        save("dx1")
+        save("dmod_ffn")
+        for copy in put:
+            copy.wait()
+
+
+def back_att_kernel(want, clip, length, chained, *refs):
+    n_need, n_state = len(ATT_NEEDS), len(ATT_STATE)
+    sec_ref, mod_ref, w_hbm = refs[:3]
+    needs = dict(zip(ATT_NEEDS, refs[3 : 3 + n_need]))
+    refs = refs[3 + n_need + (n_state if chained else 0) + (1 if clip or chained else 0) :]
+    state = dict(zip(ATT_STATE, refs[:n_state]))
+    gin_hbm, sent_hbm, token_hbm = refs[n_state : n_state + 3]
+    scratch = refs[n_state + 3 :]
+    w = scratch[0]
+    have = dict(zip(ATT_NEEDS, scratch[1 : 1 + n_need]))
+    keep = dict(zip(ATT_STATE, scratch[1 + n_need : 1 + n_need + n_state]))
+    acc, do, sent_v, w_sem, h_sem, o_sem = scratch[1 + n_need + n_state :]
+
+    @pl.when(sec_ref[0] == want)
+    def _():
+        get = {}
+
+        def fetch(name):
+            get[name] = start(needs[name], have[name], h_sem.at[ATT_NEEDS.index(name)])
+
+        fetch("da")
+        get_proj = start(w_hbm.at[pl.ds(QKV_END, D)], w.at[pl.ds(QKV_END, D)], w_sem.at[0])
+        fetch("qkv")
+        fetch("lse")
+        get_qkv = start(w_hbm.at[pl.ds(0, QKV_END)], w.at[pl.ds(0, QKV_END)], w_sem.at[1])
+        fetch("dx1")
+        fetch("xin")
+        row = lambda n: mod_ref[clip, n : n + 1, :]
+        put = []
+
+        def save(name):
+            put.append(start(keep[name], state[name], o_sem.at[len(put)]))
+
+        dx1 = have["dx1"]
+        get["da"].wait()
+        get_proj.wait()
+        do[...] = dot_nn(have["da"][...], w[QKV_END:PROJ_END, :]).astype(bf16)
         get["qkv"].wait()
         get["lse"].wait()
         low_lanes = lax.broadcasted_iota(jnp.int32, (1, 128), 1) < HEAD_DIM
@@ -435,9 +484,10 @@
             keep["dqkv"][:, at(2)] = dv.astype(bf16)
 
         save("dqkv")
-        get[0].wait()
+        get_qkv.wait()
         acc[...] = dot_nn(keep["dqkv"][...], w[0:QKV_END, :])
         get["xin"].wait()
+        get["dx1"].wait()
         shift_one = jnp.zeros((1, D), f32)
         scale_one = jnp.zeros((1, D), f32)
         for r in range(0, length, ROWS):
@@ -448,36 +498,28 @@
             sent_v[block, :] = total.astype(bf16)
             shift_one += shift_part
             scale_one += scale_part
-        keep["dmod"][0:1, :] = shift_one
-        keep["dmod"][1:2, :] = scale_one
-        save("dmod")
+        keep["dmod_att"][0:1, :] = shift_one
+        keep["dmod_att"][1:2, :] = scale_one
         put.append(start(sent_v, sent_hbm, o_sem.at[len(put)]))
+        save("dmod_att")
         put.append(start(dx1, gin_hbm.at[pl.ds(clip * length, length)], o_sem.at[len(put)]))
         for copy in put:
             copy.wait()
 
 
-def back(want, clip, clips, length, section, loss_weight, mod, g, g_offset, sheet, kept, state, gin):
+def back_ffn(want, clip, clips, length, section, loss_weight, mod, g, g_offset, sheet, kept, state):
     shapes, kept_shapes = back_shapes(length), forward_shapes(length)
     any_spec = pl.BlockSpec(memory_space=pl.ANY)
     chained = state is not None
-    operands = [section, loss_weight, mod, g, sheet] + [kept[name] for name in BACK_NEEDS]
+    operands = [section, loss_weight, mod, g, sheet] + [kept[name] for name in FFN_NEEDS]
     aliases = {}
     if chained:
-        for n, name in enumerate(BACK_STATE):
+        for n, name in enumerate(FFN_STATE):
             aliases[len(operands)] = n
             operands.append(state[name])
-    if gin is not None:
-        aliases[len(operands)] = len(BACK_STATE)
-        operands.append(gin)
-    out_shape = [jax.ShapeDtypeStruct(*shapes[name]) for name in BACK_STATE]
-    out_shape += [
-        jax.ShapeDtypeStruct((clips * length, D), f32),
-        jax.ShapeDtypeStruct((length, D), bf16),
-        jax.ShapeDtypeStruct((8, 128), f32),
-    ]
+    out_shape = [jax.ShapeDtypeStruct(*shapes[name]) for name in FFN_STATE]
     results = pl.pallas_call(
-        functools.partial(back_kernel, want, clip, g_offset, length, chained),
+        functools.partial(back_ffn_kernel, want, clip, g_offset, length, chained),
         out_shape=out_shape,
         in_specs=[
             pl.BlockSpec(memory_space=pltpu.SMEM),
@@ -486,57 +528,96 @@
         ]
         + [any_spec] * (len(operands) - 3),
         out_specs=[any_spec] * len(out_shape),
-        scratch_shapes=[pltpu.VMEM((DOWN_END, D), bf16)]
-        + [pltpu.VMEM(*kept_shapes[name]) for name in BACK_NEEDS]
-        + [pltpu.VMEM(*shapes[name]) for name in BACK_STATE]
+        scratch_shapes=[pltpu.VMEM((2 * FF, D), bf16)]
+        + [pltpu.VMEM(*kept_shapes[name]) for name in FFN_NEEDS]
+        + [pltpu.VMEM(*shapes[name]) for name in FFN_STATE]
         + [
             pltpu.VMEM((length, D), bf16),
             pltpu.VMEM((length, D), f32),
+            pltpu.SemaphoreType.DMA((2,)),
+            pltpu.SemaphoreType.DMA,
+            pltpu.SemaphoreType.DMA((len(FFN_NEEDS),)),
+            pltpu.SemaphoreType.DMA((len(FFN_STATE),)),
+        ],
+        input_output_aliases=aliases,
+        compiler_params=pltpu.CompilerParams(vmem_limit_bytes=VMEM_LIMIT),
+        cost_estimate=pl.CostEstimate(flops=15 * 10**9, bytes_accessed=24 << 20, transcendentals=0),
+        name=f"back_ffn_{want}_{clip}",
+    )(*operands)
+    return dict(zip(FFN_STATE, results))
+
+
+def back_att(want, clip, clips, length, section, mod, sheet, kept, ffn, state, gin):
+    shapes, kept_shapes = back_shapes(length), forward_shapes(length)
+    every = {**kept_shapes, **shapes}
+    any_spec = pl.BlockSpec(memory_space=pl.ANY)
+    chained = state is not None
+    operands = [section, mod, sheet] + [{**kept, **ffn}[name] for name in ATT_NEEDS]
+    aliases = {}
+    if chained:
+        for n, name in enumerate(ATT_STATE):
+            aliases[len(operands)] = n
+            operands.append(state[name])
+    if gin is not None:
+        aliases[len(operands)] = len(ATT_STATE)
+        operands.append(gin)
+    out_shape = [jax.ShapeDtypeStruct(*shapes[name]) for name in ATT_STATE]
+    out_shape += [
+        jax.ShapeDtypeStruct((clips * length, D), f32),
+        jax.ShapeDtypeStruct((length, D), bf16),
+        jax.ShapeDtypeStruct((8, 128), f32),
+    ]
+    results = pl.pallas_call(
+        functools.partial(back_att_kernel, want, clip, length, chained),
+        out_shape=out_shape,
+        in_specs=[
+            pl.BlockSpec(memory_space=pltpu.SMEM),
+            pl.BlockSpec(memory_space=pltpu.VMEM),
+        ]
+        + [any_spec] * (len(operands) - 2),
+        out_specs=[any_spec] * len(out_shape),
+        scratch_shapes=[pltpu.VMEM((PROJ_END, D), bf16)]
+        + [pltpu.VMEM(*every[name]) for name in ATT_NEEDS]
+        + [pltpu.VMEM(*shapes[name]) for name in ATT_STATE]
+        + [
             pltpu.VMEM((length, D), f32),
             pltpu.VMEM((length, D), bf16),
             pltpu.VMEM((length, D), bf16),
-            pltpu.SemaphoreType.DMA((4,)),
-            pltpu.SemaphoreType.DMA,
-            pltpu.SemaphoreType.DMA((len(BACK_NEEDS),)),
-            pltpu.SemaphoreType.DMA((len(BACK_STATE) + 2,)),
+            pltpu.SemaphoreType.DMA((2,)),
+            pltpu.SemaphoreType.DMA((len(ATT_NEEDS),)),
+            pltpu.SemaphoreType.DMA((len(ATT_STATE) + 2,)),
         ],
         input_output_aliases=aliases,
         compiler_params=pltpu.CompilerParams(vmem_limit_bytes=VMEM_LIMIT),
-        cost_estimate=pl.CostEstimate(
-            flops=2 * length * DOWN_END * D * 2, bytes_accessed=30 << 20, transcendentals=length * length * HEADS
-        ),
-        name=f"block_back_{want}_{clip}",
+        cost_estimate=pl.CostEstimate(flops=20 * 10**9, bytes_accessed=16 << 20, transcendentals=0),
+        name=f"back_att_{want}_{clip}",
     )(*operands)
-    return dict(zip(BACK_STATE, results)), results[-3], results[-2], results[-1]
-
-
-GRAD_PAIRS = (("z", "db", UP_END), ("du", "h2", PROJ_END), ("da", "o", QKV_END), ("dqkv", "h1", 0))
-
-
-def grads_kernel(clips, length, panel_rows, first_size, two, dest_ref, *refs):
-    count = 2 * len(GRAD_PAIRS) * clips
+    return dict(zip(ATT_STATE, results)), results[-3], results[-2], results[-1]
+
+
+def grads_kernel(jobs, clips, length, panel_rows, own, threaded, code_ref, index_ref, *refs):
+    count = 2 * len(jobs) * clips
     sources = refs[:count]
-    outs = refs[count : count + (2 if two else 1)]
-    scratch = refs[count + (2 if two else 1) :]
-    values = scratch[: 2 * len(GRAD_PAIRS)]
-    tile_v, in_sem, out_sem = scratch[2 * len(GRAD_PAIRS) :]
-    get = []
-    for n in range(2 * len(GRAD_PAIRS)):
-        get.append(
-            [
-                start(sources[n * clips + c], values[n].at[pl.ds(c * length, length)], in_sem.at[n, c])
-                for c in range(clips)
-            ]
-        )
+    refs = refs[count + threaded :]
+    outs = refs[:own]
+    scratch = refs[own:]
+    values = scratch[: 2 * len(jobs)]
+    tile_v, in_sem, out_sem = scratch[2 * len(jobs) :]
+    get = [
+        [
+            start(sources[n * clips + c], values[n].at[pl.ds(c * length, length)], in_sem.at[n, c])
+            for c in range(clips)
+        ]
+        for n in range(2 * len(jobs))
+    ]
     tiles = []
-    for n, (left, right, base) in enumerate(GRAD_PAIRS):
-        width = values[2 * n].shape[1]
-        tiles += [(n, column, base + column) for column in range(0, width, D)]
+    for n, (left, right, base) in enumerate(jobs):
+        tiles += [(n, column, base + column) for column in range(0, values[2 * n].shape[1], D)]
     per_tile = D // panel_rows
     seen = set()
 
     def drain(slot):
-        pltpu.make_async_copy(outs[0].at[pl.ds(0, per_tile)], tile_v.at[slot], out_sem.at[slot]).wait()
+        pltpu.make_async_copy(outs[-1].at[pl.ds(0, per_tile)], tile_v.at[slot], out_sem.at[slot]).wait()
 
     for t, (n, column, first_row) in enumerate(tiles):
         slot = t % 2
@@ -551,105 +632,191 @@
 
         @pl.loop(0, per_tile)
         def _(p):
-            where = dest_ref[first_row // panel_rows + p]
-            if not two:
-                pltpu.make_async_copy(tile_v.at[slot, p], outs[0].at[where], out_sem.at[slot]).start()
-            else:
-
-                @pl.when(where < first_size)
+            code = code_ref[first_row // panel_rows + p]
+            where = index_ref[first_row // panel_rows + p]
+            for n_out in range(own):
+
+                @pl.when(code == n_out)
                 def _():
-                    pltpu.make_async_copy(tile_v.at[slot, p], outs[0].at[where], out_sem.at[slot]).start()
-
-                @pl.when(where >= first_size)
-                def _():
-                    pltpu.make_async_copy(
-                        tile_v.at[slot, p], outs[1].at[where - first_size], out_sem.at[slot]
-                    ).start()
-
-    drain(0)
-    drain(1)
-
-
-def weight_grads(dest, kept, backs, length, panel_rows, sizes):
-    clips = len(kept)
+                    pltpu.make_async_copy(tile_v.at[slot, p], outs[n_out].at[where], out_sem.at[slot]).start()
+
+    for slot in range(min(2, len(tiles))):
+        drain(slot)
+
+
+def weight_grads(jobs, code, index, every, length, panel_rows, sizes, thread):
+    clips = len(every)
     any_spec = pl.BlockSpec(memory_space=pl.ANY)
-    operands, scratch = [], []
-    for left, right, _ in GRAD_PAIRS:
+    operands, scratch = [code, index], []
+    for left, right, _ in jobs:
         for name in (left, right):
-            arrays = [{**kept[c], **backs[c]}[name] for c in range(clips)]
+            arrays = [every[c][name] for c in range(clips)]
             operands += arrays
             scratch.append(pltpu.VMEM((clips * length, arrays[0].shape[1]), bf16))
-    two = len(sizes) == 2
+    aliases = {}
+    for n, array in enumerate(thread):
+        aliases[len(operands)] = len(sizes) - len(thread) + n
+        operands.append(array)
+    width = sum(s.shape[1] for s in scratch[0::2])
     return pl.pallas_call(
-        functools.partial(grads_kernel, clips, length, panel_rows, sizes[0], two),
+        functools.partial(grads_kernel, jobs, clips, length, panel_rows, len(sizes), len(thread)),
         out_shape=[jax.ShapeDtypeStruct((size, panel_rows, D), bf16) for size in sizes],
-        in_specs=[pl.BlockSpec(memory_space=pltpu.SMEM)] + [any_spec] * len(operands),
+        in_specs=[pl.BlockSpec(memory_space=pltpu.SMEM)] * 2 + [any_spec] * (len(operands) - 2),
         out_specs=[any_spec] * len(sizes),
         scratch_shapes=scratch
         + [
             pltpu.VMEM((2, D // panel_rows, panel_rows, D), bf16),
-            pltpu.SemaphoreType.DMA((2 * len(GRAD_PAIRS), clips)),
+            pltpu.SemaphoreType.DMA((2 * len(jobs), clips)),
             pltpu.SemaphoreType.DMA((2,)),
         ],
+        input_output_aliases=aliases,
         compiler_params=pltpu.CompilerParams(vmem_limit_bytes=VMEM_LIMIT),
         cost_estimate=pl.CostEstimate(
-            flops=2 * clips * length * DOWN_END * D, bytes_accessed=40 << 20, transcendentals=0
+            flops=4 * clips * length * width * D, bytes_accessed=12 << 20, transcendentals=0
         ),
-        name="weight_grads",
-    )(dest, *operands)
-
-
-def adam_kernel(kind_ref, row_ref, master, first, second, sums, dmod, cond, master_o, first_o, second_o, copy_o):
-    slot = pl.program_id(0)
-    rows = master.shape[1]
-    kind = kind_ref[slot]
-
-    def update(grad):
-        first_next = beta_one * first[0] + (1.0 - beta_one) * grad
-        second_next = beta_two * second[0] + (1.0 - beta_two) * grad * grad
-        first_hat = first_next / (1.0 - beta_one**STEP)
-        second_hat = second_next / (1.0 - beta_two**STEP)
-        value = master[0] - learn_rate * (
-            first_hat / (jnp.sqrt(second_hat) + adam_eps) + decay_rate * master[0]
-        )
-        master_o[0] = value
-        first_o[0] = first_next
-        second_o[0] = second_next
-        copy_o[0] = value.astype(bf16)
-
-    @pl.when(kind == 0)
-    def _():
-        update(jnp.zeros((rows, D), f32))
-
-    @pl.when(kind == 1)
-    def _():
-        update(sums[0].astype(f32))
-
-    @pl.when(kind == 2)
-    def _():
-        at = pl.multiple_of(row_ref[slot], rows)
-        update(dot_nn(dmod[pl.ds(at, rows), :], cond[...]))
-
-
-def adam(kind, row, master, first, second, sums, dmod, cond):
+        name="weight_grads_" + jobs[0][0],
+    )(*operands)
+
+
+GROUP = 8
+
+
+def adam_kernel(n_sums, code_ref, index_ref, row_ref, master, first, second, dmod, cond, *refs):
+    sums = refs[:n_sums]
+    outs = refs[n_sums : n_sums + 4]
+    scratch = refs[n_sums + 4 :]
+    held = scratch[:3]
+    made = scratch[3:7]
+    grad_v, in_sem, grad_sem, out_sem = scratch[7:]
     slots, rows = master.shape[0], master.shape[1]
-    block = pl.BlockSpec((1, rows, D), lambda s, *_: (s, 0, 0))
+    groups = [(g, min(GROUP, slots - g)) for g in range(0, slots, GROUP)]
+    get = [
+        [start(a.at[pl.ds(g, size)], h.at[pl.ds(g, size)], in_sem.at[n, i]) for i, (a, h) in enumerate(zip((master, first, second), held))]
+        for n, (g, size) in enumerate(groups)
+    ]
+    for n, (g, size) in enumerate(groups):
+
+        @pl.loop(g, g + size)
+        def _(slot):
+            code = code_ref[slot]
+            where = index_ref[slot]
+            for n_sum in range(n_sums):
+
+                @pl.when(code == n_sum)
+                def _():
+                    pltpu.make_async_copy(sums[n_sum].at[where], grad_v.at[slot], grad_sem.at[n]).start()
+
+    put = []
+    for n, (g, size) in enumerate(groups):
+        for copy in get[n]:
+            copy.wait()
+        span = pl.ds(g, size)
+
+        @pl.loop(g, g + size)
+        def _(slot):
+            code = code_ref[slot]
+
+            @pl.when(code < n_sums)
+            def _():
+                pltpu.make_async_copy(sums[0].at[0], grad_v.at[slot], grad_sem.at[n]).wait()
+
+        @pl.loop(g, g + size)
+        def _(slot):
+            code = code_ref[slot]
+
+            def update(grad):
+                first_next = beta_one * held[1][slot] + (1.0 - beta_one) * grad
+                second_next = beta_two * held[2][slot] + (1.0 - beta_two) * grad * grad
+                first_hat = first_next / (1.0 - beta_one**STEP)
+                second_hat = second_next / (1.0 - beta_two**STEP)
+                value = held[0][slot] - learn_rate * (
+                    first_hat / (jnp.sqrt(second_hat) + adam_eps) + decay_rate * held[0][slot]
+                )
+                made[0][slot] = value
+                made[1][slot] = first_next
+                made[2][slot] = second_next
+                made[3][slot] = value.astype(bf16)
+
+            @pl.when(code < n_sums)
+            def _():
+                update(grad_v[slot].astype(f32))
+
+            @pl.when(code == n_sums)
+            def _():
+                at = pl.multiple_of(row_ref[slot], rows)
+                update(dot_nn(dmod[pl.ds(at, rows), :], cond[...]))
+
+            @pl.when(code > n_sums)
+            def _():
+                update(jnp.zeros((rows, D), f32))
+
+        for i in range(4):
+            put.append(start(made[i].at[span], outs[i].at[span], out_sem.at[n, i]))
+    for copy in put:
+        copy.wait()
+
+
+def adam(code, index, row, master, first, second, dmod, cond, sums):
+    slots, rows = master.shape[0], master.shape[1]
+    any_spec = pl.BlockSpec(memory_space=pl.ANY)
+    smem, vmem = pl.BlockSpec(memory_space=pltpu.SMEM), pl.BlockSpec(memory_space=pltpu.VMEM)
+    kinds = [f32, f32, f32, bf16]
+    groups = -(-slots // GROUP)
     return pl.pallas_call(
-        adam_kernel,
-        grid_spec=pltpu.PrefetchScalarGridSpec(
-            num_scalar_prefetch=2,
-            grid=(slots,),
-            in_specs=[block] * 4
-            + [
-                pl.BlockSpec(dmod.shape, lambda s, *_: (0, 0)),
-                pl.BlockSpec(cond.shape, lambda s, *_: (0, 0)),
-            ],
-            out_specs=[block] * 4,
-        ),
-        out_shape=[jax.ShapeDtypeStruct(master.shape, f32)] * 3 + [jax.ShapeDtypeStruct(master.shape, bf16)],
+        functools.partial(adam_kernel, len(sums)),
+        in_specs=[smem] * 3 + [any_spec] * 3 + [vmem] * 2 + [any_spec] * len(sums),
+        out_specs=[any_spec] * 4,
+        out_shape=[jax.ShapeDtypeStruct(master.shape, kind) for kind in kinds],
+        scratch_shapes=[pltpu.VMEM(master.shape, f32)] * 3
+        + [pltpu.VMEM(master.shape, kind) for kind in kinds]
+        + [
+            pltpu.VMEM(master.shape, bf16),
+            pltpu.SemaphoreType.DMA((groups, 3)),
+            pltpu.SemaphoreType.DMA((groups,)),
+            pltpu.SemaphoreType.DMA((groups, 4)),
+        ],
+        compiler_params=pltpu.CompilerParams(vmem_limit_bytes=VMEM_LIMIT),
         cost_estimate=pl.CostEstimate(flops=0, bytes_accessed=slots * rows * D * 30, transcendentals=0),
         name="adam",
-    )(kind, row, master, first, second, sums, dmod, cond)
+    )(code, index, row, master, first, second, dmod, cond, *sums)
+
+
+CHIPS = 8
+LOOP = (0, 2, 4, 6, 7, 5, 3, 1)
+
+
+def swap_cores(value):
+    return lax.ppermute(value, "batch", [(d, d ^ 1) for d in range(2 * CHIPS)])
+
+
+def along(value, step):
+    pairs = [
+        (2 * LOOP[n] + core, 2 * LOOP[(n + step) % CHIPS] + core) for n in range(CHIPS) for core in range(2)
+    ]
+    return lax.ppermute(value, "batch", pairs)
+
+
+def ring_sum(place, mine, other):
+    size = mine.shape[0] // CHIPS
+    half = size // 2
+    partner = swap_cores(other)
+
+    def term(offset, low, high):
+        first = ((place + offset) % CHIPS) * size + low
+        return sum(
+            lax.dynamic_slice_in_dim(a, first, high - low, 0).astype(f32) for a in (mine, partner)
+        )
+
+    ahead = along(term(4, 0, half).astype(bf16), 1)
+    behind = along(term(-4, half, size).astype(bf16), -1)
+    ahead = jnp.concatenate([(term(3, 0, half) + ahead.astype(f32)).astype(bf16), term(3, half, size).astype(bf16)])
+    behind = jnp.concatenate([term(-3, 0, half).astype(bf16), (term(-3, half, size) + behind.astype(f32)).astype(bf16)])
+    for hop in (2, 1):
+        ahead, behind = along(ahead, 1), along(behind, -1)
+        ahead = (term(hop, 0, size) + ahead.astype(f32)).astype(bf16)
+        behind = (term(-hop, 0, size) + behind.astype(f32)).astype(bf16)
+    ahead, behind = along(ahead, 1), along(behind, -1)
+    return (term(0, 0, size) + ahead.astype(f32) + behind.astype(f32)).astype(bf16)
 
 
 def time_features(steps_in):
@@ -721,35 +888,114 @@
 
     run = functools.partial
     fwd = run(forward, clips=clips, length=length, section=section, mod=mod, sheet=sheet)
-    bwd = run(back, clips=clips, length=length, section=section, loss_weight=loss_weight, mod=mod, sheet=sheet)
+    ffn = run(back_ffn, clips=clips, length=length, section=section, loss_weight=loss_weight, mod=mod, sheet=sheet)
+    att = run(back_att, clips=clips, length=length, section=section, mod=mod, sheet=sheet)
     token = jnp.zeros((8, 128), f32)
     kept, sent, outs = [None] * clips, [None] * clips, None
     for c in range(clips):
         kept[c], outs, sent[c] = fwd(0, c, x=tokens, x_offset=c * length, token=token, state=None, outs=outs)
     received = [lax.ppermute(rows, "section", [(0, 1)]) for rows in sent]
-    backs, gin = [None] * clips, None
+    backs, atts, gin = [None] * clips, [None] * clips, None
     for c in range(clips):
         kept[c], outs, _ = fwd(1, c, x=received[c], x_offset=0, token=token, state=kept[c], outs=outs)
-        backs[c], gin, sent[c], token = bwd(1, c, g=cotangent, g_offset=c * length, kept=kept[c], state=None, gin=gin)
+        backs[c] = ffn(1, c, g=cotangent, g_offset=c * length, kept=kept[c], state=None)
+        atts[c], gin, sent[c], token = att(1, c, kept=kept[c], ffn=backs[c], state=None, gin=gin)
     received = [lax.ppermute(rows, "section", [(1, 0)]) for rows in sent]
     for c in range(clips):
-        backs[c], gin, _, token = bwd(0, c, g=received[c], g_offset=0, kept=kept[c], state=backs[c], gin=gin)
-
-    sizes = [first_size] + ([owner_total * (slots - cap)] if cap < slots else [])
-    grads = weight_grads(place, kept, backs, length, panel_rows, sizes)
-    sums = lax.psum_scatter(grads[0], "batch", scatter_dimension=0, tiled=True)
-    if cap < slots:
-        more = lax.cond(
-            over,
-            lambda part: lax.psum_scatter(part, "batch", scatter_dimension=0, tiled=True),
-            lambda part: jnp.zeros((slots - cap, panel_rows, D), bf16),
-            grads[1],
+        backs[c] = ffn(0, c, g=received[c], g_offset=0, kept=kept[c], state=backs[c])
+        if c < clips - 1:
+            atts[c], gin, _, token = att(0, c, kept=kept[c], ffn=backs[c], state=atts[c], gin=gin)
+
+    code, index, slot_code, slot_index, sizes, beyond = routes(owner, rank, mine, me, owner_total, slots, moved)
+    if beyond is not None:
+        beyond = lax.pmax(beyond.astype(f32), "section") > 0.5
+    grads = run(weight_grads, code=code, index=index, length=length, panel_rows=panel_rows)
+    last = clips - 1
+    every = [{**kept[c], **backs[c]} for c in range(clips)]
+    if owner_total == 2 * CHIPS:
+        place = me // 4 + (me // 2) % 2 * (CHIPS - 1 - 2 * (me // 4))
+        sums, thread = [], []
+        for jobs, chunk in (((("z", "db", UP_END),), 0), ((("du", "h2", PROJ_END),), 1), ((("da", "o", QKV_END), ("dqkv", "h1", 0)), 2)):
+            if chunk == 2:
+                atts[last], gin, _, token = att(
+                    0, last, kept=kept[last], ffn=backs[last], state=atts[last], gin=gin
+                )
+                every = [{**every[c], **atts[c]} for c in range(clips)]
+                made = grads(jobs, every=every, sizes=[sizes[2]] * 2 + [sizes[3]], thread=thread)
+                pair = made[:2]
+                rest = made[2]
+            else:
+                made = grads(
+                    jobs, every=every, sizes=[sizes[chunk]] * 2 + [sizes[2]] * 2 + [sizes[3]], thread=thread
+                )
+                pair, thread = made[:2], made[2:]
+            half = ring_sum(place, *pair)
+            sums += [half, swap_cores(half)]
+        sums.append(
+            lax.cond(
+                beyond,
+                lambda part: lax.psum_scatter(part, "batch", scatter_dimension=0, tiled=True),
+                lambda part: jnp.zeros((slots, panel_rows, D), bf16),
+                rest,
+            )
         )
-        sums = jnp.concatenate([sums, more], axis=0)
-    dmod = jnp.stack([b["dmod"] for b in backs]).reshape(clips, 6 * D).astype(bf16)
+    else:
+        atts[last], gin, _, token = att(0, last, kept=kept[last], ffn=backs[last], state=atts[last], gin=gin)
+        every = [{**every[c], **atts[c]} for c in range(clips)]
+        jobs = (("z", "db", UP_END), ("du", "h2", PROJ_END), ("da", "o", QKV_END), ("dqkv", "h1", 0))
+        (made,) = grads(jobs, every=every, sizes=[sizes[0]], thread=[])
+        sums = [lax.psum_scatter(made, "batch", scatter_dimension=0, tiled=True)]
+    dmod = [jnp.concatenate([t["dmod_att"], b["dmod_ffn"]]) for t, b in zip(atts, backs)]
+    dmod = jnp.stack(dmod).reshape(clips, 6 * D).astype(bf16)
     dmod = lax.all_gather(dmod, "batch", axis=0, tiled=True).T
-    results = adam(kind, mod_row, master[0], first_moment[0], second_moment[0], sums, dmod, cond)
+    slot_code = jnp.where(kind == 1, slot_code, jnp.where(kind == 2, len(sums), len(sums) + 1))
+    results = adam(
+        slot_code, slot_index, mod_row, master[0], first_moment[0], second_moment[0], dmod, cond, sums
+    )
     return (outs[None], gin[None], *(r[None] for r in results))
+
+
+CAPS = (12, 12, 26)
+
+
+def count_before(flag, group):
+    number = jnp.arange(group.shape[0], dtype=jnp.int32)
+    before = (group[:, None] == group[None, :]) & (number[None, :] < number[:, None]) & flag[None, :]
+    return jnp.sum(before.astype(jnp.int32), axis=1)
+
+
+def routes(owner, rank, mine, me, owner_total, slots, moved):
+    if owner_total != 2 * CHIPS:
+        code = jnp.zeros((moved,), jnp.int32)
+        return code, (owner * slots + rank)[:moved], jnp.zeros((slots,), jnp.int32), jnp.arange(slots, dtype=jnp.int32), [owner_total * slots], None
+    number = jnp.arange(moved, dtype=jnp.int32)
+    held, core = owner[:moved], me % 2
+    chip = held // 2
+    spot = chip // 2 + chip % 2 * (CHIPS - 1 - 2 * (chip // 2))
+    per_row = DOWN_END // moved
+    down, up = number >= UP_END // per_row, (number >= PROJ_END // per_row) & (number < UP_END // per_row)
+    kind = jnp.where(down, 0, jnp.where(up, 1, 2))
+    order = jnp.where(
+        down, count_before(down, chip), jnp.where(up, count_before(up, chip), 0)
+    )
+    cap = jnp.where(down, CAPS[0], jnp.where(up, CAPS[1], 0))
+    late = order >= cap
+    order = jnp.where(late, count_before(late, chip), order)
+    chunk = jnp.where(late, 2, kind)
+    rest = late & (order >= CAPS[2])
+    half = order % 2
+    size = jnp.where(chunk == 0, CAPS[0] // 2, jnp.where(chunk == 1, CAPS[1] // 2, CAPS[2] // 2))
+    index = jnp.where(rest, held * slots + rank[:moved], spot * size + order // 2)
+    away = (half != core).astype(jnp.int32)
+    code = jnp.where(rest, 4, jnp.where(chunk == 2, 2 + away, away))
+    last = number < PROJ_END // per_row
+    code = jnp.where(last, code - 2, code).astype(jnp.int32)
+    taken = mine[:, :moved].astype(jnp.int32)
+    found = jnp.where(rest, 6, 2 * chunk + away)
+    slot_code = jnp.sum(taken * found[None, :], axis=1)
+    slot_index = jnp.sum(taken * jnp.where(rest, rank[:moved], order // 2)[None, :], axis=1)
+    sizes = [CHIPS * CAPS[n] // 2 for n in range(3)] + [owner_total * slots]
+    return code, index.astype(jnp.int32), slot_code.astype(jnp.int32), slot_index.astype(jnp.int32), sizes, jnp.any(rest)
 
 
 def solution(mesh):

time: 1090 us -> 612 us (0.56)
  Pallas kernels: 625 us -> 212 us
  waiting for transfers between devices: 366 us -> 237 us
  starting transfers between devices: 11.8 us -> 48.6 us
  other arithmetic: 10.8 us -> 36.8 us
    pallas_call x1, Pallas kernels: 431 us -> 10.4 us  [assemble(): pl.pallas_call(functools.partial(assemble_kernel, panels, first_size), ou...]
    reduce_scatter x1 -> x0, waiting for transfers between devices: 190 us -> none  [body(): sums = lax.psum_scatter(grads[0], 'batch', scatter_dimension=0, tiled=True)]
    ppermute x0 -> x30, waiting for transfers between devices: none -> 66.9 us  [the longest x24 57.4 us: along(): return lax.ppermute(value, 'batch', pairs)]
    ppermute x0 -> x30, starting transfers between devices: none -> 36.8 us  [the longest x24 20.9 us: along(): return lax.ppermute(value, 'batch', pairs)]
    convert_element_type x0 -> x22, other arithmetic: none -> 26.8 us  [the longest x6 8.02 us: ring_sum(): ahead = (term(hop, 0, size) + ahead.astype(f32)).astype(bf16)]
    pallas_call x6 -> x12, Pallas kernels: 140 us -> 148 us  [the longest x4 50.4 us: back_ffn(): pl.pallas_call(functools.partial(back_ffn_kernel, want, clip, g_offset, l...]
  transfers between devices with their start and end apart: 7 -> 36, of which waited for: 6 -> 17; matrix products, arithmetic and copies ran while one was open for 1% -> 6% of each run, Pallas kernels for 7% -> 14%
where the time goes in v2:
time: 612 us; the launch traced here: 607 us
  waiting for transfers between devices  237 us (39%)
  Pallas kernels  212 us (35%)
  starting transfers between devices  48.6 us (8%)
  other arithmetic  36.8 us (6%)
  blocking collectives  36.5 us (6%)
  between operations  19.9 us (3%)
  local copies, waits for them, and re-layouts  15.1 us (2%)
    all_gather x1, waiting for transfers between devices, body(): sources = [lax.all_gather(low[:cap], 'batch', axis=0, tiled=True)]  84.5 us
    ppermute x2, waiting for transfers between devices, body(): received = [lax.ppermute(rows, 'section', [(1, 0)]) for rows in sent]  72.4 us
    ppermute x24, waiting for transfers between devices, along(): return lax.ppermute(value, 'batch', pairs)  57.4 us
    pallas_call x4, Pallas kernels, forward(): pl.pallas_call(functools.partial(forward_kernel, want, clip, x_offset, le...  54.4 us
    pallas_call x4, Pallas kernels, back_ffn(): pl.pallas_call(functools.partial(back_ffn_kernel, want, clip, g_offset, l...  50.4 us
    pallas_call x4, Pallas kernels, back_att(): pl.pallas_call(functools.partial(back_att_kernel, want, clip, length, cha...  48 us
    pallas_call x3, Pallas kernels, weight_grads(): pl.pallas_call(functools.partial(grads_kernel, jobs, clips, length, panel...  38.3 us
    ppermute x24, starting transfers between devices, along(): return lax.ppermute(value, 'batch', pairs)  20.9 us
  transfers between devices with their start and end apart: 36, of which 17 were waited for; matrix products, arithmetic and copies ran while one was open for 6% of the time, Pallas kernels for 14%

profile of v2, /device:TPU:1, one launch (start us, length us, event | category | flops | bytes accessed | tf_op | source)
XLA Modules:
  0.0 606.8 jit_solution(16697216456305520582)
XLA Ops:
  8.0 3.2 bitcast_convert_fusion
  17.0 4.8 all-reduce.2
  22.5 2.0 conditional.2
  22.5 2.0 broadcast.247
  26.6 11.3 %all-reduce = s32[32]{0:T(128)S(1)} all-reduce(s32[32]{0:T(128)S(1)} %dynamic-update-slice), channel_id=1, replica_groups=mesh['section'=2,'batch'=16] {'batch'}, use_global_device_ids=true, to_apply=%add | all-reduce | flops 32 | bytes 256
  40.5 6.5 %all-to-all-start = ((f32[16,2,992]{2,1,0:T(2,128)}), f32[16,2,992]{2,1,0:T(2,128)S(1)}, u32[]{:S(2)}, u32[]{:S(2)}) async-start(f32[16,2,992]{2,1,0:T(2,128)} %copy.78), calls=%async_computation.1 | async-start | bytes 262144 | tf_op jit(solution)/shard_map/all_to_all | solution.py:878
  47.8 8.6 %all-to-all-done = f32[16,2,992]{2,1,0:T(2,128)S(1)} async-done(((f32[16,2,992]{2,1,0:T(2,128)}), f32[16,2,992]{2,1,0:T(2,128)S(1)}, u32[]{:S(2)}, u32[]{:S(2)}) %all-to-all-start) | async-done | bytes 127008 | tf_op jit(solution)/shard_map/all_to_all | solution.py:878
  58.1 84.5 %all-gather.6.cloned.1.call-done.refs_0_ = bf16[432,32,768]{2,1,0:T(8,128)(2,1)} async-done(((bf16[27,32,768]{2,1,0:T(8,128)(2,1)}), bf16[432,32,768]{2,1,0:T(8,128)(2,1)}) %all-gather.6.cloned.1.call-update) | async-done | bytes 21233680 | tf_op jit(solution)/shard_map/all_gather | solution.py:857
  142.6 10.4 %assemble.1 = bf16[288,32,768]{2,1,0:T(8,128)(2,1)} custom-call(s32[288]{0:T(512)} %bitcast.62, bf16[432,32,768]{2,1,0:T(8,128)(2,1)} %all-gather.6.cloned.1.call-done.refs_0_, bf16[64,32,768]{2,1,0:T(8,128)(2,1)} %get-tuple-element.264.refs_1_), custom_call_target="tpu_custom_call" | custom-call | bytes 28311552 | tf_op jit(solution)/shard_map/assemble/pallas_call | solution.py:115
  153.5 25.9 %block_forward_0_0.1 = (bf16[512,768]{1,0:T(8,128)(2,1)}, bf16[512,768]{1,0:T(8,128)(2,1)}, bf16[512,2304]{1,0:T(8,128)(2,1)}, f32[16,512]{1,0:T(8,128)}, bf16[5...) custom-call(s32[1]{0:T(128)} %bitcast.refs_0_, ...), custom_call_target="tpu_custom_call" | custom-call | flops 14495514624 | bytes 20971520 | tf_op jit(solution)/shard_map/block_forward_0_0/pallas_call | solution.py:282
  179.4 1.3 collective-permute-start.1
  180.8 26.0 %block_forward_0_1.1 = (bf16[512,768]{1,0:T(8,128)(2,1)}, bf16[512,768]{1,0:T(8,128)(2,1)}, bf16[512,2304]{1,0:T(8,128)(2,1)}, f32[16,512]{1,0:T(8,128)}, bf16[5...) custom-call(s32[1]{0:T(128)} %bitcast.refs_0_, ...), custom_call_target="tpu_custom_call", output_to_operand_aliasing={{11}: (5, {})} | custom-call | flops 14495514624 | bytes 20971520 | tf_op jit(solution)/shard_map/block_forward_0_1/pallas_call | solution.py:282
  206.7 1.3 collective-permute-start
  209.0 1.3 block_forward_1_0.1
  210.3 9.3 %back_ffn_1_0.1 = (bf16[512,768]{1,0:T(8,128)(2,1)}, bf16[512,3072]{1,0:T(8,128)(2,1)}, bf16[512,768]{1,0:T(8,128)(2,1)}, f32[512,768]{1,0:T(8,128)}, f32[4,768]{1,0:T(4,128)}) custom-call(s32[1]{0:T(128)} %bitcast.refs_0_, f32[2]{0:T(128)} %refs_1_.7, f32[2,6,768]{2,1,0:T(8,128)} %reshape.156.refs_1_.refs_2_, bf16[1024,768]{1,0:T(8,128)(2,1)} %refs_3_.3, ...), custom_call_target="tpu_custom_call" | custom-call | flops 15000000512 | bytes 25165824 | tf_op jit(solution)/shard_map/back_ffn_1_0/pallas_call | solution.py:521
  220.5 1.3 collective-permute-start.3
  221.8 3.5 collective-permute-done.refs_2_
  227.4 6.1 %back_ffn_1_1.1 = (bf16[512,768]{1,0:T(8,128)(2,1)}, bf16[512,3072]{1,0:T(8,128)(2,1)}, bf16[512,768]{1,0:T(8,128)(2,1)}, f32[512,768]{1,0:T(8,128)}, f32[4,768]{1,0:T(4,128)}) custom-call(s32[1]{0:T(128)} %bitcast.refs_0_, f32[2]{0:T(128)} %refs_1_.7, f32[2,6,768]{2,1,0:T(8,128)} %reshape.156.refs_1_.refs_2_, bf16[1024,768]{1,0:T(8,128)(2,1)} %refs_3_.3, ...), custom_call_target="tpu_custom_call" | custom-call | flops 15000000512 | bytes 25165824 | tf_op jit(solution)/shard_map/back_ffn_1_1/pallas_call | solution.py:521
  233.5 4.4 back_att_1_1.1
  237.9 1.3 collective-permute-start.2
  239.2 45.0 %collective-permute-done.3.refs_3_ = bf16[512,768]{1,0:T(8,128)(2,1)S(1)} collective-permute-done((bf16[512,768]{1,0:T(8,128)(2,1)}, bf16[512,768]{1,0:T(8,128)(2,1)S(1)}, u32[]{:S(2)}, u32[]{:S(2)}) %collective-permute-start.3) | collective-permute-done | bytes 786464 | tf_op jit(solution)/shard_map/ppermute | solution.py:903
  285.1 17.5 %back_ffn_0_0.1 = (bf16[512,768]{1,0:T(8,128)(2,1)}, bf16[512,3072]{1,0:T(8,128)(2,1)}, bf16[512,768]{1,0:T(8,128)(2,1)}, f32[512,768]{1,0:T(8,128)}, f32[4,768]{1,0:T(4,128)}) custom-call(s32[1]{0:T(128)} %bitcast.refs_0_, f32[2]{0:T(128)} %refs_1_.7, ...), custom_call_target="tpu_custom_call", output_to_operand_aliasing={{0}: (9, {}), {1}: (10, {}), {2}: (11, {}), {3}: (12, {}), ... | custom-call | flops 15000000512 | bytes 25165824 | tf_op jit(solution)/shard_map/back_ffn_0_0/pallas_call | solution.py:521
  302.6 21.2 %back_att_0_0.1 = (bf16[512,2304]{1,0:T(8,128)(2,1)}, f32[2,768]{1,0:T(2,128)}, f32[1024,768]{1,0:T(8,128)}, bf16[512,768]{1,0:T(8,128)(2,1)}, f32[8,128]{1,0:T(8,128)}) custom-call(s32[1]{0:T(128)} %bitcast.refs_0_, f32[2,6,768]{2,1,0:T(8,128)} %reshape.156.refs_1_.refs_2_, ...), custom_call_target="tpu_custom_call", output_to_operand_aliasing={{0}: (8, {}), {1}: (9, {}), {2}: (10, {})} | custom-call | flops 20000000000 | bytes 16777216 | tf_op jit(solution)/shard_map/back_att_0_0/pallas_call | solution.py:570
  323.9 27.4 %collective-permute-done.2.refs_3_ = bf16[512,768]{1,0:T(8,128)(2,1)S(1)} collective-permute-done((bf16[512,768]{1,0:T(8,128)(2,1)}, bf16[512,768]{1,0:T(8,128)(2,1)S(1)}, u32[]{:S(2)}, u32[]{:S(2)}) %collective-permute-start.2) | collective-permute-done | bytes 786464 | tf_op jit(solution)/shard_map/ppermute | solution.py:903
  352.1 17.5 %back_ffn_0_1.1 = (bf16[512,768]{1,0:T(8,128)(2,1)}, bf16[512,3072]{1,0:T(8,128)(2,1)}, bf16[512,768]{1,0:T(8,128)(2,1)}, f32[512,768]{1,0:T(8,128)}, f32[4,768]{1,0:T(4,128)}) custom-call(s32[1]{0:T(128)} %bitcast.refs_0_, f32[2]{0:T(128)} %refs_1_.7, ...), custom_call_target="tpu_custom_call", output_to_operand_aliasing={{0}: (9, {}), {1}: (10, {}), {2}: (11, {}), {3}: (12, {}), ... | custom-call | flops 15000000512 | bytes 25165824 | tf_op jit(solution)/shard_map/back_ffn_0_1/pallas_call | solution.py:521
  369.6 21.5 %back_att_0_1.1 = (bf16[512,2304]{1,0:T(8,128)(2,1)}, f32[2,768]{1,0:T(2,128)}, f32[1024,768]{1,0:T(8,128)}, bf16[512,768]{1,0:T(8,128)(2,1)}, f32[8,128]{1,0:T(8,128)}) custom-call(s32[1]{0:T(128)} %bitcast.refs_0_, f32[2,6,768]{2,1,0:T(8,128)} %reshape.156.refs_1_.refs_2_, ...), custom_call_target="tpu_custom_call", output_to_operand_aliasing={{0}: (8, {}), {1}: (9, {}), {2}: (10, {})} | custom-call | flops 20000000000 | bytes 16777216 | tf_op jit(solution)/shard_map/back_att_0_1/pallas_call | solution.py:570
  391.1 13.3 %weight_grads_z.1 = (bf16[48,32,768]{2,1,0:T(8,128)(2,1)}, bf16[48,32,768]{2,1,0:T(8,128)(2,1)}, bf16[104,32,768]{2,1,0:T(8,128)(2,1)}, bf16[104,32,768]{2,1,0:T(8,128)(2,1)}, bf16[496,32,768]{2,1,0:T(8,128)(2,1)}) custom-call(s32[288]{0:T(512)} %get-tuple-element.230.code_ref, s32[288]{0:T(512)} %get-tuple-element.227.index_ref, ...), custom_call_target="tpu_custom_call" | custom-call | flops 9663676416 | bytes 12582912 | tf_op jit(solution)/shard_map/weight_grads_z/pallas_call | solution.py:661
  404.4 13.2 %weight_grads_du.1 = (bf16[48,32,768]{2,1,0:T(8,128)(2,1)}, bf16[48,32,768]{2,1,0:T(8,128)(2,1)}, bf16[104,32,768]{2,1,0:T(8,128)(2,1)}, bf16[104,32,768]{2,1,0:T(8,128)(2,1)}, bf16[496,32,768]{2,1,0:T(8,128)(2,1)}) custom-call(s32[288]{0:T(512)} %get-tuple-element.230.code_ref, ...), custom_call_target="tpu_custom_call", output_to_operand_aliasing={{2}: (6, {}), {3}: (7, {}), {4}: (8, {})} | custom-call | flops 9663676416 | bytes 12582912 | tf_op jit(solution)/shard_map/weight_grads_du/pallas_call | solution.py:661
  417.7 11.9 %weight_grads_da.1 = (bf16[104,32,768]{2,1,0:T(8,128)(2,1)}, bf16[104,32,768]{2,1,0:T(8,128)(2,1)}, bf16[496,32,768]{2,1,0:T(8,128)(2,1)}) custom-call(s32[288]{0:T(512)} %get-tuple-element.230.code_ref, s32[288]{0:T(512)} %get-tuple-element.227.index_ref, ...), custom_call_target="tpu_custom_call", output_to_operand_aliasing={{0}: (10, {}), {1}: (11, {}), {2}: (12, {})} | custom-call | flops 9663676416 | bytes 12582912 | tf_op jit(solution)/shard_map/weight_grads_da/pallas_call | solution.py:661
  429.6 1.3 collective-permute-start.24
  433.2 9.6 %collective-permute-done.4 = bf16[48,32,768]{2,1,0:T(8,128)(2,1)} collective-permute-done((bf16[48,32,768]{2,1,0:T(8,128)(2,1)}, bf16[48,32,768]{2,1,0:T(8,128)(2,1)}, u32[]{:S(2)}, u32[]{:S(2)}) %collective-permute-start.4) | collective-permute-done | bytes 2359328 | tf_op jit(solution)/shard_map/ppermute | solution.py:789
  443.8 2.0 collective-permute-start.5
  449.1 1.6 add_convert_fusion.31
  450.8 1.8 collective-permute-start.6
  453.7 1.5 collective-permute-start.25
  455.2 1.3 add_convert_fusion.25
  459.4 6.4 %collective-permute-done.25 = bf16[6,32,768]{2,1,0:T(8,128)(2,1)S(1)} collective-permute-done((bf16[6,32,768]{2,1,0:T(8,128)(2,1)S(1)}, bf16[6,32,768]{2,1,0:T(8,128)(2,1)S(1)}, u32[]{:S(2)}, u32[]{:S(2)}) %collective-permute-start.25) | collective-permute-done | bytes 294944 | tf_op jit(solution)/shard_map/ppermute | solution.py:796
  469.6 3.2 collective-permute-done.29
  474.0 11.4 %collective-permute-done.26 = bf16[13,32,768]{2,1,0:T(8,128)(2,1)S(1)} collective-permute-done((bf16[13,32,768]{2,1,0:T(8,128)(2,1)S(1)}, bf16[13,32,768]{2,1,0:T(8,128)(2,1)S(1)}, u32[]{:S(2)}, u32[]{:S(2)}) %collective-permute-start.26) | collective-permute-done | bytes 639008 | tf_op jit(solution)/shard_map/ppermute | solution.py:796
  485.9 1.4 add_convert_fusion.4
  493.0 6.5 %collective-permute-done.30 = bf16[13,32,768]{2,1,0:T(8,128)(2,1)S(1)} collective-permute-done((bf16[13,32,768]{2,1,0:T(8,128)(2,1)S(1)}, bf16[13,32,768]{2,1,0:T(8,128)(2,1)S(1)}, u32[]{:S(2)}, u32[]{:S(2)}) %collective-permute-start.30) | collective-permute-done | bytes 639008 | tf_op jit(solution)/shard_map/ppermute | solution.py:796
  500.7 1.9 add_convert_fusion.3
  502.7 1.4 collective-permute-start.31
  504.1 3.0 collective-permute-done.7
  507.1 1.3 add_convert_fusion.19
  508.3 1.4 collective-permute-start.11
  510.0 3.4 collective-permute-done.17
  513.4 1.3 add_convert_fusion.14
  514.7 1.4 collective-permute-start.21
  516.2 7.6 %collective-permute-done.11 = bf16[6,32,768]{2,1,0:T(8,128)(2,1)S(1)} collective-permute-done((bf16[6,32,768]{2,1,0:T(8,128)(2,1)S(1)}, bf16[6,32,768]{2,1,0:T(8,128)(2,1)S(1)}, u32[]{:S(2)}, u32[]{:S(2)}) %collective-permute-start.11) | collective-permute-done | bytes 294944 | tf_op jit(solution)/shard_map/ppermute | solution.py:796
  524.9 1.4 collective-permute-start.28
  526.4 1.4 add_convert_fusion.1
  527.7 2.4 collective-permute-done.21
  531.2 2.1 collective-permute-start.22
  533.3 3.1 collective-permute-done.12
  537.5 9.1 %collective-permute-start.13 = (bf16[6,32,768]{2,1,0:T(8,128)(2,1)S(1)}, bf16[6,32,768]{2,1,0:T(8,128)(2,1)S(1)}, u32[]{:S(2)}, u32[]{:S(2)}) collective-permute-start(bf16[6,32,768]{2,1,0:T(8,128)(2,1)S(1)} %add_convert_fusion.16.refs_0_), channel_id=1, source_target_pairs={{0,1},{1,0},{2,3},{3,2},{4,5},{5,4},{6,7},{7,6},{8,9},{9,8},{10,11... | collective-permute-start | bytes 884744 | tf_op jit(solution)/shard_map/ppermute | solution.py:789
  546.7 9.7 %collective-permute-done.22 = bf16[6,32,768]{2,1,0:T(8,128)(2,1)S(1)} collective-permute-done((bf16[6,32,768]{2,1,0:T(8,128)(2,1)S(1)}, bf16[6,32,768]{2,1,0:T(8,128)(2,1)S(1)}, u32[]{:S(2)}, u32[]{:S(2)}) %collective-permute-start.22) | collective-permute-done | bytes 294944 | tf_op jit(solution)/shard_map/ppermute | solution.py:796
  557.5 4.8 collective-permute-start.23
  562.3 1.5 add_convert_fusion.refs_4_
  564.0 20.4 %all-gather = bf16[16,2,4608]{2,1,0:T(2,128)(2,1)S(1)} all-gather(bf16[1,2,4608]{2,1,0:T(2,128)(2,1)S(1)} %maximum_bitcast_fusion), channel_id=1, replica_groups=mesh['section'=2,'batch'=16] {'batch'}, dimensions={0}, use_global_device_ids=true | all-gather | bytes 313344 | tf_op jit(solution)/shard_map/all_gather | solution.py:950
  584.5 1.4 copy.82
  585.9 1.4 conditional.3
  585.9 1.4 broadcast.248
  588.3 10.8 %adam.1 = (f32[31,32,768]{2,1,0:T(8,128)}, f32[31,32,768]{2,1,0:T(8,128)}, f32[31,32,768]{2,1,0:T(8,128)}, bf16[31,32,768]{2,1,0:T(8,128)(2,1)}) custom-call(s32[31]{0:T(128)} %get-tuple-element.261.code_ref, s32[31]{0:T(128)} %get-tuple-element.219.index_ref, s32[31]{0:T(128)} %get-tuple-element.260.row_ref, f32[31,32,768]{2,1,0:T(8,128)} %bitcast.52, ...), custom_call_target="tpu_custom_call" | custom-call | bytes 22855680 | tf_op jit(solution)/shard_map/adam/pallas_call | solution.py:765
  (178 shorter events, 45.4 us)
Async XLA Ops:
  8.0 3.2 copy-start.11
  11.5 35.6 %copy-start.9 = (s32[432]{0:T(512)}, s32[432]{0:T(512)S(1)}, u32[]{:S(2)}) copy-start(s32[432]{0:T(512)S(1)} %convert_reduce_fusion) | copy-start | bytes 5188
  13.7 33.4 %copy-start.15 = (pred[288]{0:T(512)(128)(4,1)}, pred[288]{0:T(512)(128)(4,1)S(1)}, u32[]{:S(2)}) copy-start(pred[288]{0:T(512)(128)(4,1)S(1)} %select_compare_fusion) | copy-start | bytes 868
  14.6 32.6 %copy-start.22 = (pred[288]{0:T(512)(128)(4,1)}, pred[288]{0:T(512)(128)(4,1)S(1)}, u32[]{:S(2)}) copy-start(pred[288]{0:T(512)(128)(4,1)S(1)} %get-tuple-element.228) | copy-start | bytes 868
  22.5 2.6 copy-start.32
  22.5 3.9 copy-start.31
  24.6 118.0 %all-gather.6.cloned.1.call-start = ((), (), s32[]{:S(2)}) async-start(), calls=%async_computation.4 | async-start | bytes 22560768 | tf_op jit(solution)/shard_map/all_gather | solution.py:857
  40.5 15.9 %all-to-all-start = ((f32[16,2,992]{2,1,0:T(2,128)}), f32[16,2,992]{2,1,0:T(2,128)S(1)}, u32[]{:S(2)}, u32[]{:S(2)}) async-start(f32[16,2,992]{2,1,0:T(2,128)} %copy.78), calls=%async_computation.1 | async-start | bytes 262144 | tf_op jit(solution)/shard_map/all_to_all | solution.py:878
  179.4 28.7 %collective-permute-start.1 = (bf16[512,768]{1,0:T(8,128)(2,1)}, bf16[512,768]{1,0:T(8,128)(2,1)S(1)}, u32[]{:S(2)}, u32[]{:S(2)}) collective-permute-start(bf16[512,768]{1,0:T(8,128)(2,1)} %get-tuple-element.119), channel_id=1, source_target_pairs={{0,16},{1,17},{2,18},{3,19},{4,20},{5,21},{6,22},{7,23},{8,24},{9,... | collective-permute-start | bytes 2359304 | tf_op jit(solution)/shard_map/ppermute | solution.py:897
  206.7 18.6 %collective-permute-start = (bf16[512,768]{1,0:T(8,128)(2,1)}, bf16[512,768]{1,0:T(8,128)(2,1)S(1)}, u32[]{:S(2)}, u32[]{:S(2)}) collective-permute-start(bf16[512,768]{1,0:T(8,128)(2,1)} %get-tuple-element.118), channel_id=1, source_target_pairs={{0,16},{1,17},{2,18},{3,19},{4,20},{5,21},{6,22},{7,23},{8,24},{9,... | collective-permute-start | bytes 2359304 | tf_op jit(solution)/shard_map/ppermute | solution.py:897
  208.1 0.9 copy-start.30
  220.5 63.7 %collective-permute-start.3 = (bf16[512,768]{1,0:T(8,128)(2,1)}, bf16[512,768]{1,0:T(8,128)(2,1)S(1)}, u32[]{:S(2)}, u32[]{:S(2)}) collective-permute-start(bf16[512,768]{1,0:T(8,128)(2,1)} %get-tuple-element.173), channel_id=1, source_target_pairs={{16,0},{17,1},{18,2},{19,3},{20,4},{21,5},{22,6},{23,7},{24,8},{25... | collective-permute-start | bytes 2359304 | tf_op jit(solution)/shard_map/ppermute | solution.py:903
  225.3 0.9 copy-start.27
  237.9 113.3 %collective-permute-start.2 = (bf16[512,768]{1,0:T(8,128)(2,1)}, bf16[512,768]{1,0:T(8,128)(2,1)S(1)}, u32[]{:S(2)}, u32[]{:S(2)}) collective-permute-start(bf16[512,768]{1,0:T(8,128)(2,1)} %get-tuple-element.165), channel_id=1, source_target_pairs={{16,0},{17,1},{18,2},{19,3},{20,4},{21,5},{22,6},{23,7},{24,8},{25... | collective-permute-start | bytes 2359304 | tf_op jit(solution)/shard_map/ppermute | solution.py:903
  351.2 0.9 copy-start.29
  417.6 13.8 %copy-start.12 = (s32[1,432]{1,0:T(1,128)S(1)}, s32[1,432]{1,0:T(1,128)}, u32[]{:S(2)}) copy-start(s32[1,432]{1,0:T(1,128)} %param.16) | copy-start | bytes 5188
  417.6 13.9 %copy-start.10 = (s32[432]{0:T(512)S(1)}, s32[432]{0:T(512)}, u32[]{:S(2)}) copy-start(s32[432]{0:T(512)} %copy-done.9) | copy-start | bytes 5188
  417.6 14.0 %copy-start.16 = (pred[288]{0:T(512)(128)(4,1)S(1)}, pred[288]{0:T(512)(128)(4,1)}, u32[]{:S(2)}) copy-start(pred[288]{0:T(512)(128)(4,1)} %copy-done.15) | copy-start | bytes 868
  417.6 14.0 %copy-start.23 = (pred[288]{0:T(512)(128)(4,1)S(1)}, pred[288]{0:T(512)(128)(4,1)}, u32[]{:S(2)}) copy-start(pred[288]{0:T(512)(128)(4,1)} %copy-done.22) | copy-start | bytes 868
  417.7 14.0 %copy-start.26 = (pred[288]{0:T(512)(128)(4,1)S(1)}, pred[288]{0:T(512)(128)(4,1)}, u32[]{:S(2)}) copy-start(pred[288]{0:T(512)(128)(4,1)} %get-tuple-element.231) | copy-start | bytes 868
  417.7 14.0 %copy-start.19 = (s32[288]{0:T(512)S(1)}, s32[288]{0:T(512)}, u32[]{:S(2)}) copy-start(s32[288]{0:T(512)} %get-tuple-element.258) | copy-start | bytes 3460
  417.7 15.3 %copy-start.14 = (f32[384]{0:T(512)S(1)}, f32[384]{0:T(512)}, u32[]{:S(2)}) copy-start(f32[384]{0:T(512)} %copy-done.13) | copy-start | bytes 4612
  417.7 15.2 %copy-start.25 = (f32[32]{0:T(128)S(1)}, f32[32]{0:T(128)}, u32[]{:S(2)}) copy-start(f32[32]{0:T(128)} %copy-done.24) | copy-start | bytes 388
  417.7 29.4 %copy-start.18 = (f32[4,768]{1,0:T(4,128)S(1)}, f32[4,768]{1,0:T(4,128)}, u32[]{:S(2)}) copy-start(f32[4,768]{1,0:T(4,128)} %get-tuple-element.187) | copy-start | bytes 36868
  417.7 29.5 %copy-start.21 = (f32[2,768]{1,0:T(2,128)S(1)}, f32[2,768]{1,0:T(2,128)}, u32[]{:S(2)}) copy-start(f32[2,768]{1,0:T(2,128)} %get-tuple-element.186) | copy-start | bytes 18436
  417.7 29.5 %copy-start.2 = (bf16[48,32,768]{2,1,0:T(8,128)(2,1)S(1)}, bf16[48,32,768]{2,1,0:T(8,128)(2,1)}, u32[]{:S(2)}) copy-start(bf16[48,32,768]{2,1,0:T(8,128)(2,1)} %get-tuple-element.201) | copy-start | bytes 7077892
  429.6 23.0 %collective-permute-start.24 = (bf16[104,32,768]{2,1,0:T(8,128)(2,1)}, bf16[104,32,768]{2,1,0:T(8,128)(2,1)}, u32[]{:S(2)}, u32[]{:S(2)}) collective-permute-start(bf16[104,32,768]{2,1,0:T(8,128)(2,1)} %get-tuple-element.213), channel_id=1, source_target_pairs={{0,1},{1,0},{2,3},{3,2},{4,5},{5,4},{6,7},{7,6},{8,9},{9,8},{10,11... | collective-permute-start | bytes 15335432 | tf_op jit(solution)/shard_map/ppermute | solution.py:789
  430.9 11.8 %collective-permute-start.4 = (bf16[48,32,768]{2,1,0:T(8,128)(2,1)}, bf16[48,32,768]{2,1,0:T(8,128)(2,1)}, u32[]{:S(2)}, u32[]{:S(2)}) collective-permute-start(bf16[48,32,768]{2,1,0:T(8,128)(2,1)} %get-tuple-element.193), channel_id=1, source_target_pairs={{0,1},{1,0},{2,3},{3,2},{4,5},{5,4},{6,7},{7,6},{8,9},{9,8},{10,11... | collective-permute-start | bytes 7077896 | tf_op jit(solution)/shard_map/ppermute | solution.py:789
  431.0 16.2 %collective-permute-start.14 = (bf16[48,32,768]{2,1,0:T(8,128)(2,1)}, bf16[48,32,768]{2,1,0:T(8,128)(2,1)}, u32[]{:S(2)}, u32[]{:S(2)}) collective-permute-start(bf16[48,32,768]{2,1,0:T(8,128)(2,1)} %get-tuple-element.202), channel_id=1, source_target_pairs={{0,1},{1,0},{2,3},{3,2},{4,5},{5,4},{6,7},{7,6},{8,9},{9,8},{10,11... | collective-permute-start | bytes 7077896 | tf_op jit(solution)/shard_map/ppermute | solution.py:789
  443.8 5.3 collective-permute-start.5
  448.2 7.1 %collective-permute-start.15 = (bf16[3,32,768]{2,1,0:T(8,128)(2,1)S(1)}, bf16[3,32,768]{2,1,0:T(8,128)(2,1)S(1)}, u32[]{:S(2)}, u32[]{:S(2)}) collective-permute-start(bf16[3,32,768]{2,1,0:T(8,128)(2,1)S(1)} %add_convert_fusion.26), channel_id=1, source_target_pairs={{0,4},{1,5},{4,8},{5,9},{8,12},{9,13},{12,14},{13,15},{14,10},{15,... | collective-permute-start | bytes 442376 | tf_op jit(solution)/shard_map/ppermute | solution.py:796
  449.1 9.0 %copy-start = (bf16[104,32,768]{2,1,0:T(8,128)(2,1)S(1)}, bf16[104,32,768]{2,1,0:T(8,128)(2,1)}, u32[]{:S(2)}) copy-start(bf16[104,32,768]{2,1,0:T(8,128)(2,1)} %get-tuple-element.212) | copy-start | bytes 15335428
  450.8 38.5 %collective-permute-start.6 = (bf16[6,32,768]{2,1,0:T(8,128)(2,1)S(1)}, bf16[6,32,768]{2,1,0:T(8,128)(2,1)S(1)}, u32[]{:S(2)}, u32[]{:S(2)}) collective-permute-start(bf16[6,32,768]{2,1,0:T(8,128)(2,1)S(1)} %pad_maximum_fusion.2), channel_id=1, source_target_pairs={{0,4},{1,5},{4,8},{5,9},{8,12},{9,13},{12,14},{13,15},{14,10},{15,... | collective-permute-start | bytes 884744 | tf_op jit(solution)/shard_map/ppermute | solution.py:796
  452.6 15.1 %collective-permute-start.9 = (bf16[3,32,768]{2,1,0:T(8,128)(2,1)S(1)}, bf16[3,32,768]{2,1,0:T(8,128)(2,1)S(1)}, u32[]{:S(2)}, u32[]{:S(2)}) collective-permute-start(bf16[3,32,768]{2,1,0:T(8,128)(2,1)S(1)} %get-tuple-element.247), channel_id=1, source_target_pairs={{0,2},{1,3},{4,0},{5,1},{8,4},{9,5},{12,8},{13,9},{14,12},{15,13},... | collective-permute-start | bytes 442376 | tf_op jit(solution)/shard_map/ppermute | solution.py:796
  453.7 12.1 %collective-permute-start.25 = (bf16[6,32,768]{2,1,0:T(8,128)(2,1)S(1)}, bf16[6,32,768]{2,1,0:T(8,128)(2,1)S(1)}, u32[]{:S(2)}, u32[]{:S(2)}) collective-permute-start(bf16[6,32,768]{2,1,0:T(8,128)(2,1)S(1)} %add_convert_fusion.10), channel_id=1, source_target_pairs={{0,4},{1,5},{4,8},{5,9},{8,12},{9,13},{12,14},{13,15},{14,10},{15,... | collective-permute-start | bytes 884744 | tf_op jit(solution)/shard_map/ppermute | solution.py:796
  456.6 34.4 %collective-permute-start.16 = (bf16[6,32,768]{2,1,0:T(8,128)(2,1)S(1)}, bf16[6,32,768]{2,1,0:T(8,128)(2,1)S(1)}, u32[]{:S(2)}, u32[]{:S(2)}) collective-permute-start(bf16[6,32,768]{2,1,0:T(8,128)(2,1)S(1)} %pad_maximum_fusion.4), channel_id=1, source_target_pairs={{0,4},{1,5},{4,8},{5,9},{8,12},{9,13},{12,14},{13,15},{14,10},{15,... | collective-permute-start | bytes 884744 | tf_op jit(solution)/shard_map/ppermute | solution.py:796
  457.0 11.6 %copy-start.3 = (bf16[48,32,768]{2,1,0:T(8,128)(2,1)S(1)}, bf16[48,32,768]{2,1,0:T(8,128)(2,1)}, u32[]{:S(2)}) copy-start(bf16[48,32,768]{2,1,0:T(8,128)(2,1)} %get-tuple-element.192) | copy-start | bytes 7077892
  457.0 30.3 %collective-permute-start.19 = (bf16[3,32,768]{2,1,0:T(8,128)(2,1)S(1)}, bf16[3,32,768]{2,1,0:T(8,128)(2,1)S(1)}, u32[]{:S(2)}, u32[]{:S(2)}) collective-permute-start(bf16[3,32,768]{2,1,0:T(8,128)(2,1)S(1)} %get-tuple-element.241), channel_id=1, source_target_pairs={{0,2},{1,3},{4,0},{5,1},{8,4},{9,5},{12,8},{13,9},{14,12},{15,13},... | collective-permute-start | bytes 442376 | tf_op jit(solution)/shard_map/ppermute | solution.py:796
  465.8 7.0 %collective-permute-start.29 = (bf16[7,32,768]{2,1,0:T(8,128)(2,1)S(1)}, bf16[7,32,768]{2,1,0:T(8,128)(2,1)S(1)}, u32[]{:S(2)}, u32[]{:S(2)}) collective-permute-start(bf16[7,32,768]{2,1,0:T(8,128)(2,1)S(1)} %get-tuple-element.237), channel_id=1, source_target_pairs={{0,2},{1,3},{4,0},{5,1},{8,4},{9,5},{12,8},{13,9},{14,12},{15,13},... | collective-permute-start | bytes 1032200 | tf_op jit(solution)/shard_map/ppermute | solution.py:796
  467.7 17.7 %collective-permute-start.26 = (bf16[13,32,768]{2,1,0:T(8,128)(2,1)S(1)}, bf16[13,32,768]{2,1,0:T(8,128)(2,1)S(1)}, u32[]{:S(2)}, u32[]{:S(2)}) collective-permute-start(bf16[13,32,768]{2,1,0:T(8,128)(2,1)S(1)} %pad_maximum_fusion), channel_id=1, source_target_pairs={{0,4},{1,5},{4,8},{5,9},{8,12},{9,13},{12,14},{13,15},{14,10},{15,... | collective-permute-start | bytes 1916936 | tf_op jit(solution)/shard_map/ppermute | solution.py:796
  472.8 31.3 %collective-permute-start.10 = (bf16[6,32,768]{2,1,0:T(8,128)(2,1)S(1)}, bf16[6,32,768]{2,1,0:T(8,128)(2,1)S(1)}, u32[]{:S(2)}, u32[]{:S(2)}) collective-permute-start(bf16[6,32,768]{2,1,0:T(8,128)(2,1)S(1)} %pad_maximum_fusion.3), channel_id=1, source_target_pairs={{0,2},{1,3},{4,0},{5,1},{8,4},{9,5},{12,8},{13,9},{14,12},{15,13},... | collective-permute-start | bytes 884744 | tf_op jit(solution)/shard_map/ppermute | solution.py:796
  485.4 14.1 %collective-permute-start.30 = (bf16[13,32,768]{2,1,0:T(8,128)(2,1)S(1)}, bf16[13,32,768]{2,1,0:T(8,128)(2,1)S(1)}, u32[]{:S(2)}, u32[]{:S(2)}) collective-permute-start(bf16[13,32,768]{2,1,0:T(8,128)(2,1)S(1)} %pad_maximum_fusion.1), channel_id=1, source_target_pairs={{0,2},{1,3},{4,0},{5,1},{8,4},{9,5},{12,8},{13,9},{14,12},{15,13},... | collective-permute-start | bytes 1916936 | tf_op jit(solution)/shard_map/ppermute | solution.py:796
  487.3 13.4 %collective-permute-start.27 = (bf16[13,32,768]{2,1,0:T(8,128)(2,1)S(1)}, bf16[13,32,768]{2,1,0:T(8,128)(2,1)S(1)}, u32[]{:S(2)}, u32[]{:S(2)}) collective-permute-start(bf16[13,32,768]{2,1,0:T(8,128)(2,1)S(1)} %add_convert_fusion.4), channel_id=1, source_target_pairs={{0,4},{1,5},{4,8},{5,9},{8,12},{9,13},{12,14},{13,15},{14,10},{15,... | collective-permute-start | bytes 1916936 | tf_op jit(solution)/shard_map/ppermute | solution.py:796
  489.3 20.7 %collective-permute-start.20 = (bf16[6,32,768]{2,1,0:T(8,128)(2,1)S(1)}, bf16[6,32,768]{2,1,0:T(8,128)(2,1)S(1)}, u32[]{:S(2)}, u32[]{:S(2)}) collective-permute-start(bf16[6,32,768]{2,1,0:T(8,128)(2,1)S(1)} %pad_maximum_fusion.5), channel_id=1, source_target_pairs={{0,2},{1,3},{4,0},{5,1},{8,4},{9,5},{12,8},{13,9},{14,12},{15,13},... | collective-permute-start | bytes 884744 | tf_op jit(solution)/shard_map/ppermute | solution.py:796
  491.0 16.1 %collective-permute-start.7 = (bf16[6,32,768]{2,1,0:T(8,128)(2,1)S(1)}, bf16[6,32,768]{2,1,0:T(8,128)(2,1)S(1)}, u32[]{:S(2)}, u32[]{:S(2)}) collective-permute-start(bf16[6,32,768]{2,1,0:T(8,128)(2,1)S(1)} %add_convert_fusion.20), channel_id=1, source_target_pairs={{0,4},{1,5},{4,8},{5,9},{8,12},{9,13},{12,14},{13,15},{14,10},{15,... | collective-permute-start | bytes 884744 | tf_op jit(solution)/shard_map/ppermute | solution.py:796
  499.5 13.9 %collective-permute-start.17 = (bf16[6,32,768]{2,1,0:T(8,128)(2,1)S(1)}, bf16[6,32,768]{2,1,0:T(8,128)(2,1)S(1)}, u32[]{:S(2)}, u32[]{:S(2)}) collective-permute-start(bf16[6,32,768]{2,1,0:T(8,128)(2,1)S(1)} %add_convert_fusion.15), channel_id=1, source_target_pairs={{0,4},{1,5},{4,8},{5,9},{8,12},{9,13},{12,14},{13,15},{14,10},{15,... | collective-permute-start | bytes 884744 | tf_op jit(solution)/shard_map/ppermute | solution.py:796
  502.7 7.1 %copy-start.17 = (f32[4,768]{1,0:T(4,128)S(1)}, f32[4,768]{1,0:T(4,128)}, u32[]{:S(2)}) copy-start(f32[4,768]{1,0:T(4,128)} %get-tuple-element.185) | copy-start | bytes 36868
  502.7 7.1 %copy-start.20 = (f32[2,768]{1,0:T(2,128)S(1)}, f32[2,768]{1,0:T(2,128)}, u32[]{:S(2)}) copy-start(f32[2,768]{1,0:T(2,128)} %get-tuple-element.184) | copy-start | bytes 18436
  502.7 22.2 %collective-permute-start.31 = (bf16[13,32,768]{2,1,0:T(8,128)(2,1)S(1)}, bf16[13,32,768]{2,1,0:T(8,128)(2,1)S(1)}, u32[]{:S(2)}, u32[]{:S(2)}) collective-permute-start(bf16[13,32,768]{2,1,0:T(8,128)(2,1)S(1)} %get-tuple-element.233), channel_id=1, source_target_pairs={{0,2},{1,3},{4,0},{5,1},{8,4},{9,5},{12,8},{13,9},{14,12},{15,13},... | collective-permute-start | bytes 1916936 | tf_op jit(solution)/shard_map/ppermute | solution.py:796
  508.3 15.4 %collective-permute-start.11 = (bf16[6,32,768]{2,1,0:T(8,128)(2,1)S(1)}, bf16[6,32,768]{2,1,0:T(8,128)(2,1)S(1)}, u32[]{:S(2)}, u32[]{:S(2)}) collective-permute-start(bf16[6,32,768]{2,1,0:T(8,128)(2,1)S(1)} %get-tuple-element.245), channel_id=1, source_target_pairs={{0,2},{1,3},{4,0},{5,1},{8,4},{9,5},{12,8},{13,9},{14,12},{15,13},... | collective-permute-start | bytes 884744 | tf_op jit(solution)/shard_map/ppermute | solution.py:796
  509.8 21.4 %collective-permute-start.8 = (bf16[6,32,768]{2,1,0:T(8,128)(2,1)S(1)}, bf16[6,32,768]{2,1,0:T(8,128)(2,1)S(1)}, u32[]{:S(2)}, u32[]{:S(2)}) collective-permute-start(bf16[6,32,768]{2,1,0:T(8,128)(2,1)S(1)} %get-tuple-element.244), channel_id=1, source_target_pairs={{0,4},{1,5},{4,8},{5,9},{8,12},{9,13},{12,14},{13,15},{14,10},{15,... | collective-permute-start | bytes 884744 | tf_op jit(solution)/shard_map/ppermute | solution.py:796
  514.7 15.4 %collective-permute-start.21 = (bf16[6,32,768]{2,1,0:T(8,128)(2,1)S(1)}, bf16[6,32,768]{2,1,0:T(8,128)(2,1)S(1)}, u32[]{:S(2)}, u32[]{:S(2)}) collective-permute-start(bf16[6,32,768]{2,1,0:T(8,128)(2,1)S(1)} %get-tuple-element.239), channel_id=1, source_target_pairs={{0,2},{1,3},{4,0},{5,1},{8,4},{9,5},{12,8},{13,9},{14,12},{15,13},... | collective-permute-start | bytes 884744 | tf_op jit(solution)/shard_map/ppermute | solution.py:796
  516.1 30.6 %collective-permute-start.18 = (bf16[6,32,768]{2,1,0:T(8,128)(2,1)S(1)}, bf16[6,32,768]{2,1,0:T(8,128)(2,1)S(1)}, u32[]{:S(2)}, u32[]{:S(2)}) collective-permute-start(bf16[6,32,768]{2,1,0:T(8,128)(2,1)S(1)} %get-tuple-element.238), channel_id=1, source_target_pairs={{0,4},{1,5},{4,8},{5,9},{8,12},{9,13},{12,14},{13,15},{14,10},{15,... | collective-permute-start | bytes 884744 | tf_op jit(solution)/shard_map/ppermute | solution.py:796
  524.8 11.6 %collective-permute-start.12 = (bf16[6,32,768]{2,1,0:T(8,128)(2,1)S(1)}, bf16[6,32,768]{2,1,0:T(8,128)(2,1)S(1)}, u32[]{:S(2)}, u32[]{:S(2)}) collective-permute-start(bf16[6,32,768]{2,1,0:T(8,128)(2,1)S(1)} %add_convert_fusion.17), channel_id=1, source_target_pairs={{0,2},{1,3},{4,0},{5,1},{8,4},{9,5},{12,8},{13,9},{14,12},{15,13},... | collective-permute-start | bytes 884744 | tf_op jit(solution)/shard_map/ppermute | solution.py:796
  524.9 37.4 %collective-permute-start.28 = (bf16[13,32,768]{2,1,0:T(8,128)(2,1)S(1)}, bf16[13,32,768]{2,1,0:T(8,128)(2,1)S(1)}, u32[]{:S(2)}, u32[]{:S(2)}) collective-permute-start(bf16[13,32,768]{2,1,0:T(8,128)(2,1)S(1)} %get-tuple-element.232), channel_id=1, source_target_pairs={{0,4},{1,5},{4,8},{5,9},{8,12},{9,13},{12,14},{13,15},{14,10},{15,... | collective-permute-start | bytes 1916936 | tf_op jit(solution)/shard_map/ppermute | solution.py:796
  530.1 32.3 %collective-permute-start.32 = (bf16[13,32,768]{2,1,0:T(8,128)(2,1)S(1)}, bf16[13,32,768]{2,1,0:T(8,128)(2,1)S(1)}, u32[]{:S(2)}, u32[]{:S(2)}) collective-permute-start(bf16[13,32,768]{2,1,0:T(8,128)(2,1)S(1)} %add_convert_fusion.1), channel_id=1, source_target_pairs={{0,2},{1,3},{4,0},{5,1},{8,4},{9,5},{12,8},{13,9},{14,12},{15,13},... | collective-permute-start | bytes 1916936 | tf_op jit(solution)/shard_map/ppermute | solution.py:796
  531.2 25.2 %collective-permute-start.22 = (bf16[6,32,768]{2,1,0:T(8,128)(2,1)S(1)}, bf16[6,32,768]{2,1,0:T(8,128)(2,1)S(1)}, u32[]{:S(2)}, u32[]{:S(2)}) collective-permute-start(bf16[6,32,768]{2,1,0:T(8,128)(2,1)S(1)} %add_convert_fusion.12), channel_id=1, source_target_pairs={{0,2},{1,3},{4,0},{5,1},{8,4},{9,5},{12,8},{13,9},{14,12},{15,13},... | collective-permute-start | bytes 884744 | tf_op jit(solution)/shard_map/ppermute | solution.py:796
  537.5 26.5 %copy-start.4 = (bf16[6,32,768]{2,1,0:T(8,128)(2,1)}, bf16[6,32,768]{2,1,0:T(8,128)(2,1)S(1)}, u32[]{:S(2)}) copy-start(bf16[6,32,768]{2,1,0:T(8,128)(2,1)S(1)} %add_convert_fusion.16.refs_0_) | copy-start | bytes 884740
  537.5 49.7 %collective-permute-start.13 = (bf16[6,32,768]{2,1,0:T(8,128)(2,1)S(1)}, bf16[6,32,768]{2,1,0:T(8,128)(2,1)S(1)}, u32[]{:S(2)}, u32[]{:S(2)}) collective-permute-start(bf16[6,32,768]{2,1,0:T(8,128)(2,1)S(1)} %add_convert_fusion.16.refs_0_), channel_id=1, source_target_pairs={{0,1},{1,0},{2,3},{3,2},{4,5},{5,4},{6,7},{7,6},{8,9},{9,8},{10,11... | collective-permute-start | bytes 884744 | tf_op jit(solution)/shard_map/ppermute | solution.py:789
  557.5 28.3 %copy-start.5 = (bf16[6,32,768]{2,1,0:T(8,128)(2,1)}, bf16[6,32,768]{2,1,0:T(8,128)(2,1)S(1)}, u32[]{:S(2)}) copy-start(bf16[6,32,768]{2,1,0:T(8,128)(2,1)S(1)} %add_convert_fusion.11.refs_2_) | copy-start | bytes 884740
  557.5 29.7 %collective-permute-start.23 = (bf16[6,32,768]{2,1,0:T(8,128)(2,1)S(1)}, bf16[6,32,768]{2,1,0:T(8,128)(2,1)S(1)}, u32[]{:S(2)}, u32[]{:S(2)}) collective-permute-start(bf16[6,32,768]{2,1,0:T(8,128)(2,1)S(1)} %add_convert_fusion.11.refs_2_), channel_id=1, source_target_pairs={{0,1},{1,0},{2,3},{3,2},{4,5},{5,4},{6,7},{7,6},{8,9},{9,8},{10,11... | collective-permute-start | bytes 884744 | tf_op jit(solution)/shard_map/ppermute | solution.py:789
  563.8 22.0 %copy-start.1 = (bf16[13,32,768]{2,1,0:T(8,128)(2,1)}, bf16[13,32,768]{2,1,0:T(8,128)(2,1)S(1)}, u32[]{:S(2)}) copy-start(bf16[13,32,768]{2,1,0:T(8,128)(2,1)S(1)} %add_convert_fusion.refs_4_) | copy-start | bytes 1916932
  563.8 23.4 %collective-permute-start.33 = (bf16[13,32,768]{2,1,0:T(8,128)(2,1)S(1)}, bf16[13,32,768]{2,1,0:T(8,128)(2,1)S(1)}, u32[]{:S(2)}, u32[]{:S(2)}) collective-permute-start(bf16[13,32,768]{2,1,0:T(8,128)(2,1)S(1)} %add_convert_fusion.refs_4_), channel_id=1, source_target_pairs={{0,1},{1,0},{2,3},{3,2},{4,5},{5,4},{6,7},{7,6},{8,9},{9,8},{10,11... | collective-permute-start | bytes 1916936 | tf_op jit(solution)/shard_map/ppermute | solution.py:789
  587.3 1.0 copy-start.6
  (5 other events, 3.5 us)
Sparse Core Ops, SparseCore 1:
  27.3 115.2 all-gather.5

commit v3 on v0

v3 whole, which is shorter than its diff:
```python
import functools
import math

import jax
import jax.numpy as jnp
from jax import lax
from jax.experimental import pallas as pl
from jax.experimental.pallas import tpu as pltpu
from jax.sharding import PartitionSpec as P

D = 768
HEADS = 12
HEAD_DIM = 64
FF = 3072
STEP = 10
QKV_END = 3 * D
PROJ_END = 4 * D
UP_END = 4 * D + FF
DOWN_END = 4 * D + 2 * FF

norm_eps = 1e-06
adam_eps = 1e-08
learn_rate = 0.03
decay_rate = 0.1
beta_one = 0.5
beta_two = 0.5

bf16 = jnp.bfloat16
f32 = jnp.float32
SECTION, BATCH = "section", "batch"
VMEM_LIMIT = 46 * 1024 * 1024
VMEM_ALL = 58 * 1024 * 1024
ROWS = 128
GELU_C = math.sqrt(2.0 / math.pi)


def dot_nn(a, b):
    return lax.dot_general(a, b, (((1,), (0,)), ((), ())), preferred_element_type=f32)


def dot_nt(a, b):
    return lax.dot_general(a, b, (((1,), (1,)), ((), ())), preferred_element_type=f32)


def dot_tn(a, b):
    return lax.dot_general(a, b, (((0,), (0,)), ((), ())), preferred_element_type=f32)


def in_hbm(arrays):
    return [pltpu.with_memory_space_constraint(a, pltpu.HBM) for a in arrays]


def start(src, dst, sem):
    copy = pltpu.make_async_copy(src, dst, sem)
    copy.start()
    return copy


def norm(values):
    average = jnp.mean(values, axis=-1, keepdims=True)
    centred = values - average
    variance = jnp.mean(centred * centred, axis=-1, keepdims=True)
    inverse = lax.rsqrt(variance + norm_eps)
    return centred * inverse, inverse


def norm_back(grad, values, scale_row):
    normed, inverse = norm(values)
    dn = grad * (1.0 + scale_row)
    mean_one = jnp.mean(dn, axis=-1, keepdims=True)
    mean_two = jnp.mean(dn * normed, axis=-1, keepdims=True)
    dx = inverse * (dn - mean_one - normed * mean_two)
    return dx, jnp.sum(grad, axis=0, keepdims=True), jnp.sum(grad * normed, axis=0, keepdims=True)


def gelu_both(u):
    square = u * u
    half = 0.5 * jnp.tanh(u * (square * (0.044715 * GELU_C) + GELU_C)) + 0.5
    bend = u * (square * (6.0 * 0.044715 * GELU_C) + 2.0 * GELU_C)
    return u * half, half + half * (1.0 - half) * bend


def assemble_kernel(panels, first_size, index_ref, *refs):
    sources, sheet, sem = refs[:-2], refs[-2], refs[-1]
    rows = sheet.shape[0] // panels

    @pl.loop(0, panels, unroll=4)
    def _(p):
        where = index_ref[p]
        target = sheet.at[pl.ds(pl.multiple_of(p * rows, rows), rows)]
        if len(sources) == 1:
            pltpu.make_async_copy(sources[0].at[where], target, sem).start()
        else:

            @pl.when(where < first_size)
            def _():
                pltpu.make_async_copy(sources[0].at[where], target, sem).start()

            @pl.when(where >= first_size)
            def _():
                pltpu.make_async_copy(sources[1].at[where - first_size], target, sem).start()

    pltpu.make_async_copy(sheet, sheet, sem).wait()


def assemble(index, sources, panels):
    first_size = sources[0].shape[0]
    rows = sources[0].shape[1]
    return pl.pallas_call(
        functools.partial(assemble_kernel, panels, first_size),
        out_shape=pltpu.VMEM((panels * rows, D), bf16),
        in_specs=[pl.BlockSpec(memory_space=pltpu.SMEM)]
        + [pl.BlockSpec(memory_space=pltpu.HBM)] * len(sources),
        out_specs=pl.BlockSpec(memory_space=pltpu.VMEM),
        scratch_shapes=[pltpu.SemaphoreType.DMA],
        compiler_params=pltpu.CompilerParams(vmem_limit_bytes=VMEM_LIMIT),
        cost_estimate=pl.CostEstimate(flops=0, bytes_accessed=2 * panels * rows * D, transcendentals=0),
        name="assemble",
    )(index, *in_hbm(sources))


(
    N_XIN,
    N_H1,
    N_QKV,
    N_LSE,
    N_O,
    N_A,
    N_X1,
    N_H2,
    N_SLOPE,
    N_Z,
    N_B,
    N_OUT,
    N_DB,
    N_DU,
    N_DA,
    N_DX1,
    N_DMOD_FFN,
    N_DQKV,
    N_DMOD_ATT,
    N_G,
    N_SENT,
    N_DO,
    N_ACC,
    N_LSE_COLS,
    N_OUTS,
    N_GIN,
    N_MOD,
    N_X,
    N_AFTER,
    N_SECTION,
    N_LOSS,
) = range(31)


TILE = D
TILES = FF // TILE
PAIRS = HEADS // 2


def shapes_of(length):
    return {
        N_XIN: ((length, D), bf16),
        N_H1: ((length, D), bf16),
        N_QKV: ((length, 3 * D), bf16),
        N_LSE: ((16, length), f32),
        N_O: ((length, D), bf16),
        N_A: ((length, D), bf16),
        N_X1: ((length, D), f32),
        N_H2: ((length, D), bf16),
        N_SLOPE: ((length, FF), f32),
        N_Z: ((length, FF), bf16),
        N_B: ((length, D), bf16),
        N_OUT: ((length, D), bf16),
        N_DB: ((length, D), bf16),
        N_DU: ((length, FF), bf16),
        N_DA: ((length, D), bf16),
        N_DX1: ((length, D), f32),
        N_DMOD_FFN: ((4, D), f32),
        N_DQKV: ((length, 3 * D), bf16),
        N_DMOD_ATT: ((2, D), f32),
        N_G: ((length, D), bf16),
        N_SENT: ((length, D), bf16),
        N_DO: ((length, D), bf16),
        N_ACC: ((length, D), f32),
        N_LSE_COLS: ((length, 128), f32),
    }


def blocks_of(length):
    return [pl.ds(r, ROWS) for r in range(0, length, ROWS)]


def low_half():
    return lax.broadcasted_iota(jnp.int32, (1, 128), 1) < HEAD_DIM


def forward_qkv(v, w_qkv, row, length):
    for block in blocks_of(length):
        normed, _ = norm(v[N_XIN][block, :].astype(f32))
        v[N_H1][block, :] = (normed * (1.0 + row(1)) + row(0)).astype(bf16)
    for n in range(3):
        part = dot_nt(v[N_H1][...], w_qkv(n))
        v[N_QKV][:, n * D : (n + 1) * D] = part.astype(bf16)


def forward_attention(v, length):
    v[N_LSE_COLS][...] = jnp.zeros_like(v[N_LSE_COLS])
    low_lanes = low_half()

    @pl.loop(0, PAIRS, unroll=PAIRS)
    def _(pair):
        at = lambda n: pl.ds(pl.multiple_of(n * D + pair * 128, 128), 128)
        q = v[N_QKV][:, at(0)] * jnp.asarray(HEAD_DIM ** (-0.5), bf16)
        k = v[N_QKV][:, at(1)]
        value = v[N_QKV][:, at(2)]
        mixed = []
        for h in range(2):
            qh = jnp.where(low_lanes if h == 0 else ~low_lanes, q, jnp.zeros_like(q))
            v[N_SLOPE][:, h * length : (h + 1) * length] = dot_nt(qh, k)
        for h in range(2):
            lane = lax.broadcasted_iota(jnp.int32, (1, 128), 1) == pair * 2 + h
            span = slice(h * length, (h + 1) * length)
            for block in blocks_of(length):
                s = v[N_SLOPE][block, span]
                top = jnp.max(s, axis=-1, keepdims=True)
                e = jnp.exp(s - top)
                total = jnp.sum(e, axis=-1, keepdims=True)
                v[N_Z][block, span] = (e * (1.0 / total)).astype(bf16)
                v[N_LSE_COLS][block, :] = jnp.where(lane, top + jnp.log(total), v[N_LSE_COLS][block, :])
            mixed.append(dot_nn(v[N_Z][:, span], value))
        v[N_O][:, at(0)] = jnp.where(low_lanes, mixed[0], mixed[1]).astype(bf16)

    v[N_LSE][...] = v[N_LSE_COLS][...].T[:16, :]


def forward_proj(v, w_proj, row, length):
    v[N_ACC][...] = dot_nt(v[N_O][...], w_proj)
    for block in blocks_of(length):
        branch = v[N_ACC][block, :]
        v[N_A][block, :] = branch.astype(bf16)
        middle = v[N_XIN][block, :].astype(f32) + row(2) * branch
        v[N_X1][block, :] = middle
        normed, _ = norm(middle)
        v[N_H2][block, :] = (normed * (1.0 + row(4)) + row(3)).astype(bf16)


def forward_ffn(v, w_up, w_down, row, length, after):
    for n in range(TILES):
        span = slice(n * TILE, (n + 1) * TILE)
        v[N_SLOPE][:, span] = dot_nt(v[N_H2][...], w_up(n))
        for block in blocks_of(length):
            value, slope = gelu_both(v[N_SLOPE][block, span])
            v[N_Z][block, span] = value.astype(bf16)
            v[N_SLOPE][block, span] = slope
        part = dot_nn(v[N_Z][:, span], w_down(n))
        if n:
            v[N_ACC][...] += part
        else:
            v[N_ACC][...] = part
        after(n)
    for block in blocks_of(length):
        branch = v[N_ACC][block, :]
        v[N_B][block, :] = branch.astype(bf16)
        v[N_OUT][block, :] = (v[N_X1][block, :] + row(5) * branch).astype(bf16)


def back_gate(v, row, length, scale):
    gate_two = jnp.zeros((1, D), f32)
    for block in blocks_of(length):
        g = v[N_G][block, :].astype(f32)
        if scale is not None:
            g = g * scale
        v[N_DX1][block, :] = g
        v[N_DB][block, :] = (row(5) * g).astype(bf16)
        gate_two += jnp.sum(g * v[N_B][block, :].astype(f32), axis=0, keepdims=True)
    v[N_DMOD_FFN][3:4, :] = gate_two


def back_ffn_part(v, w_up, w_down, row, length, before, after):
    for n in range(TILES):
        span = slice(n * TILE, (n + 1) * TILE)
        before(n)
        dz = dot_nt(v[N_DB][...], w_down(n))
        v[N_DU][:, span] = (dz * v[N_SLOPE][:, span]).astype(bf16)
        part = dot_nn(v[N_DU][:, span], w_up(n))
        if n:
            v[N_ACC][...] += part
        else:
            v[N_ACC][...] = part
        after(n)


def back_middle(v, row, length):
    shift_two = jnp.zeros((1, D), f32)
    scale_two = jnp.zeros((1, D), f32)
    gate_one = jnp.zeros((1, D), f32)
    for block in blocks_of(length):
        dx, shift_part, scale_part = norm_back(v[N_ACC][block, :], v[N_X1][block, :], row(4))
        total = v[N_DX1][block, :] + dx
        v[N_DX1][block, :] = total
        shift_two += shift_part
        scale_two += scale_part
        gate_one += jnp.sum(total * v[N_A][block, :].astype(f32), axis=0, keepdims=True)
        v[N_DA][block, :] = (row(2) * total).astype(bf16)
    v[N_DMOD_FFN][0:1, :] = gate_one
    v[N_DMOD_FFN][1:2, :] = shift_two
    v[N_DMOD_FFN][2:3, :] = scale_two


def back_attention(v, w_proj, length):
    v[N_DO][...] = dot_nn(v[N_DA][...], w_proj).astype(bf16)
    low_lanes = low_half()
    scale = HEAD_DIM ** (-0.5)

    @pl.loop(0, PAIRS, unroll=PAIRS)
    def _(pair):
        at = lambda n: pl.ds(pl.multiple_of(n * D + pair * 128, 128), 128)
        q = v[N_QKV][:, at(0)]
        k = v[N_QKV][:, at(1)]
        value = v[N_QKV][:, at(2)]
        dop = v[N_DO][:, at(0)]
        zero = jnp.zeros_like(q)
        dq = dk = dv = None
        for h in range(2):
            lanes = low_lanes if h == 0 else ~low_lanes
            qh = jnp.where(lanes, q, zero)
            kh = jnp.where(lanes, k, zero)
            doh = jnp.where(lanes, dop, zero)
            st = dot_nt(k, qh * jnp.asarray(scale, bf16))
            pt = jnp.exp(st - v[N_LSE][pl.ds(pair * 2 + h, 1), :])
            dpt = dot_nt(value, doh)
            dv_part = dot_nn(pt.astype(bf16), doh)
            inner = jnp.sum(dpt * pt, axis=0, keepdims=True)
            drt = (pt * (dpt - inner) * scale).astype(bf16)
            dk_part = dot_nn(drt, qh)
            dq_part = dot_tn(drt, kh)
            dq = dq_part if h == 0 else dq + dq_part
            dk = dk_part if h == 0 else dk + dk_part
            dv = dv_part if h == 0 else dv + dv_part
        v[N_DQKV][:, at(0)] = dq.astype(bf16)
        v[N_DQKV][:, at(1)] = dk.astype(bf16)
        v[N_DQKV][:, at(2)] = dv.astype(bf16)


def back_input(v, w_qkv, row, length):
    v[N_ACC][...] = dot_nn(v[N_DQKV][...], w_qkv)
    shift_one = jnp.zeros((1, D), f32)
    scale_one = jnp.zeros((1, D), f32)
    for block in blocks_of(length):
        dx, shift_part, scale_part = norm_back(v[N_ACC][block, :], v[N_XIN][block, :].astype(f32), row(1))
        total = v[N_DX1][block, :] + dx
        v[N_DX1][block, :] = total
        v[N_SENT][block, :] = total.astype(bf16)
        shift_one += shift_part
        scale_one += scale_part
    v[N_DMOD_ATT][0:1, :] = shift_one
    v[N_DMOD_ATT][1:2, :] = scale_one


class Mover:
    def __init__(self, sems):
        self.sems, self.used, self.coming, self.going = sems, 0, {}, []

    def start(self, src, dst):
        copy = pltpu.make_async_copy(src, dst, self.sems.at[self.used])
        self.used += 1
        copy.start()
        return copy

    def fetch(self, name, src, dst):
        self.coming[name] = self.start(src, dst)

    def need(self, *names):
        for name in names:
            if name in self.coming:
                self.coming.pop(name).wait()

    def save(self, src, dst):
        self.going.append(self.start(src, dst))

    def finish(self):
        assert not self.coming
        for copy in self.going:
            copy.wait()


SEMS = 48


def call_block(kernel, name, want, clip, length, smem, sheet, read, write, hold, shared, chain, flops, moved, loose=None):
    any_spec = pl.BlockSpec(memory_space=pltpu.HBM)
    shapes = shapes_of(length)
    s_names, r_names, w_names = list(smem), list(read), list(write)
    chained = [n for n in w_names if chain.get(n) is not None]
    operands = [smem[n] for n in s_names] + [pltpu.with_memory_space_constraint(sheet, pltpu.VMEM)]
    operands += [read[n] if n == loose else in_hbm([read[n]])[0] for n in r_names]
    aliases = {len(operands) + i: w_names.index(n) for i, n in enumerate(chained)}
    operands += in_hbm([chain[n] for n in chained])

    def run(*refs):
        refs = list(refs)
        take = lambda names: dict(zip(names, [refs.pop(0) for _ in names]))
        s, w, r = take(s_names), refs.pop(0), take(r_names)
        take(chained)
        o = take(w_names)
        v = take(hold)
        v |= {n: v[other] for n, other in shared.items()}
        m, sems = refs

        @pl.when(s[N_SECTION][0] == want)
        def _():
            kernel(clip, length, s, m, r, o, v, w, Mover(sems))

    results = pl.pallas_call(
        run,
        out_shape=[pltpu.HBM(*write[n]) for n in w_names],
        in_specs=[pl.BlockSpec(memory_space=pltpu.SMEM)] * len(s_names)
        + [pl.BlockSpec(memory_space=pltpu.VMEM)]
        + [any_spec] * (len(r_names) + len(chained)),
        out_specs=[any_spec] * len(w_names),
        scratch_shapes=[pltpu.VMEM(*shapes[n]) for n in hold]
        + [pltpu.VMEM((6, D), f32), pltpu.SemaphoreType.DMA((SEMS,))],
        input_output_aliases=aliases,
        compiler_params=pltpu.CompilerParams(vmem_limit_bytes=VMEM_LIMIT),
        cost_estimate=pl.CostEstimate(flops=flops, bytes_accessed=moved, transcendentals=0),
        name=f"{name}_{clip}",
    )(*operands)
    return dict(zip(w_names, results))


def mod_row(m):
    return lambda n: m[n : n + 1, :]


def forward_body(clip, length, x_offset, m, r, v, w, mover, keep):
    row = mod_row(m)
    mover.fetch(N_MOD, r[N_MOD].at[clip], m)
    mover.fetch(N_XIN, r[N_X].at[pl.ds(x_offset, length)], v[N_XIN])
    mover.need(N_MOD, N_XIN)
    forward_qkv(v, lambda n: w[n * D : (n + 1) * D, :], row, length)
    keep(N_H1)
    keep(N_QKV)
    forward_attention(v, length)
    keep(N_LSE)
    keep(N_O)
    forward_proj(v, w[QKV_END:PROJ_END, :], row, length)
    keep(N_A)
    keep(N_X1)
    keep(N_H2)
    forward_ffn(
        v,
        lambda n: w[PROJ_END + n * D : PROJ_END + (n + 1) * D, :],
        lambda n: w[UP_END + n * D : UP_END + (n + 1) * D, :],
        row,
        length,
        lambda n: (keep(N_SLOPE, n), keep(N_Z, n)),
    )
    keep(N_B)


def saver(mover, v, o):
    def keep(name, n=None):
        if name not in o:
            return
        if n is None:
            mover.save(v[name], o[name])
        else:
            span = pl.ds(n * TILE, TILE)
            mover.save(v[name].at[:, span], o[name].at[:, span])

    return keep


FIRST_KEEP = (N_H1, N_QKV, N_LSE, N_O, N_A, N_X1, N_H2, N_SLOPE, N_Z, N_B)
BOTH_KEEP = (N_H1, N_O, N_H2, N_Z, N_DB, N_DU, N_DA, N_DQKV, N_DMOD_FFN, N_DMOD_ATT)


def first_forward(clip, clips, length, section, mod, x, sheet, outs):
    def kernel(clip, length, s, m, r, o, v, w, mover):
        forward_body(clip, length, clip * length, m, r, v, w, mover, saver(mover, v, o))
        mover.save(v[N_OUT], o[N_SENT])
        mover.save(v[N_OUT], o[N_OUTS].at[pl.ds(clip * length, length)])
        mover.finish()

    shapes = shapes_of(length)
    write = {n: shapes[n] for n in FIRST_KEEP}
    write |= {N_OUTS: ((clips * length, D), bf16), N_SENT: ((length, D), bf16)}
    hold = FIRST_KEEP + (N_XIN, N_OUT, N_ACC, N_LSE_COLS)
    return call_block(
        kernel, "first_forward", 0, clip, length, {N_SECTION: section}, sheet, {N_MOD: mod, N_X: x},
        write, hold, {}, {N_OUTS: outs}, 17 * 10**9, 30 << 20,
    )


def second_both(clip, clips, length, section, loss_weight, mod, x, g, sheet, chain):
    def kernel(clip, length, s, m, r, o, v, w, mover):
        keep = saver(mover, v, o)
        row = mod_row(m)
        forward_body(clip, length, 0, m, r, v, w, mover, keep)
        mover.fetch(N_G, r[N_G].at[pl.ds(clip * length, length)], v[N_G])
        mover.save(v[N_OUT], o[N_OUTS].at[pl.ds(clip * length, length)])
        mover.need(N_G)
        back_gate(v, row, length, s[N_LOSS][clip])
        keep(N_DB)
        back_ffn_part(
            v,
            lambda n: w[PROJ_END + n * D : PROJ_END + (n + 1) * D, :],
            lambda n: w[UP_END + n * D : UP_END + (n + 1) * D, :],
            row, length, lambda n: None, lambda n: keep(N_DU, n),
        )
        back_middle(v, row, length)
        keep(N_DA)
        keep(N_DMOD_FFN)
        back_attention(v, w[QKV_END:PROJ_END, :], length)
        keep(N_DQKV)
        back_input(v, w[0:QKV_END, :], row, length)
        mover.save(v[N_SENT], o[N_SENT])
        keep(N_DMOD_ATT)
        mover.save(v[N_DX1], o[N_GIN].at[pl.ds(clip * length, length)])
        mover.finish()

    shapes = shapes_of(length)
    write = {n: shapes[n] for n in BOTH_KEEP}
    write |= {N_OUTS: ((clips * length, D), bf16), N_GIN: ((clips * length, D), f32), N_SENT: ((length, D), bf16)}
    hold = (N_XIN, N_H1, N_QKV, N_LSE, N_O, N_A, N_X1, N_H2, N_SLOPE, N_Z, N_B, N_OUT, N_DB, N_DU, N_DX1)
    hold += (N_DMOD_FFN, N_DMOD_ATT, N_G, N_ACC, N_LSE_COLS)
    shared = {N_DQKV: N_QKV, N_DO: N_B, N_DA: N_A, N_SENT: N_G}
    return call_block(
        kernel, "second_both", 1, clip, length, {N_SECTION: section, N_LOSS: loss_weight},  sheet,
        {N_MOD: mod, N_X: x, N_G: g}, write, hold, shared, chain, 40 * 10**9, 40 << 20, N_X,
    )


BACK_MAKES = (N_DB, N_DU, N_DA, N_DQKV, N_DMOD_FFN, N_DMOD_ATT)


def first_back(clip, clips, length, section, mod, x, g, sheet, kept, chain, after):
    def kernel(clip, length, s, m, r, o, v, w, mover):
        keep = saver(mover, v, o)
        row = mod_row(m)
        mover.fetch(N_MOD, r[N_MOD].at[clip], m)
        mover.fetch(N_G, r[N_G], v[N_G])
        mover.fetch(N_B, r[N_B], v[N_B])
        for n in range(TILES):
            span = pl.ds(n * TILE, TILE)
            mover.fetch((N_SLOPE, n), r[N_SLOPE].at[:, span], v[N_SLOPE].at[:, span])
        for name in (N_X1, N_A, N_QKV, N_LSE):
            mover.fetch(name, r[name], v[name])
        mover.fetch(N_XIN, r[N_X].at[pl.ds(clip * length, length)], v[N_XIN])
        mover.need(N_MOD, N_G, N_B)
        back_gate(v, row, length, None)
        keep(N_DB)
        back_ffn_part(
            v,
            lambda n: w[PROJ_END + n * D : PROJ_END + (n + 1) * D, :],
            lambda n: w[UP_END + n * D : UP_END + (n + 1) * D, :],
            row, length, lambda n: mover.need((N_SLOPE, n)), lambda n: keep(N_DU, n),
        )
        mover.need(N_X1, N_A)
        back_middle(v, row, length)
        keep(N_DA)
        keep(N_DMOD_FFN)
        mover.need(N_QKV, N_LSE)
        back_attention(v, w[QKV_END:PROJ_END, :], length)
        keep(N_DQKV)
        mover.need(N_XIN)
        back_input(v, w[0:QKV_END, :], row, length)
        keep(N_DMOD_ATT)
        mover.save(v[N_DX1], o[N_GIN].at[pl.ds(clip * length, length)])
        mover.finish()

    shapes = shapes_of(length)
    read = {N_MOD: mod, N_X: x, N_G: g} | {n: kept[n] for n in (N_B, N_SLOPE, N_X1, N_A, N_QKV, N_LSE)}
    read[N_AFTER] = after
    write = {n: shapes[n] for n in BACK_MAKES} | {N_GIN: ((clips * length, D), f32)}
    hold = (N_G, N_B, N_SLOPE, N_X1, N_A, N_QKV, N_LSE, N_XIN, N_DB, N_DU, N_DX1, N_DMOD_FFN, N_DMOD_ATT, N_ACC)
    shared = {N_DQKV: N_QKV, N_DO: N_B, N_DA: N_A, N_SENT: N_G}
    return call_block(
        kernel, "first_back", 0, clip, length, {N_SECTION: section}, sheet, read,
        write, hold, shared, chain, 25 * 10**9, 30 << 20, N_G,
    )


def grads_kernel(jobs, clips, length, panel_rows, own, passed, others, code_ref, index_ref, *refs):
    count = 2 * len(jobs) * clips
    sources = refs[:count]
    refs = refs[count + others :]
    outs = refs[:own]
    scratch = refs[own + passed :]
    values = scratch[: 2 * len(jobs)]
    tile_v, in_sem, out_sem = scratch[2 * len(jobs) :]
    tiles = []
    for n, (left, right, base) in enumerate(jobs):
        tiles += [(n, column, base + column) for column in range(0, values[2 * n].shape[1], D)]
    get = {}

    def fetch(n, column):
        get[n, column] = [
            start(
                sources[n * clips + c].at[:, pl.ds(column, D)],
                values[n].at[pl.ds(c * length, length), pl.ds(column, D)],
                in_sem.at[len(get), c],
            )
            for c in range(clips)
        ]

    def fetch_tile(t):
        if t < len(tiles):
            n, column, _ = tiles[t]
            if column == 0:
                fetch(2 * n + 1, 0)
            fetch(2 * n, column)

    for t in range(3):
        fetch_tile(t)
    per_tile = D // panel_rows

    def drain(slot):
        pltpu.make_async_copy(outs[-1].at[pl.ds(0, per_tile)], tile_v.at[slot], out_sem.at[slot]).wait()

    for t, (n, column, first_row) in enumerate(tiles):
        slot = t % 2
        if column == 0:
            for copy in get[2 * n + 1, 0]:
                copy.wait()
        for copy in get[2 * n, column]:
            copy.wait()
        fetch_tile(t + 3)
        if t >= 2:
            drain(slot)
        part = dot_tn(values[2 * n][:, column : column + D], values[2 * n + 1][...])
        tile_v[slot, :, :, :] = part.astype(bf16).reshape(per_tile, panel_rows, D)

        @pl.loop(0, per_tile)
        def _(p):
            code = code_ref[first_row // panel_rows + p]
            where = index_ref[first_row // panel_rows + p]

            def put(numbers):
                for n_out in numbers:

                    @pl.when(code == n_out)
                    def _():
                        pltpu.make_async_copy(tile_v.at[slot, p], outs[n_out].at[where], out_sem.at[slot]).start()

            put(range(min(2, own)))
            if own > 2:

                @pl.when(code >= 2)
                def _():
                    put(range(2, own))

    for slot in range(min(2, len(tiles))):
        drain(slot)


def weight_grads(jobs, code, index, every, length, panel_rows, sizes, thread, after, through=()):
    clips = len(every)
    any_spec = pl.BlockSpec(memory_space=pltpu.HBM)
    operands, scratch = [code, index], []
    for left, right, _ in jobs:
        for name in (left, right):
            arrays = [every[c][name] for c in range(clips)]
            operands += arrays
            scratch.append(pltpu.VMEM((clips * length, arrays[0].shape[1]), bf16))
    aliases = {}
    for n, array in enumerate(thread):
        aliases[len(operands)] = len(sizes) - len(thread) + n
        operands.append(array)
    passed = [pltpu.HBM(a.shape, a.dtype) for a in through]
    for n, array in enumerate(through):
        aliases[len(operands)] = len(sizes) + n
        operands.append(array)
    operands += after
    width = sum(s.shape[1] for s in scratch[0::2])
    return pl.pallas_call(
        functools.partial(grads_kernel, jobs, clips, length, panel_rows, len(sizes), len(passed), len(thread) + len(through) + len(after)),
        out_shape=[pltpu.HBM((size, panel_rows, D), bf16) for size in sizes] + passed,
        in_specs=[pl.BlockSpec(memory_space=pltpu.SMEM)] * 2 + [any_spec] * (len(operands) - 2),
        out_specs=[any_spec] * (len(sizes) + len(passed)),
        scratch_shapes=scratch
        + [
            pltpu.VMEM((2, D // panel_rows, panel_rows, D), bf16),
            pltpu.SemaphoreType.DMA((width // D + len(jobs), clips)),
            pltpu.SemaphoreType.DMA((2,)),
        ],
        input_output_aliases=aliases,
        compiler_params=pltpu.CompilerParams(vmem_limit_bytes=VMEM_ALL),
        cost_estimate=pl.CostEstimate(
            flops=4 * clips * length * width * D, bytes_accessed=12 << 20, transcendentals=0
        ),
        name=f"grads_{jobs[0][2]}",
    )(*operands[:2], *in_hbm(operands[2:]))


GROUP = 8


def adam_kernel(n_sums, code_ref, index_ref, row_ref, master, first, second, dmod, cond, *refs):
    sums = refs[:n_sums]
    outs = refs[n_sums : n_sums + 4]
    scratch = refs[n_sums + 4 :]
    held = scratch[:3]
    made = scratch[3:7]
    grad_v, in_sem, grad_sem, out_sem = scratch[7:]
    slots, rows = master.shape[0], master.shape[1]
    groups = [(g, min(GROUP, slots - g)) for g in range(0, slots, GROUP)]
    get = [
        [start(a.at[pl.ds(g, size)], h.at[pl.ds(g, size)], in_sem.at[n, i]) for i, (a, h) in enumerate(zip((master, first, second), held))]
        for n, (g, size) in enumerate(groups)
    ]
    for n, (g, size) in enumerate(groups):

        @pl.loop(g, g + size)
        def _(slot):
            code = code_ref[slot]
            where = index_ref[slot]
            for n_sum in range(n_sums):

                @pl.when(code == n_sum)
                def _():
                    pltpu.make_async_copy(sums[n_sum].at[where], grad_v.at[slot], grad_sem.at[n]).start()

    put = []
    for n, (g, size) in enumerate(groups):
        for copy in get[n]:
            copy.wait()
        span = pl.ds(g, size)

        @pl.loop(g, g + size)
        def _(slot):
            code = code_ref[slot]

            @pl.when(code < n_sums)
            def _():
                pltpu.make_async_copy(sums[0].at[0], grad_v.at[slot], grad_sem.at[n]).wait()

        @pl.loop(g, g + size)
        def _(slot):
            code = code_ref[slot]

            def update(grad):
                first_next = beta_one * held[1][slot] + (1.0 - beta_one) * grad
                second_next = beta_two * held[2][slot] + (1.0 - beta_two) * grad * grad
                first_hat = first_next / (1.0 - beta_one**STEP)
                second_hat = second_next / (1.0 - beta_two**STEP)
                value = held[0][slot] - learn_rate * (
                    first_hat / (jnp.sqrt(second_hat) + adam_eps) + decay_rate * held[0][slot]
                )
                made[0][slot] = value
                made[1][slot] = first_next
                made[2][slot] = second_next
                made[3][slot] = value.astype(bf16)

            @pl.when(code < n_sums)
            def _():
                update(grad_v[slot].astype(f32))

            @pl.when(code == n_sums)
            def _():
                at = pl.multiple_of(row_ref[slot], rows)
                update(dot_nn(dmod[pl.ds(at, rows), :], cond[...]))

            @pl.when(code > n_sums)
            def _():
                update(jnp.zeros((rows, D), f32))

        for i in range(4):
            put.append(start(made[i].at[span], outs[i].at[span], out_sem.at[n, i]))
    for copy in put:
        copy.wait()


def adam(code, index, row, master, first, second, dmod, cond, sums):
    slots, rows = master.shape[0], master.shape[1]
    any_spec = pl.BlockSpec(memory_space=pltpu.HBM)
    smem, vmem = pl.BlockSpec(memory_space=pltpu.SMEM), pl.BlockSpec(memory_space=pltpu.VMEM)
    kinds = [f32, f32, f32, bf16]
    groups = -(-slots // GROUP)
    return pl.pallas_call(
        functools.partial(adam_kernel, len(sums)),
        in_specs=[smem] * 3 + [any_spec] * 3 + [vmem] * 2 + [any_spec] * len(sums),
        out_specs=[any_spec] * 4,
        out_shape=[pltpu.HBM(master.shape, kind) for kind in kinds],
        scratch_shapes=[pltpu.VMEM(master.shape, f32)] * 3
        + [pltpu.VMEM(master.shape, kind) for kind in kinds]
        + [
            pltpu.VMEM(master.shape, bf16),
            pltpu.SemaphoreType.DMA((groups, 3)),
            pltpu.SemaphoreType.DMA((groups,)),
            pltpu.SemaphoreType.DMA((groups, 4)),
        ],
        compiler_params=pltpu.CompilerParams(vmem_limit_bytes=VMEM_ALL),
        cost_estimate=pl.CostEstimate(flops=0, bytes_accessed=slots * rows * D * 30, transcendentals=0),
        name="adam",
    )(code, index, row, *in_hbm((master, first, second)), dmod, cond, *in_hbm(sums))


CHIPS = 8
LOOP = (0, 2, 4, 6, 7, 5, 3, 1)


def swap_cores(value):
    return lax.ppermute(value, BATCH, [(d, d ^ 1) for d in range(2 * CHIPS)])


def along(value, step):
    pairs = [
        (2 * LOOP[n] + core, 2 * LOOP[(n + step) % CHIPS] + core) for n in range(CHIPS) for core in range(2)
    ]
    return lax.ppermute(value, BATCH, pairs)


class Ring:
    def __init__(self, place, mine, other):
        self.place, self.size, self.left = place, mine.shape[0] // CHIPS, 4
        self.half = self.size // 2
        self.terms = (mine, swap_cores(other))

    def term(self, offset, low, high):
        first = ((self.place + offset) % CHIPS) * self.size + low
        return sum(lax.dynamic_slice_in_dim(a, first, high - low, 0).astype(f32) for a in self.terms)

    def hop(self):
        n, half, size = self.left, self.half, self.size
        if n == 4:
            ahead, behind = self.term(4, 0, half), self.term(-4, half, size)
        elif n == 3:
            ahead = jnp.concatenate([self.term(3, 0, half) + self.ahead.astype(f32), self.term(3, half, size)])
            behind = jnp.concatenate([self.term(-3, 0, half), self.term(-3, half, size) + self.behind.astype(f32)])
        else:
            ahead = self.term(n, 0, size) + self.ahead.astype(f32)
            behind = self.term(-n, 0, size) + self.behind.astype(f32)
        self.payload = [ahead.astype(bf16), behind.astype(bf16)]
        self.left -= 1
        self.send()

    def send(self):
        self.ahead, self.behind = along(self.payload[0], 1), along(self.payload[1], -1)

    def held(self, count=2):
        self.count = count
        return list(self.terms[:count])

    def later(self, made):
        self.terms = tuple(made[-self.count :]) + self.terms[self.count :]
        return made[: -self.count]

    def finish(self):
        while self.left:
            self.hop()
        return (self.term(0, 0, self.size) + self.ahead.astype(f32) + self.behind.astype(f32)).astype(bf16)


def time_features(steps_in):
    half_width = D // 2
    freqs = jnp.exp(-math.log(10000.0) * jnp.arange(half_width, dtype=f32) / half_width)
    angles = steps_in.astype(f32)[:, None] * freqs[None, :]
    return jnp.concatenate([jnp.cos(angles), jnp.sin(angles)], axis=1)


def body(tokens, cotangent, loss_weight, timesteps, owners, master, first_moment, second_moment):
    section_index = lax.axis_index(SECTION)
    me = lax.axis_index(BATCH)
    owner_total = lax.axis_size(BATCH)
    slots, panel_rows = master.shape[1], master.shape[2]
    clips = timesteps.shape[0]
    length = tokens.shape[0] // clips
    owner = owners[0]
    panels = owner.shape[0]
    moved = DOWN_END // panel_rows
    cap = min(slots, max(4, (slots * 27 + 30) // 31))
    section = jnp.reshape(section_index, (1,)).astype(jnp.int32)

    number = jnp.arange(panels, dtype=jnp.int32)
    same = (owner[:, None] == owner[None, :]) & (number[None, :] < number[:, None])
    rank = jnp.sum(same.astype(jnp.int32), axis=1)
    first_size = owner_total * cap
    place = jnp.where(
        rank < cap, owner * cap + rank, first_size + owner * (slots - cap) + rank - cap
    )[:moved]
    mine = (owner[None, :] == me) & (
        rank[None, :] == jnp.arange(slots, dtype=jnp.int32)[:, None]
    )
    slot_panel = jnp.sum(jnp.where(mine, number[None, :] + 1, 0), axis=1) - 1
    kind = jnp.where(slot_panel < 0, 0, jnp.where(slot_panel < moved, 1, 2)).astype(jnp.int32)
    grad_row = jnp.where(kind == 2, (slot_panel - moved) * panel_rows, 0).astype(jnp.int32)

    rings = owner_total == 2 * CHIPS
    code, index, slot_code, slot_index, sizes, beyond = routes(owner, rank, mine, me, owner_total, slots, moved)
    low = master[0].astype(bf16)
    gathered = lax.all_gather(low[:cap], BATCH, axis=0, tiled=True)
    spot = jnp.arange(owner_total * clips, dtype=jnp.int32) // clips == me
    news = [jnp.where(spot, jnp.tile(timesteps.astype(f32), owner_total), 0.0)]
    past = jnp.max(jnp.where(number < moved, rank, 0)) >= cap
    news.append(jnp.stack([past, beyond]).astype(f32) + 0.0 * low[0, 0, 0].astype(f32))
    news = lax.pmax(jnp.concatenate(news), (SECTION, BATCH))
    all_steps = news[:-2]
    beyond = news[-1] > 0.5
    sources = [gathered]
    if cap < slots:
        rest_shape = (owner_total * (slots - cap), panel_rows, D)
        sources.append(
            lax.cond(
                news[-2] + 0.0 * gathered[0, 0, 0].astype(f32) > 0.5,
                lambda part: lax.all_gather(part, BATCH, axis=0, tiled=True),
                lambda part: jnp.zeros(rest_shape, bf16),
                low[cap:],
            )
        )
    sheet = assemble(place, sources, moved)

    cond = jax.nn.silu(time_features(all_steps)).astype(bf16)
    clip_total = cond.shape[0]
    share = jnp.einsum("cd,sd->cs", cond, low.reshape(slots * panel_rows, D), preferred_element_type=f32)
    share = lax.all_to_all(
        share.reshape(owner_total, clips, slots * panel_rows), BATCH, split_axis=0, concat_axis=0, tiled=True
    )
    share = share.reshape(owner_total, clips, slots, panel_rows).transpose(1, 0, 2, 3)
    share = share.reshape(clips, owner_total * slots, panel_rows)
    pick = (
        (owner * slots + rank)[moved:, None] == jnp.arange(owner_total * slots, dtype=jnp.int32)[None, :]
    ).astype(f32)
    mod = jnp.einsum("ps,csr->cpr", pick, share, precision=lax.Precision.HIGHEST)
    mod = mod.reshape(clips, 6, D)

    run = functools.partial
    base = dict(clips=clips, length=length, section=section, mod=mod, sheet=sheet)
    firsts, outs = [], None
    for c in range(clips):
        firsts.append(first_forward(c, x=tokens, outs=outs, **base))
        outs = firsts[c][N_OUTS]
    received = [lax.ppermute(f[N_SENT], SECTION, [(0, 1)]) for f in firsts]
    seconds, gin = [], None
    for c in range(clips):
        chain = {n: firsts[c][n] for n in (N_H1, N_O, N_H2, N_Z)} | {N_OUTS: outs, N_GIN: gin}
        seconds.append(second_both(c, loss_weight=loss_weight, x=received[c], g=cotangent, chain=chain, **base))
        outs, gin = seconds[c][N_OUTS], seconds[c][N_GIN]
    received = [lax.ppermute(f[N_SENT], SECTION, [(1, 0)]) for f in seconds]
    every = [dict(f) for f in seconds]

    for c in range(clips):
        chain = {n: every[c][n] for n in BACK_MAKES} | {N_GIN: gin}
        every[c] |= first_back(c, x=tokens, g=received[c], kept=firsts[c], chain=chain, after=every[0][N_DMOD_ATT] if c else mod, **base)
        gin = every[c][N_GIN]

    dmod = [jnp.concatenate([e[N_DMOD_ATT], e[N_DMOD_FFN]]) for e in every]
    dmod = jnp.stack(dmod).reshape(1, clips, 6 * D).astype(bf16)
    dmod = lax.all_to_all(jnp.broadcast_to(dmod, (owner_total, clips, 6 * D)), BATCH, split_axis=0, concat_axis=0, tiled=True)
    dmod = dmod.reshape(clip_total, 6 * D).T
    grads = run(weight_grads, code=code, index=index, every=every, length=length, panel_rows=panel_rows)
    if rings:
        place = me // 4 + (me // 2) % 2 * (CHIPS - 1 - 2 * (me // 4))
        wide = [sizes[1]] * 2 + [sizes[2]]
        first_jobs = ((N_DA, N_O, QKV_END), (N_DQKV, N_H1, 0), (N_DU, N_H2, PROJ_END))
        made = grads(first_jobs, sizes=[sizes[0]] * 2 + wide, thread=[], after=[])
        first = Ring(place, *made[:2])
        made = grads(((N_Z, N_DB, UP_END),), sizes=wide, thread=made[2:], after=[dmod], through=first.held(1))
        made = first.later(made)
        second = Ring(place, *made[:2])
        sums = []
        for ring in (first, second):
            half = ring.finish()
            sums += [half, swap_cores(half)]
        sums.append(
            lax.cond(
                beyond,
                lambda part: lax.psum_scatter(part, BATCH, scatter_dimension=0, tiled=True),
                lambda part: jnp.zeros((slots, panel_rows, D), bf16),
                made[2],
            )
        )
    else:
        jobs = ((N_Z, N_DB, UP_END), (N_DU, N_H2, PROJ_END), (N_DA, N_O, QKV_END), (N_DQKV, N_H1, 0))
        (made,) = grads(jobs, sizes=[sizes[0]], thread=[], after=[])
        sums = [lax.psum_scatter(made, BATCH, scatter_dimension=0, tiled=True)]
    slot_code = jnp.where(kind == 1, slot_code, jnp.where(kind == 2, len(sums), len(sums) + 1))
    results = adam(
        slot_code, slot_index, grad_row, master[0], first_moment[0], second_moment[0], dmod, cond, sums
    )
    return (outs[None], gin[None], *(r[None] for r in results))


CAPS = (24, 24)


def count_before(flag, group):
    number = jnp.arange(group.shape[0], dtype=jnp.int32)
    before = (group[:, None] == group[None, :]) & (number[None, :] < number[:, None]) & flag[None, :]
    return jnp.sum(before.astype(jnp.int32), axis=1)


def routes(owner, rank, mine, me, owner_total, slots, moved):
    if owner_total != 2 * CHIPS:
        code = jnp.zeros((moved,), jnp.int32)
        return code, (owner * slots + rank)[:moved], jnp.zeros((slots,), jnp.int32), jnp.arange(slots, dtype=jnp.int32), [owner_total * slots], jnp.bool_(False)
    number = jnp.arange(moved, dtype=jnp.int32)
    held, core = owner[:moved], me % 2
    chip = held // 2
    spot = chip // 2 + chip % 2 * (CHIPS - 1 - 2 * (chip // 2))
    per_row = DOWN_END // moved
    down = number >= UP_END // per_row
    order = count_before(~down, chip)
    late = down | (order >= CAPS[0])
    order = jnp.where(late, count_before(late, chip), order)
    rest = late & (order >= CAPS[1])
    half = order % 2
    size = jnp.where(late, CAPS[1] // 2, CAPS[0] // 2)
    index = jnp.where(rest, held * slots + rank[:moved], spot * size + order // 2)
    away = (half != core).astype(jnp.int32)
    code = jnp.where(rest, 4, jnp.where(late, 2 + away, away))
    code = jnp.where(down, code - 2, code).astype(jnp.int32)
    taken = mine[:, :moved].astype(jnp.int32)
    found = jnp.where(rest, 4, 2 * late.astype(jnp.int32) + away)
    slot_code = jnp.sum(taken * found[None, :], axis=1)
    slot_index = jnp.sum(taken * jnp.where(rest, rank[:moved], order // 2)[None, :], axis=1)
    sizes = [CHIPS * cap // 2 for cap in CAPS] + [owner_total * slots]
    return code, index.astype(jnp.int32), slot_code.astype(jnp.int32), slot_index.astype(jnp.int32), sizes, jnp.any(rest)


def solution(mesh):
    placed = (
        P(BATCH, None),
        P(BATCH, None),
        P(BATCH),
        P(BATCH),
        P(SECTION, None),
        P(SECTION, BATCH, None, None),
        P(SECTION, BATCH, None, None),
        P(SECTION, BATCH, None, None),
    )
    return jax.shard_map(
        body,
        mesh=mesh,
        in_specs=placed,
        out_specs=(
            P(SECTION, BATCH, None),
            P(SECTION, BATCH, None),
            P(SECTION, BATCH, None, None),
            P(SECTION, BATCH, None, None),
            P(SECTION, BATCH, None, None),
            P(SECTION, BATCH, None, None),
        ),
        check_vma=False,
    )
```

time: 1340 us -> 495 us (0.37)
  waiting for transfers between devices: 585 us -> 165 us
  matrix products: 375 us -> 1.12 us
  Pallas kernels: 0 us -> 167 us
  other arithmetic: 191 us -> 37 us
  local copies, waits for them, and re-layouts: 144 us -> 16.5 us
  blocking collectives: 0 us -> 42.5 us
  starting transfers between devices: 20.5 us -> 42.4 us
    unnamed x3 -> x1, waiting for transfers between devices: 450 us -> 0.02 us
    dot_general x60 -> x2, matrix products: 375 us -> 1.12 us  [the longest x1 0.59 us: body(): jnp.einsum('ps,csr->cpr', pick, share, precision=lax.Precision.HIGHEST)]
    pallas_call x0 -> x10, Pallas kernels: none -> 167 us  [the longest x6 118 us: call_block(): pl.pallas_call(run, out_shape=[pltpu.HBM(*write[n]) for n in w_names], in...]
    ppermute x4 -> x24, waiting for transfers between devices: 16 us -> 109 us  [the longest x16 70.2 us: along(): return lax.ppermute(value, BATCH, pairs)]
    all_gather x1, waiting for transfers between devices: 120 us -> 48.4 us  [body(): gathered = lax.all_gather(low[:cap], BATCH, axis=0, tiled=True)]
    gather x2 -> x0, local copies, waits for them, and re-layouts: 60.3 us -> none  [the longest x1 36.9 us: slot_terms(): picked = grad_panels[jnp.maximum(slot_panel, 0)]]
    add x7 -> x3, other arithmetic: 45.7 us -> 1.94 us  [the longest x1 1.21 us: body(): owner * slots + rank]
    pmax x0 -> x1, blocking collectives: none -> 42.5 us  [body(): news = lax.pmax(jnp.concatenate(news), (SECTION, BATCH))]
  transfers between devices with their start and end apart: 6 -> 27, of which waited for: 4 -> 14; matrix products, arithmetic and copies ran while one was open for 7% -> 8% of each run, Pallas kernels for 0% -> 22%
where the time goes in v3:
time: 495 us; the launch traced here: 490 us
  Pallas kernels  167 us (34%)
  waiting for transfers between devices  165 us (33%)
  blocking collectives  42.5 us (9%)
  starting transfers between devices  42.4 us (9%)
  other arithmetic  37 us (7%)
  between operations  18.1 us (4%)
  local copies, waits for them, and re-layouts  16.5 us (3%)
    pallas_call x6, Pallas kernels, call_block(): pl.pallas_call(run, out_shape=[pltpu.HBM(*write[n]) for n in w_names], in...  118 us
    ppermute x16, waiting for transfers between devices, along(): return lax.ppermute(value, BATCH, pairs)  70.2 us
    all_gather x1, waiting for transfers between devices, body(): gathered = lax.all_gather(low[:cap], BATCH, axis=0, tiled=True)  48.4 us
    pmax x1, blocking collectives, body(): news = lax.pmax(jnp.concatenate(news), (SECTION, BATCH))  42.5 us
    ppermute x2, waiting for transfers between devices, body(): received = [lax.ppermute(f[N_SENT], SECTION, [(1, 0)]) for f in seconds]  38.6 us
    pallas_call x2, Pallas kernels, weight_grads(): pl.pallas_call(functools.partial(grads_kernel, jobs, clips, length, panel...  32.4 us
    ppermute x16, starting transfers between devices, along(): return lax.ppermute(value, BATCH, pairs)  14.3 us
    convert_element_type x8, other arithmetic, hop(): self.payload = [ahead.astype(bf16), behind.astype(bf16)]  12.5 us
  transfers between devices with their start and end apart: 27, of which 14 were waited for; matrix products, arithmetic and copies ran while one was open for 8% of the time, Pallas kernels for 22%

profile of v3, /device:TPU:1, one launch (start us, length us, event | category | flops | bytes accessed | tf_op | source)
XLA Modules:
  0.0 490.2 jit_solution(6385778023690031221)
XLA Ops:
  7.2 3.2 fusion.28
  10.5 1.2 slice.61
  14.3 1.2 multiply_add_fusion
  17.6 42.5 %pmax.7 = f32[34]{0:T(128)S(1)} all-reduce(f32[34]{0:T(128)S(1)} %pad_maximum_fusion.7), channel_id=1, replica_groups=mesh['section'=2,'batch'=16] {'section','batch'}, use_global_device_ids=true, to_apply=%region_5.6 | all-reduce | flops 34 | bytes 272 | tf_op jit(solution)/shard_map/pmax | solution.py:899
  62.2 5.9 %all-to-all-start = ((f32[16,2,992]{2,1,0:T(2,128)}), f32[16,2,992]{2,1,0:T(2,128)S(1)}, u32[]{:S(2)}, u32[]{:S(2)}) async-start(f32[16,2,992]{2,1,0:T(2,128)} %copy.59), calls=%async_computation.1 | async-start | bytes 262144 | tf_op jit(solution)/shard_map/all_to_all | solution.py:918
  69.4 8.0 %all-to-all-done = f32[16,2,992]{2,1,0:T(2,128)S(1)} async-done(((f32[16,2,992]{2,1,0:T(2,128)}), f32[16,2,992]{2,1,0:T(2,128)S(1)}, u32[]{:S(2)}, u32[]{:S(2)}) %all-to-all-start) | async-done | bytes 127008 | tf_op jit(solution)/shard_map/all_to_all | solution.py:918
  79.1 48.4 %all-gather.5.cloned.1.call-done.refs_0_ = bf16[432,32,768]{2,1,0:T(8,128)(2,1)} async-done(((bf16[27,32,768]{2,1,0:T(8,128)(2,1)}), bf16[432,32,768]{2,1,0:T(8,128)(2,1)}) %all-gather.5.cloned.1.call-update) | async-done | bytes 21233680 | tf_op jit(solution)/shard_map/all_gather | solution.py:894
  127.5 1.2 slice.63
  130.0 2.1 conditional.2
  130.0 2.0 broadcast.202
  132.1 5.8 %assemble.1.refs_1_.refs_2_ = bf16[9216,768]{1,0:T(8,128)(2,1)S(1)} custom-call(s32[288]{0:T(512)} %bitcast.54, bf16[432,32,768]{2,1,0:T(8,128)(2,1)} %all-gather.5.cloned.1.call-done.refs_0_, bf16[64,32,768]{2,1,0:T(8,128)(2,1)} %get-tuple-element.204.refs_1_), custom_call_target="tpu_custom_call" | custom-call | bytes 14155776 | tf_op jit(solution)/shard_map/assemble/pallas_call | solution.py:109
  137.9 18.8 %first_forward_0.1 = (bf16[512,768]{1,0:T(8,128)(2,1)}, bf16[512,2304]{1,0:T(8,128)(2,1)}, f32[16,512]{1,0:T(8,128)}, bf16[512,768]{1,0:T(8,128)(2,1)}, bf16[512...) custom-call(s32[1]{0:T(128)} %bitcast.refs_0_, ...), custom_call_target="tpu_custom_call" | custom-call | flops 16999999488 | bytes 31457280 | tf_op jit(solution)/shard_map/first_forward_0/pallas_call | solution.py:416
  156.7 1.3 collective-permute-start.1
  158.0 18.4 %first_forward_1.1 = (bf16[512,768]{1,0:T(8,128)(2,1)}, bf16[512,2304]{1,0:T(8,128)(2,1)}, f32[16,512]{1,0:T(8,128)}, bf16[512,768]{1,0:T(8,128)(2,1)}, bf16[512...) custom-call(s32[1]{0:T(128)} %bitcast.refs_0_, ...), custom_call_target="tpu_custom_call", output_to_operand_aliasing={{10}: (4, {})} | custom-call | flops 16999999488 | bytes 31457280 | tf_op jit(solution)/shard_map/first_forward_1/pallas_call | solution.py:416
  176.4 1.3 collective-permute-start
  178.7 15.0 %second_both_0.1 = (bf16[512,768]{1,0:T(8,128)(2,1)}, bf16[512,768]{1,0:T(8,128)(2,1)}, bf16[512,768]{1,0:T(8,128)(2,1)}, bf16[512,3072]{1,0:T(8,128)(2,1)}, bf1...) custom-call(s32[1]{0:T(128)} %bitcast.refs_0_, ...), custom_call_target="tpu_custom_call", output_to_operand_aliasing={{0}: (6, {}), {1}: (7, {}), {2}: (8, {}), {3}: (9, {}), {10... | custom-call | flops 40000000000 | bytes 41943040 | tf_op jit(solution)/shard_map/second_both_0/pallas_call | solution.py:416
  193.7 1.3 collective-permute-start.3
  195.9 15.0 %second_both_1.1 = (bf16[512,768]{1,0:T(8,128)(2,1)}, bf16[512,768]{1,0:T(8,128)(2,1)}, bf16[512,768]{1,0:T(8,128)(2,1)}, bf16[512,3072]{1,0:T(8,128)(2,1)}, bf1...) custom-call(s32[1]{0:T(128)} %bitcast.refs_0_, ...), custom_call_target="tpu_custom_call", output_to_operand_aliasing={{0}: (6, {}), {1}: (7, {}), {2}: (8, {}), {3}: (9, {}), {10... | custom-call | flops 40000000000 | bytes 41943040 | tf_op jit(solution)/shard_map/second_both_1/pallas_call | solution.py:416
  211.0 1.3 collective-permute-start.2
  212.3 24.6 %collective-permute-done.3.refs_4_ = bf16[512,768]{1,0:T(8,128)(2,1)S(1)} collective-permute-done((bf16[512,768]{1,0:T(8,128)(2,1)}, bf16[512,768]{1,0:T(8,128)(2,1)S(1)}, u32[]{:S(2)}, u32[]{:S(2)}) %collective-permute-start.3) | collective-permute-done | bytes 786464 | tf_op jit(solution)/shard_map/ppermute | solution.py:941
  237.7 25.7 %first_back_0.1 = (bf16[512,768]{1,0:T(8,128)(2,1)}, bf16[512,3072]{1,0:T(8,128)(2,1)}, bf16[512,768]{1,0:T(8,128)(2,1)}, bf16[512,2304]{1,0:T(8,128)(2,1)}, f32...) custom-call(s32[1]{0:T(128)} %bitcast.refs_0_, ...), custom_call_target="tpu_custom_call", output_to_operand_aliasing={{0}: (12, {}), {1}: (13, {}), {2}: (14, {}), {3}: (15, {}),... | custom-call | flops 24999999488 | bytes 31457280 | tf_op jit(solution)/shard_map/first_back_0/pallas_call | solution.py:416
  264.8 14.0 %collective-permute-done.2.refs_4_ = bf16[512,768]{1,0:T(8,128)(2,1)S(1)} collective-permute-done((bf16[512,768]{1,0:T(8,128)(2,1)}, bf16[512,768]{1,0:T(8,128)(2,1)S(1)}, u32[]{:S(2)}, u32[]{:S(2)}) %collective-permute-start.2) | collective-permute-done | bytes 786464 | tf_op jit(solution)/shard_map/ppermute | solution.py:941
  279.7 25.5 %first_back_1.1 = (bf16[512,768]{1,0:T(8,128)(2,1)}, bf16[512,3072]{1,0:T(8,128)(2,1)}, bf16[512,768]{1,0:T(8,128)(2,1)}, bf16[512,2304]{1,0:T(8,128)(2,1)}, f32...) custom-call(s32[1]{0:T(128)} %bitcast.refs_0_, ...), custom_call_target="tpu_custom_call", output_to_operand_aliasing={{0}: (12, {}), {1}: (13, {}), {2}: (14, {}), {3}: (15, {}),... | custom-call | flops 24999999488 | bytes 31457280 | tf_op jit(solution)/shard_map/first_back_1/pallas_call | solution.py:416
  307.6 5.9 %all-to-all-start.1 = ((bf16[16,2,4608]{2,1,0:T(2,128)(2,1)}), bf16[16,2,4608]{2,1,0:T(2,128)(2,1)S(1)}, u32[]{:S(2)}, u32[]{:S(2)}) async-start(bf16[16,2,4608]{2,1,0:T(2,128)(2,1)} %broadcast_in_dim.101), calls=%async_computation.2 | async-start | bytes 589824 | tf_op jit(solution)/shard_map/all_to_all | solution.py:951
  313.4 20.5 %grads_2304.1 = (bf16[96,32,768]{2,1,0:T(8,128)(2,1)}, bf16[96,32,768]{2,1,0:T(8,128)(2,1)}, bf16[96,32,768]{2,1,0:T(8,128)(2,1)}, bf16[96,32,768]{2,1,0:T(8,128)(2,1)}, bf16[496,32,768]{2,1,0:T(8,128)(2,1)}) custom-call(s32[288]{0:T(512)} %get-tuple-element.176.code_ref, s32[288]{0:T(512)} %get-tuple-element.173.index_ref, ...), custom_call_target="tpu_custom_call" | custom-call | flops 19327352832 | bytes 12582912 | tf_op jit(solution)/shard_map/grads_2304/pallas_call | solution.py:678
  334.3 1.4 copy.63
  335.7 11.8 %grads_6144.1 = (bf16[96,32,768]{2,1,0:T(8,128)(2,1)}, bf16[96,32,768]{2,1,0:T(8,128)(2,1)}, bf16[496,32,768]{2,1,0:T(8,128)(2,1)}, bf16[96,32,768]{2,1,0:T(8,128)(2,1)}) custom-call(s32[288]{0:T(512)} %get-tuple-element.176.code_ref, s32[288]{0:T(512)} %get-tuple-element.173.index_ref, ...), custom_call_target="tpu_custom_call", output_to_operand_aliasing={{0}: (6, {}), {1}: (7, {}), {2}: (8, {}), {3}: (9, {})} | custom-call | flops 9663676416 | bytes 12582912 | tf_op jit(solution)/shard_map/grads_6144/pallas_call | solution.py:678
  348.0 1.1 add_convert_fusion.21
  349.2 1.4 collective-permute-start.5
  350.6 7.1 %collective-permute-done.5 = bf16[6,32,768]{2,1,0:T(8,128)(2,1)S(1)} collective-permute-done((bf16[6,32,768]{2,1,0:T(8,128)(2,1)S(1)}, bf16[6,32,768]{2,1,0:T(8,128)(2,1)S(1)}, u32[]{:S(2)}, u32[]{:S(2)}) %collective-permute-start.5) | collective-permute-done | bytes 294944 | tf_op jit(solution)/shard_map/ppermute | solution.py:813
  357.7 2.0 add_convert_fusion.20
  359.7 1.2 collective-permute-start.9
  362.4 1.2 collective-permute-start.15
  363.6 3.7 collective-permute-done.9
  367.3 1.2 add_convert_fusion.16
  370.2 10.4 %collective-permute-done.15 = bf16[6,32,768]{2,1,0:T(8,128)(2,1)S(1)} collective-permute-done((bf16[6,32,768]{2,1,0:T(8,128)(2,1)S(1)}, bf16[6,32,768]{2,1,0:T(8,128)(2,1)S(1)}, u32[]{:S(2)}, u32[]{:S(2)}) %collective-permute-start.15) | collective-permute-done | bytes 294944 | tf_op jit(solution)/shard_map/ppermute | solution.py:813
  380.6 2.0 add_convert_fusion.14
  382.7 1.2 collective-permute-start.19
  384.3 1.5 add_convert_fusion.9
  386.4 2.4 collective-permute-done.19
  388.8 1.2 add_convert_fusion.10
  390.8 1.2 collective-permute-start.20
  392.0 4.1 collective-permute-done.16
  396.1 1.5 add_convert_fusion.4
  398.0 10.8 %collective-permute-done.7 = bf16[12,32,768]{2,1,0:T(8,128)(2,1)S(1)} collective-permute-done((bf16[12,32,768]{2,1,0:T(8,128)(2,1)S(1)}, bf16[12,32,768]{2,1,0:T(8,128)(2,1)S(1)}, u32[]{:S(2)}, u32[]{:S(2)}) %collective-permute-start.7) | collective-permute-done | bytes 589856 | tf_op jit(solution)/shard_map/ppermute | solution.py:813
  408.8 2.2 add_convert_fusion.8
  411.0 1.2 collective-permute-start.11
  412.2 9.2 %collective-permute-done.17 = bf16[12,32,768]{2,1,0:T(8,128)(2,1)S(1)} collective-permute-done((bf16[12,32,768]{2,1,0:T(8,128)(2,1)S(1)}, bf16[12,32,768]{2,1,0:T(8,128)(2,1)S(1)}, u32[]{:S(2)}, u32[]{:S(2)}) %collective-permute-start.17) | collective-permute-done | bytes 589856 | tf_op jit(solution)/shard_map/ppermute | solution.py:813
  421.4 2.2 add_convert_fusion.3
  423.6 1.2 collective-permute-start.21
  425.5 1.5 add_convert_fusion.6
  427.0 1.2 collective-permute-start.12
  428.2 8.6 %collective-permute-done.21 = bf16[12,32,768]{2,1,0:T(8,128)(2,1)S(1)} collective-permute-done((bf16[12,32,768]{2,1,0:T(8,128)(2,1)S(1)}, bf16[12,32,768]{2,1,0:T(8,128)(2,1)S(1)}, u32[]{:S(2)}, u32[]{:S(2)}) %collective-permute-start.21) | collective-permute-done | bytes 589856 | tf_op jit(solution)/shard_map/ppermute | solution.py:813
  436.8 1.5 add_convert_fusion.1
  438.3 1.2 collective-permute-start.22
  440.0 9.5 %collective-permute-done.12 = bf16[12,32,768]{2,1,0:T(8,128)(2,1)S(1)} collective-permute-done((bf16[12,32,768]{2,1,0:T(8,128)(2,1)S(1)}, bf16[12,32,768]{2,1,0:T(8,128)(2,1)S(1)}, u32[]{:S(2)}, u32[]{:S(2)}) %collective-permute-start.12) | collective-permute-done | bytes 589856 | tf_op jit(solution)/shard_map/ppermute | solution.py:813
  449.5 1.6 add_convert_fusion.5.refs_0_
  451.1 6.7 %collective-permute-start.13 = (bf16[12,32,768]{2,1,0:T(8,128)(2,1)S(1)}, bf16[12,32,768]{2,1,0:T(8,128)(2,1)S(1)}, u32[]{:S(2)}, u32[]{:S(2)}) collective-permute-start(bf16[12,32,768]{2,1,0:T(8,128)(2,1)S(1)} %add_convert_fusion.5.refs_0_), channel_id=1, source_target_pairs={{0,1},{1,0},{2,3},{3,2},{4,5},{5,4},{6,7},{7,6},{8,9},{9,8},{10,11... | collective-permute-start | bytes 1769480 | tf_op jit(solution)/shard_map/ppermute | solution.py:806
  457.8 4.3 collective-permute-done.22
  462.1 1.6 add_convert_fusion.refs_2_
  463.7 3.6 collective-permute-start.23
  469.8 1.4 conditional.3
  469.8 1.4 broadcast.203
  472.3 10.9 %adam.1 = (f32[31,32,768]{2,1,0:T(8,128)}, f32[31,32,768]{2,1,0:T(8,128)}, f32[31,32,768]{2,1,0:T(8,128)}, bf16[31,32,768]{2,1,0:T(8,128)(2,1)}) custom-call(s32[31]{0:T(128)} %get-tuple-element.203.code_ref, s32[31]{0:T(128)} %get-tuple-element.169.index_ref, s32[31]{0:T(128)} %get-tuple-element.202.row_ref, f32[31,32,768]{2,1,0:T(8,128)} %bitcast.43, ...), custom_call_target="tpu_custom_call" | custom-call | bytes 22855680 | tf_op jit(solution)/shard_map/adam/pallas_call | solution.py:782
  (126 shorter events, 26.1 us)
Async XLA Ops:
  7.2 120.4 %all-gather.5.cloned.1.call-start = ((), (), s32[]{:S(2)}) async-start(), calls=%async_computation.5 | async-start | bytes 22560768 | tf_op jit(solution)/shard_map/all_gather | solution.py:894
  10.4 1.7 copy-start.22
  10.5 1.8 copy-start.8
  12.5 65.1 %copy-start.6 = (s32[288]{0:T(512)}, s32[288]{0:T(512)S(1)}, u32[]{:S(2)}) copy-start(s32[288]{0:T(512)S(1)} %convert_reduce_fusion.2) | copy-start | bytes 3460
  13.0 64.6 %copy-start.4 = (s32[432]{0:T(512)}, s32[432]{0:T(512)S(1)}, u32[]{:S(2)}) copy-start(s32[432]{0:T(512)S(1)} %convert_reduce_fusion) | copy-start | bytes 5188
  13.6 64.0 %copy-start.15 = (pred[288]{0:T(512)(128)(4,1)}, pred[288]{0:T(512)(128)(4,1)S(1)}, u32[]{:S(2)}) copy-start(pred[288]{0:T(512)(128)(4,1)S(1)} %get-tuple-element.174) | copy-start | bytes 868
  60.1 17.5 %copy-start.12 = (f32[34]{0:T(128)}, f32[34]{0:T(128)S(1)}, u32[]{:S(2)}) copy-start(f32[34]{0:T(128)S(1)} %pmax.7) | copy-start | bytes 412
  60.3 0.6 copy-start.10
  62.2 15.2 %all-to-all-start = ((f32[16,2,992]{2,1,0:T(2,128)}), f32[16,2,992]{2,1,0:T(2,128)S(1)}, u32[]{:S(2)}, u32[]{:S(2)}) async-start(f32[16,2,992]{2,1,0:T(2,128)} %copy.59), calls=%async_computation.1 | async-start | bytes 262144 | tf_op jit(solution)/shard_map/all_to_all | solution.py:918
  156.7 21.1 %collective-permute-start.1 = (bf16[512,768]{1,0:T(8,128)(2,1)}, bf16[512,768]{1,0:T(8,128)(2,1)S(1)}, u32[]{:S(2)}, u32[]{:S(2)}) collective-permute-start(bf16[512,768]{1,0:T(8,128)(2,1)} %get-tuple-element.98), channel_id=1, source_target_pairs={{0,16},{1,17},{2,18},{3,19},{4,20},{5,21},{6,22},{7,23},{8,24},{9,... | collective-permute-start | bytes 2359304 | tf_op jit(solution)/shard_map/ppermute | solution.py:935
  176.4 18.6 %collective-permute-start = (bf16[512,768]{1,0:T(8,128)(2,1)}, bf16[512,768]{1,0:T(8,128)(2,1)S(1)}, u32[]{:S(2)}, u32[]{:S(2)}) collective-permute-start(bf16[512,768]{1,0:T(8,128)(2,1)} %get-tuple-element.93), channel_id=1, source_target_pairs={{0,16},{1,17},{2,18},{3,19},{4,20},{5,21},{6,22},{7,23},{8,24},{9,... | collective-permute-start | bytes 2359304 | tf_op jit(solution)/shard_map/ppermute | solution.py:935
  177.8 0.9 copy-start.21
  193.7 43.1 %collective-permute-start.3 = (bf16[512,768]{1,0:T(8,128)(2,1)}, bf16[512,768]{1,0:T(8,128)(2,1)S(1)}, u32[]{:S(2)}, u32[]{:S(2)}) collective-permute-start(bf16[512,768]{1,0:T(8,128)(2,1)} %get-tuple-element.114), channel_id=1, source_target_pairs={{16,0},{17,1},{18,2},{19,3},{20,4},{21,5},{22,6},{23,7},{24,8},{25... | collective-permute-start | bytes 2359304 | tf_op jit(solution)/shard_map/ppermute | solution.py:941
  195.0 0.9 copy-start.20
  211.0 67.9 %collective-permute-start.2 = (bf16[512,768]{1,0:T(8,128)(2,1)}, bf16[512,768]{1,0:T(8,128)(2,1)S(1)}, u32[]{:S(2)}, u32[]{:S(2)}) collective-permute-start(bf16[512,768]{1,0:T(8,128)(2,1)} %get-tuple-element.107), channel_id=1, source_target_pairs={{16,0},{17,1},{18,2},{19,3},{20,4},{21,5},{22,6},{23,7},{24,8},{25... | collective-permute-start | bytes 2359304 | tf_op jit(solution)/shard_map/ppermute | solution.py:941
  236.8 0.9 copy-start.19
  278.8 0.9 copy-start.18
  307.6 26.6 %all-to-all-start.1 = ((bf16[16,2,4608]{2,1,0:T(2,128)(2,1)}), bf16[16,2,4608]{2,1,0:T(2,128)(2,1)S(1)}, u32[]{:S(2)}, u32[]{:S(2)}) async-start(bf16[16,2,4608]{2,1,0:T(2,128)(2,1)} %broadcast_in_dim.101), calls=%async_computation.2 | async-start | bytes 589824 | tf_op jit(solution)/shard_map/all_to_all | solution.py:951
  334.0 14.0 %collective-permute-start.4 = (bf16[96,32,768]{2,1,0:T(8,128)(2,1)}, bf16[96,32,768]{2,1,0:T(8,128)(2,1)}, u32[]{:S(2)}, u32[]{:S(2)}) collective-permute-start(bf16[96,32,768]{2,1,0:T(8,128)(2,1)} %get-tuple-element.161), channel_id=1, source_target_pairs={{0,1},{1,0},{2,3},{3,2},{4,5},{5,4},{6,7},{7,6},{8,9},{9,8},{10,11... | collective-permute-start | bytes 14155784 | tf_op jit(solution)/shard_map/ppermute | solution.py:806
  347.6 13.7 %collective-permute-start.14 = (bf16[96,32,768]{2,1,0:T(8,128)(2,1)}, bf16[96,32,768]{2,1,0:T(8,128)(2,1)}, u32[]{:S(2)}, u32[]{:S(2)}) collective-permute-start(bf16[96,32,768]{2,1,0:T(8,128)(2,1)} %get-tuple-element.163), channel_id=1, source_target_pairs={{0,1},{1,0},{2,3},{3,2},{4,5},{5,4},{6,7},{7,6},{8,9},{9,8},{10,11... | collective-permute-start | bytes 14155784 | tf_op jit(solution)/shard_map/ppermute | solution.py:806
  349.2 8.5 %collective-permute-start.5 = (bf16[6,32,768]{2,1,0:T(8,128)(2,1)S(1)}, bf16[6,32,768]{2,1,0:T(8,128)(2,1)S(1)}, u32[]{:S(2)}, u32[]{:S(2)}) collective-permute-start(bf16[6,32,768]{2,1,0:T(8,128)(2,1)S(1)} %add_convert_fusion.21), channel_id=1, source_target_pairs={{0,4},{1,5},{4,8},{5,9},{8,12},{9,13},{12,14},{13,15},{14,10},{15,... | collective-permute-start | bytes 884744 | tf_op jit(solution)/shard_map/ppermute | solution.py:813
  359.7 7.6 %collective-permute-start.9 = (bf16[6,32,768]{2,1,0:T(8,128)(2,1)S(1)}, bf16[6,32,768]{2,1,0:T(8,128)(2,1)S(1)}, u32[]{:S(2)}, u32[]{:S(2)}) collective-permute-start(bf16[6,32,768]{2,1,0:T(8,128)(2,1)S(1)} %get-tuple-element.187), channel_id=1, source_target_pairs={{0,2},{1,3},{4,0},{5,1},{8,4},{9,5},{12,8},{13,9},{14,12},{15,13},... | collective-permute-start | bytes 884744 | tf_op jit(solution)/shard_map/ppermute | solution.py:813
  360.9 23.4 %collective-permute-start.6 = (bf16[12,32,768]{2,1,0:T(8,128)(2,1)S(1)}, bf16[12,32,768]{2,1,0:T(8,128)(2,1)S(1)}, u32[]{:S(2)}, u32[]{:S(2)}) collective-permute-start(bf16[12,32,768]{2,1,0:T(8,128)(2,1)S(1)} %pad_maximum_fusion), channel_id=1, source_target_pairs={{0,4},{1,5},{4,8},{5,9},{8,12},{9,13},{12,14},{13,15},{14,10},{15,... | collective-permute-start | bytes 1769480 | tf_op jit(solution)/shard_map/ppermute | solution.py:813
  362.4 18.2 %collective-permute-start.15 = (bf16[6,32,768]{2,1,0:T(8,128)(2,1)S(1)}, bf16[6,32,768]{2,1,0:T(8,128)(2,1)S(1)}, u32[]{:S(2)}, u32[]{:S(2)}) collective-permute-start(bf16[6,32,768]{2,1,0:T(8,128)(2,1)S(1)} %add_convert_fusion.15), channel_id=1, source_target_pairs={{0,4},{1,5},{4,8},{5,9},{8,12},{9,13},{12,14},{13,15},{14,10},{15,... | collective-permute-start | bytes 884744 | tf_op jit(solution)/shard_map/ppermute | solution.py:813
  369.3 28.6 %collective-permute-start.10 = (bf16[12,32,768]{2,1,0:T(8,128)(2,1)}, bf16[12,32,768]{2,1,0:T(8,128)(2,1)S(1)}, u32[]{:S(2)}, u32[]{:S(2)}) collective-permute-start(bf16[12,32,768]{2,1,0:T(8,128)(2,1)} %pad_maximum_fusion.1), channel_id=1, source_target_pairs={{0,2},{1,3},{4,0},{5,1},{8,4},{9,5},{12,8},{13,9},{14,12},{15,13},... | collective-permute-start | bytes 1769480 | tf_op jit(solution)/shard_map/ppermute | solution.py:813
  382.7 6.1 %collective-permute-start.19 = (bf16[6,32,768]{2,1,0:T(8,128)(2,1)S(1)}, bf16[6,32,768]{2,1,0:T(8,128)(2,1)S(1)}, u32[]{:S(2)}, u32[]{:S(2)}) collective-permute-start(bf16[6,32,768]{2,1,0:T(8,128)(2,1)S(1)} %get-tuple-element.181), channel_id=1, source_target_pairs={{0,2},{1,3},{4,0},{5,1},{8,4},{9,5},{12,8},{13,9},{14,12},{15,13},... | collective-permute-start | bytes 884744 | tf_op jit(solution)/shard_map/ppermute | solution.py:813
  383.9 12.2 %collective-permute-start.16 = (bf16[12,32,768]{2,1,0:T(8,128)(2,1)S(1)}, bf16[12,32,768]{2,1,0:T(8,128)(2,1)S(1)}, u32[]{:S(2)}, u32[]{:S(2)}) collective-permute-start(bf16[12,32,768]{2,1,0:T(8,128)(2,1)S(1)} %pad_maximum_fusion.2), channel_id=1, source_target_pairs={{0,4},{1,5},{4,8},{5,9},{8,12},{9,13},{12,14},{13,15},{14,10},{15,... | collective-permute-start | bytes 1769480 | tf_op jit(solution)/shard_map/ppermute | solution.py:813
  385.8 23.0 %collective-permute-start.7 = (bf16[12,32,768]{2,1,0:T(8,128)(2,1)S(1)}, bf16[12,32,768]{2,1,0:T(8,128)(2,1)S(1)}, u32[]{:S(2)}, u32[]{:S(2)}) collective-permute-start(bf16[12,32,768]{2,1,0:T(8,128)(2,1)S(1)} %add_convert_fusion.9), channel_id=1, source_target_pairs={{0,4},{1,5},{4,8},{5,9},{8,12},{9,13},{12,14},{13,15},{14,10},{15,... | collective-permute-start | bytes 1769480 | tf_op jit(solution)/shard_map/ppermute | solution.py:813
  390.0 8.0 %copy-start.9 = (s32[1,432]{1,0:T(1,128)S(1)}, s32[1,432]{1,0:T(1,128)}, u32[]{:S(2)}) copy-start(s32[1,432]{1,0:T(1,128)} %param.16) | copy-start | bytes 5188
  390.8 21.4 %collective-permute-start.20 = (bf16[12,32,768]{2,1,0:T(8,128)(2,1)}, bf16[12,32,768]{2,1,0:T(8,128)(2,1)S(1)}, u32[]{:S(2)}, u32[]{:S(2)}) collective-permute-start(bf16[12,32,768]{2,1,0:T(8,128)(2,1)} %pad_maximum_fusion.3), channel_id=1, source_target_pairs={{0,2},{1,3},{4,0},{5,1},{8,4},{9,5},{12,8},{13,9},{14,12},{15,13},... | collective-permute-start | bytes 1769480 | tf_op jit(solution)/shard_map/ppermute | solution.py:813
  397.6 23.8 %collective-permute-start.17 = (bf16[12,32,768]{2,1,0:T(8,128)(2,1)S(1)}, bf16[12,32,768]{2,1,0:T(8,128)(2,1)S(1)}, u32[]{:S(2)}, u32[]{:S(2)}) collective-permute-start(bf16[12,32,768]{2,1,0:T(8,128)(2,1)S(1)} %add_convert_fusion.4), channel_id=1, source_target_pairs={{0,4},{1,5},{4,8},{5,9},{8,12},{9,13},{12,14},{13,15},{14,10},{15,... | collective-permute-start | bytes 1769480 | tf_op jit(solution)/shard_map/ppermute | solution.py:813
  411.0 13.8 %copy-start.7 = (s32[288]{0:T(512)S(1)}, s32[288]{0:T(512)}, u32[]{:S(2)}) copy-start(s32[288]{0:T(512)} %copy-done.6) | copy-start | bytes 3460
  411.0 13.8 %copy-start.16 = (pred[288]{0:T(512)(128)(4,1)S(1)}, pred[288]{0:T(512)(128)(4,1)}, u32[]{:S(2)}) copy-start(pred[288]{0:T(512)(128)(4,1)} %copy-done.15) | copy-start | bytes 868
  411.0 13.8 %copy-start.17 = (pred[288]{0:T(512)(128)(4,1)S(1)}, pred[288]{0:T(512)(128)(4,1)}, u32[]{:S(2)}) copy-start(pred[288]{0:T(512)(128)(4,1)} %get-tuple-element.177) | copy-start | bytes 868
  411.0 14.5 %collective-permute-start.11 = (bf16[12,32,768]{2,1,0:T(8,128)(2,1)S(1)}, bf16[12,32,768]{2,1,0:T(8,128)(2,1)S(1)}, u32[]{:S(2)}, u32[]{:S(2)}) collective-permute-start(bf16[12,32,768]{2,1,0:T(8,128)(2,1)S(1)} %get-tuple-element.185), channel_id=1, source_target_pairs={{0,2},{1,3},{4,0},{5,1},{8,4},{9,5},{12,8},{13,9},{14,12},{15,13},... | collective-permute-start | bytes 1769480 | tf_op jit(solution)/shard_map/ppermute | solution.py:813
  423.6 13.3 %collective-permute-start.21 = (bf16[12,32,768]{2,1,0:T(8,128)(2,1)S(1)}, bf16[12,32,768]{2,1,0:T(8,128)(2,1)S(1)}, u32[]{:S(2)}, u32[]{:S(2)}) collective-permute-start(bf16[12,32,768]{2,1,0:T(8,128)(2,1)S(1)} %get-tuple-element.179), channel_id=1, source_target_pairs={{0,2},{1,3},{4,0},{5,1},{8,4},{9,5},{12,8},{13,9},{14,12},{15,13},... | collective-permute-start | bytes 1769480 | tf_op jit(solution)/shard_map/ppermute | solution.py:813
  424.8 15.1 %collective-permute-start.8 = (bf16[12,32,768]{2,1,0:T(8,128)(2,1)S(1)}, bf16[12,32,768]{2,1,0:T(8,128)(2,1)S(1)}, u32[]{:S(2)}, u32[]{:S(2)}) collective-permute-start(bf16[12,32,768]{2,1,0:T(8,128)(2,1)S(1)} %get-tuple-element.184), channel_id=1, source_target_pairs={{0,4},{1,5},{4,8},{5,9},{8,12},{9,13},{12,14},{13,15},{14,10},{15,... | collective-permute-start | bytes 1769480 | tf_op jit(solution)/shard_map/ppermute | solution.py:813
  425.2 32.6 %collective-permute-start.18 = (bf16[12,32,768]{2,1,0:T(8,128)(2,1)S(1)}, bf16[12,32,768]{2,1,0:T(8,128)(2,1)S(1)}, u32[]{:S(2)}, u32[]{:S(2)}) collective-permute-start(bf16[12,32,768]{2,1,0:T(8,128)(2,1)S(1)} %get-tuple-element.178), channel_id=1, source_target_pairs={{0,4},{1,5},{4,8},{5,9},{8,12},{9,13},{12,14},{13,15},{14,10},{15,... | collective-permute-start | bytes 1769480 | tf_op jit(solution)/shard_map/ppermute | solution.py:813
  426.9 12.6 %copy-start.5 = (s32[432]{0:T(512)S(1)}, s32[432]{0:T(512)}, u32[]{:S(2)}) copy-start(s32[432]{0:T(512)} %copy-done.4) | copy-start | bytes 5188
  427.0 12.7 %copy-start.11 = (f32[384]{0:T(512)S(1)}, f32[384]{0:T(512)}, u32[]{:S(2)}) copy-start(f32[384]{0:T(512)} %copy-done.10) | copy-start | bytes 4612
  427.0 12.7 %copy-start.13 = (f32[34]{0:T(128)S(1)}, f32[34]{0:T(128)}, u32[]{:S(2)}) copy-start(f32[34]{0:T(128)} %copy-done.12) | copy-start | bytes 412
  427.0 22.5 %collective-permute-start.12 = (bf16[12,32,768]{2,1,0:T(8,128)(2,1)S(1)}, bf16[12,32,768]{2,1,0:T(8,128)(2,1)S(1)}, u32[]{:S(2)}, u32[]{:S(2)}) collective-permute-start(bf16[12,32,768]{2,1,0:T(8,128)(2,1)S(1)} %add_convert_fusion.6), channel_id=1, source_target_pairs={{0,2},{1,3},{4,0},{5,1},{8,4},{9,5},{12,8},{13,9},{14,12},{15,13},... | collective-permute-start | bytes 1769480 | tf_op jit(solution)/shard_map/ppermute | solution.py:813
  438.3 23.8 %collective-permute-start.22 = (bf16[12,32,768]{2,1,0:T(8,128)(2,1)S(1)}, bf16[12,32,768]{2,1,0:T(8,128)(2,1)S(1)}, u32[]{:S(2)}, u32[]{:S(2)}) collective-permute-start(bf16[12,32,768]{2,1,0:T(8,128)(2,1)S(1)} %add_convert_fusion.1), channel_id=1, source_target_pairs={{0,2},{1,3},{4,0},{5,1},{8,4},{9,5},{12,8},{13,9},{14,12},{15,13},... | collective-permute-start | bytes 1769480 | tf_op jit(solution)/shard_map/ppermute | solution.py:813
  451.1 18.2 %copy-start = (bf16[12,32,768]{2,1,0:T(8,128)(2,1)}, bf16[12,32,768]{2,1,0:T(8,128)(2,1)S(1)}, u32[]{:S(2)}) copy-start(bf16[12,32,768]{2,1,0:T(8,128)(2,1)S(1)} %add_convert_fusion.5.refs_0_) | copy-start | bytes 1769476
  451.1 17.5 %copy-start.14 = (s32[288]{0:T(512)S(1)}, s32[288]{0:T(512)}, u32[]{:S(2)}) copy-start(s32[288]{0:T(512)} %get-tuple-element.198) | copy-start | bytes 3460
  451.1 20.1 %collective-permute-start.13 = (bf16[12,32,768]{2,1,0:T(8,128)(2,1)S(1)}, bf16[12,32,768]{2,1,0:T(8,128)(2,1)S(1)}, u32[]{:S(2)}, u32[]{:S(2)}) collective-permute-start(bf16[12,32,768]{2,1,0:T(8,128)(2,1)S(1)} %add_convert_fusion.5.refs_0_), channel_id=1, source_target_pairs={{0,1},{1,0},{2,3},{3,2},{4,5},{5,4},{6,7},{7,6},{8,9},{9,8},{10,11... | collective-permute-start | bytes 1769480 | tf_op jit(solution)/shard_map/ppermute | solution.py:806
  463.7 6.1 %copy-start.1 = (bf16[12,32,768]{2,1,0:T(8,128)(2,1)}, bf16[12,32,768]{2,1,0:T(8,128)(2,1)S(1)}, u32[]{:S(2)}) copy-start(bf16[12,32,768]{2,1,0:T(8,128)(2,1)S(1)} %add_convert_fusion.refs_2_) | copy-start | bytes 1769476
  463.7 7.5 %collective-permute-start.23 = (bf16[12,32,768]{2,1,0:T(8,128)(2,1)S(1)}, bf16[12,32,768]{2,1,0:T(8,128)(2,1)S(1)}, u32[]{:S(2)}, u32[]{:S(2)}) collective-permute-start(bf16[12,32,768]{2,1,0:T(8,128)(2,1)S(1)} %add_convert_fusion.refs_2_), channel_id=1, source_target_pairs={{0,1},{1,0},{2,3},{3,2},{4,5},{5,4},{6,7},{7,6},{8,9},{9,8},{10,11... | collective-permute-start | bytes 1769480 | tf_op jit(solution)/shard_map/ppermute | solution.py:806
  471.2 0.8 copy-start.2
  471.2 1.0 copy-start.3
Sparse Core Ops, SparseCore 0:
  11.8 115.7 all-gather.4

commit v4 on v3

--- a/solution.py
+++ b/solution.py
@@ -206,32 +206,43 @@
 
 
 def forward_attention(v, length):
-    v[N_LSE_COLS][...] = jnp.zeros_like(v[N_LSE_COLS])
     low_lanes = low_half()
-
-    @pl.loop(0, PAIRS, unroll=PAIRS)
-    def _(pair):
-        at = lambda n: pl.ds(pl.multiple_of(n * D + pair * 128, 128), 128)
-        q = v[N_QKV][:, at(0)] * jnp.asarray(HEAD_DIM ** (-0.5), bf16)
-        k = v[N_QKV][:, at(1)]
-        value = v[N_QKV][:, at(2)]
-        mixed = []
-        for h in range(2):
-            qh = jnp.where(low_lanes if h == 0 else ~low_lanes, q, jnp.zeros_like(q))
-            v[N_SLOPE][:, h * length : (h + 1) * length] = dot_nt(qh, k)
-        for h in range(2):
-            lane = lax.broadcasted_iota(jnp.int32, (1, 128), 1) == pair * 2 + h
-            span = slice(h * length, (h + 1) * length)
-            for block in blocks_of(length):
-                s = v[N_SLOPE][block, span]
-                top = jnp.max(s, axis=-1, keepdims=True)
-                e = jnp.exp(s - top)
-                total = jnp.sum(e, axis=-1, keepdims=True)
-                v[N_Z][block, span] = (e * (1.0 / total)).astype(bf16)
-                v[N_LSE_COLS][block, :] = jnp.where(lane, top + jnp.log(total), v[N_LSE_COLS][block, :])
-            mixed.append(dot_nn(v[N_Z][:, span], value))
-        v[N_O][:, at(0)] = jnp.where(low_lanes, mixed[0], mixed[1]).astype(bf16)
-
+    room = FF // length
+    columns = lax.broadcasted_iota(jnp.int32, (1, 128), 1)
+
+    def scores(head):
+        at = slice(head // 2 * 128, head // 2 * 128 + 128)
+        q = v[N_QKV][:, at] * jnp.asarray(HEAD_DIM ** (-0.5), bf16)
+        qh = jnp.where(low_lanes if head % 2 == 0 else ~low_lanes, q, jnp.zeros_like(q))
+        first = head % room * length
+        v[N_SLOPE][:, first : first + length] = dot_nt(qh, v[N_QKV][:, D + at.start : D + at.stop])
+
+    def softmax(head):
+        span = slice(head % room * length, head % room * length + length)
+        for block in blocks_of(length):
+            s = v[N_SLOPE][block, span]
+            top = jnp.max(s, axis=-1, keepdims=True)
+            e = jnp.exp(s - top)
+            total = jnp.sum(e, axis=-1, keepdims=True)
+            v[N_Z][block, span] = (e * (1.0 / total)).astype(bf16)
+            line = top + jnp.log(total)
+            v[N_LSE_COLS][block, :] = jnp.where(columns == head, line, v[N_LSE_COLS][block, :]) if head else jnp.where(columns == 0, line, 0.0)
+
+    def mix(head):
+        at = slice(2 * D + head // 2 * 128, 2 * D + head // 2 * 128 + 128)
+        span = slice(head % room * length, head % room * length + length)
+        return dot_nn(v[N_Z][:, span], v[N_QKV][:, at])
+
+    scores(0)
+    mixed = [None] * HEADS
+    for head in range(HEADS):
+        if head + 1 < HEADS:
+            scores(head + 1)
+        softmax(head)
+        mixed[head] = mix(head)
+        if head % 2:
+            at = slice(head // 2 * 128, head // 2 * 128 + 128)
+            v[N_O][:, at] = jnp.where(low_lanes, mixed[head - 1], mixed[head]).astype(bf16)
     v[N_LSE][...] = v[N_LSE_COLS][...].T[:16, :]
 
 
@@ -314,34 +325,39 @@
     low_lanes = low_half()
     scale = HEAD_DIM ** (-0.5)
 
-    @pl.loop(0, PAIRS, unroll=PAIRS)
-    def _(pair):
-        at = lambda n: pl.ds(pl.multiple_of(n * D + pair * 128, 128), 128)
-        q = v[N_QKV][:, at(0)]
-        k = v[N_QKV][:, at(1)]
-        value = v[N_QKV][:, at(2)]
-        dop = v[N_DO][:, at(0)]
-        zero = jnp.zeros_like(q)
-        dq = dk = dv = None
-        for h in range(2):
-            lanes = low_lanes if h == 0 else ~low_lanes
-            qh = jnp.where(lanes, q, zero)
-            kh = jnp.where(lanes, k, zero)
-            doh = jnp.where(lanes, dop, zero)
-            st = dot_nt(k, qh * jnp.asarray(scale, bf16))
-            pt = jnp.exp(st - v[N_LSE][pl.ds(pair * 2 + h, 1), :])
-            dpt = dot_nt(value, doh)
-            dv_part = dot_nn(pt.astype(bf16), doh)
-            inner = jnp.sum(dpt * pt, axis=0, keepdims=True)
-            drt = (pt * (dpt - inner) * scale).astype(bf16)
-            dk_part = dot_nn(drt, qh)
-            dq_part = dot_tn(drt, kh)
-            dq = dq_part if h == 0 else dq + dq_part
-            dk = dk_part if h == 0 else dk + dk_part
-            dv = dv_part if h == 0 else dv + dv_part
-        v[N_DQKV][:, at(0)] = dq.astype(bf16)
-        v[N_DQKV][:, at(1)] = dk.astype(bf16)
-        v[N_DQKV][:, at(2)] = dv.astype(bf16)
+    def parts(head):
+        at = head // 2 * 128
+        keep = lambda a: jnp.where(low_lanes if head % 2 == 0 else ~low_lanes, a, jnp.zeros_like(a))
+        qh, doh = keep(v[N_QKV][:, at : at + 128]), keep(v[N_DO][:, at : at + 128])
+        kh = keep(v[N_QKV][:, D + at : D + at + 128])
+        return qh, kh, doh
+
+    def first(head):
+        at = head // 2 * 128
+        qh, kh, doh = parts(head)
+        st = dot_nt(v[N_QKV][:, D + at : D + at + 128], qh * jnp.asarray(scale, bf16))
+        dpt = dot_nt(v[N_QKV][:, 2 * D + at : 2 * D + at + 128], doh)
+        return st, dpt, qh, kh, doh
+
+    def rest(head, st, dpt, qh, kh, doh):
+        pt = jnp.exp(st - v[N_LSE][head : head + 1, :])
+        dv = dot_nn(pt.astype(bf16), doh)
+        inner = jnp.sum(dpt * pt, axis=0, keepdims=True)
+        drt = (pt * (dpt - inner) * scale).astype(bf16)
+        return dot_tn(drt, kh), dot_nn(drt, qh), dv
+
+    ahead = first(0)
+    made = None
+    for head in range(HEADS):
+        now = ahead
+        if head + 1 < HEADS:
+            ahead = first(head + 1)
+        made_now = rest(head, *now)
+        if head % 2:
+            for n in range(3):
+                at = n * D + head // 2 * 128
+                v[N_DQKV][:, at : at + 128] = (made[n] + made_now[n]).astype(bf16)
+        made = made_now
 
 
 def back_input(v, w_qkv, row, length):
@@ -695,107 +711,98 @@
     )(*operands[:2], *in_hbm(operands[2:]))
 
 
-GROUP = 8
-
-
-def adam_kernel(n_sums, code_ref, index_ref, row_ref, master, first, second, dmod, cond, *refs):
+def adam_kernel(low, high, n_sums, chained, code_ref, index_ref, row_ref, master, first, second, dmod, cond, *refs):
     sums = refs[:n_sums]
-    outs = refs[n_sums : n_sums + 4]
-    scratch = refs[n_sums + 4 :]
-    held = scratch[:3]
-    made = scratch[3:7]
-    grad_v, in_sem, grad_sem, out_sem = scratch[7:]
+    refs = refs[n_sums + (4 if chained else 0) :]
+    outs, held, made = refs[:4], refs[4:7], refs[7:11]
+    grad_v, in_sem, grad_sem, out_sem = refs[11:]
     slots, rows = master.shape[0], master.shape[1]
-    groups = [(g, min(GROUP, slots - g)) for g in range(0, slots, GROUP)]
-    get = [
-        [start(a.at[pl.ds(g, size)], h.at[pl.ds(g, size)], in_sem.at[n, i]) for i, (a, h) in enumerate(zip((master, first, second), held))]
-        for n, (g, size) in enumerate(groups)
-    ]
-    for n, (g, size) in enumerate(groups):
-
-        @pl.loop(g, g + size)
+    sources = (master, first, second)
+
+    def each(step):
+        @pl.loop(0, slots)
         def _(slot):
             code = code_ref[slot]
-            where = index_ref[slot]
-            for n_sum in range(n_sums):
-
-                @pl.when(code == n_sum)
-                def _():
-                    pltpu.make_async_copy(sums[n_sum].at[where], grad_v.at[slot], grad_sem.at[n]).start()
-
-    put = []
-    for n, (g, size) in enumerate(groups):
-        for copy in get[n]:
-            copy.wait()
-        span = pl.ds(g, size)
-
-        @pl.loop(g, g + size)
-        def _(slot):
-            code = code_ref[slot]
-
-            @pl.when(code < n_sums)
+
+            @pl.when((code >= low) & (code < high))
             def _():
-                pltpu.make_async_copy(sums[0].at[0], grad_v.at[slot], grad_sem.at[n]).wait()
-
-        @pl.loop(g, g + size)
-        def _(slot):
-            code = code_ref[slot]
-
-            def update(grad):
-                first_next = beta_one * held[1][slot] + (1.0 - beta_one) * grad
-                second_next = beta_two * held[2][slot] + (1.0 - beta_two) * grad * grad
-                first_hat = first_next / (1.0 - beta_one**STEP)
-                second_hat = second_next / (1.0 - beta_two**STEP)
-                value = held[0][slot] - learn_rate * (
-                    first_hat / (jnp.sqrt(second_hat) + adam_eps) + decay_rate * held[0][slot]
-                )
-                made[0][slot] = value
-                made[1][slot] = first_next
-                made[2][slot] = second_next
-                made[3][slot] = value.astype(bf16)
-
-            @pl.when(code < n_sums)
+                step(slot, code)
+
+    def fetch(slot, code):
+        for source, target in zip(sources, held):
+            pltpu.make_async_copy(source.at[slot], target.at[slot], in_sem.at[slot]).start()
+        for n in range(max(low, 2), min(high, n_sums + 2)):
+
+            @pl.when(code == n)
             def _():
+                pltpu.make_async_copy(sums[n - 2].at[index_ref[slot]], grad_v.at[slot], grad_sem.at[slot]).start()
+
+    def work(slot, code):
+        for source, target in zip(sources, held):
+            pltpu.make_async_copy(source.at[slot], target.at[slot], in_sem.at[slot]).wait()
+
+        def update(grad):
+            first_next = beta_one * held[1][slot] + (1.0 - beta_one) * grad
+            second_next = beta_two * held[2][slot] + (1.0 - beta_two) * grad * grad
+            first_hat = first_next / (1.0 - beta_one**STEP)
+            second_hat = second_next / (1.0 - beta_two**STEP)
+            value = held[0][slot] - learn_rate * (
+                first_hat / (jnp.sqrt(second_hat) + adam_eps) + decay_rate * held[0][slot]
+            )
+            made[0][slot] = value
+            made[1][slot] = first_next
+            made[2][slot] = second_next
+            made[3][slot] = value.astype(bf16)
+
+        if high > 2:
+
+            @pl.when(code >= 2)
+            def _():
+                pltpu.make_async_copy(sums[0].at[0], grad_v.at[slot], grad_sem.at[slot]).wait()
                 update(grad_v[slot].astype(f32))
 
-            @pl.when(code == n_sums)
+        if low < 2:
+
+            @pl.when(code == 1)
             def _():
                 at = pl.multiple_of(row_ref[slot], rows)
                 update(dot_nn(dmod[pl.ds(at, rows), :], cond[...]))
 
-            @pl.when(code > n_sums)
+            @pl.when(code == 0)
             def _():
                 update(jnp.zeros((rows, D), f32))
 
-        for i in range(4):
-            put.append(start(made[i].at[span], outs[i].at[span], out_sem.at[n, i]))
-    for copy in put:
-        copy.wait()
-
-
-def adam(code, index, row, master, first, second, dmod, cond, sums):
+        for source, target in zip(made, outs):
+            pltpu.make_async_copy(source.at[slot], target.at[slot], out_sem.at[slot]).start()
+
+    def close(slot, code):
+        for source, target in zip(made, outs):
+            pltpu.make_async_copy(source.at[slot], target.at[slot], out_sem.at[slot]).wait()
+
+    each(fetch)
+    each(work)
+    each(close)
+
+
+def adam(low, high, code, index, row, master, first, second, dmod, cond, sums, chain):
     slots, rows = master.shape[0], master.shape[1]
     any_spec = pl.BlockSpec(memory_space=pltpu.HBM)
     smem, vmem = pl.BlockSpec(memory_space=pltpu.SMEM), pl.BlockSpec(memory_space=pltpu.VMEM)
     kinds = [f32, f32, f32, bf16]
-    groups = -(-slots // GROUP)
     return pl.pallas_call(
-        functools.partial(adam_kernel, len(sums)),
-        in_specs=[smem] * 3 + [any_spec] * 3 + [vmem] * 2 + [any_spec] * len(sums),
+        functools.partial(adam_kernel, low, high, len(sums), bool(chain)),
+        in_specs=[smem] * 3 + [any_spec] * 3 + [vmem] * 2 + [any_spec] * (len(sums) + len(chain)),
         out_specs=[any_spec] * 4,
         out_shape=[pltpu.HBM(master.shape, kind) for kind in kinds],
         scratch_shapes=[pltpu.VMEM(master.shape, f32)] * 3
         + [pltpu.VMEM(master.shape, kind) for kind in kinds]
-        + [
-            pltpu.VMEM(master.shape, bf16),
-            pltpu.SemaphoreType.DMA((groups, 3)),
-            pltpu.SemaphoreType.DMA((groups,)),
-            pltpu.SemaphoreType.DMA((groups, 4)),
-        ],
+        + [pltpu.VMEM(master.shape, bf16)]
+        + [pltpu.SemaphoreType.DMA((slots,))] * 3,
+        input_output_aliases={8 + len(sums) + n: n for n in range(len(chain))},
         compiler_params=pltpu.CompilerParams(vmem_limit_bytes=VMEM_ALL),
-        cost_estimate=pl.CostEstimate(flops=0, bytes_accessed=slots * rows * D * 30, transcendentals=0),
-        name="adam",
-    )(code, index, row, *in_hbm((master, first, second)), dmod, cond, *in_hbm(sums))
+        cost_estimate=pl.CostEstimate(flops=0, bytes_accessed=slots * rows * D * 15, transcendentals=0),
+        name=f"adam_{low}",
+    )(code, index, row, *in_hbm((master, first, second)), dmod, cond, *in_hbm(list(sums) + list(chain)))
 
 
 CHIPS = 8
@@ -813,32 +820,76 @@
     return lax.ppermute(value, BATCH, pairs)
 
 
+def hop_kernel(spans, adds, others, spot_ref, *refs):
+    n_in = 2 + len(adds)
+    terms, came, refs = refs[:2], refs[2:n_in], refs[n_in + others :]
+    outs = refs[: len(spans)]
+    held, sem, out_sem = refs[len(spans) : -2], refs[-2], refs[-1]
+    get, at = [], 0
+    parts = []
+    for n, (low, high) in enumerate(spans):
+        rows = []
+        for source in terms:
+            span = pl.ds(spot_ref[n] + low, high - low)
+            get.append(start(source.at[span], held[at], sem.at[at]))
+            rows.append(at)
+            at += 1
+        parts.append(rows)
+    for n, source in enumerate(came):
+        get.append(start(source, held[at], sem.at[at]))
+        at += 1
+    for copy in get:
+        copy.wait()
+    put = []
+    for n, (low, high) in enumerate(spans):
+        made = held[at + n]
+        for r in range(high - low):
+            total = held[parts[n][0]][r].astype(f32) + held[parts[n][1]][r].astype(f32)
+            for m, (target, first, last, skip) in enumerate(adds):
+                if target == n and first <= r + low < last:
+                    total = total + held[2 * len(spans) + m][r + low - skip].astype(f32)
+            made[r] = total.astype(bf16)
+        put.append(start(made, outs[n], out_sem.at[n]))
+    for copy in put:
+        copy.wait()
+
+
+def hop_sums(spots, terms, spans, adds, came, after):
+    rows, width = terms[0].shape[1:]
+    shapes = [(high - low, rows, width) for low, high in spans]
+    scratch = [pltpu.VMEM(shape, bf16) for shape in shapes for _ in range(2)]
+    scratch += [pltpu.VMEM(array.shape, bf16) for array in came] + [pltpu.VMEM(shape, bf16) for shape in shapes]
+    return pl.pallas_call(
+        functools.partial(hop_kernel, spans, adds, len(after)),
+        in_specs=[pl.BlockSpec(memory_space=pltpu.SMEM)]
+        + [pl.BlockSpec(memory_space=pltpu.HBM)] * 2
+        + [pl.BlockSpec(memory_space=pl.ANY)] * (len(came) + len(after)),
+        out_specs=[pl.BlockSpec(memory_space=pltpu.HBM)] * len(spans),
+        out_shape=[pltpu.HBM(shape, bf16) for shape in shapes],
+        scratch_shapes=scratch + [pltpu.SemaphoreType.DMA((8,)), pltpu.SemaphoreType.DMA((2,))],
+        compiler_params=pltpu.CompilerParams(vmem_limit_bytes=VMEM_ALL),
+        cost_estimate=pl.CostEstimate(flops=0, bytes_accessed=8 * shapes[0][0] * rows * width * 2, transcendentals=0),
+        name="hop",
+    )(spots, *in_hbm(terms), *came, *after)
+
+
 class Ring:
     def __init__(self, place, mine, other):
         self.place, self.size, self.left = place, mine.shape[0] // CHIPS, 4
         self.half = self.size // 2
         self.terms = (mine, swap_cores(other))
 
-    def term(self, offset, low, high):
-        first = ((self.place + offset) % CHIPS) * self.size + low
-        return sum(lax.dynamic_slice_in_dim(a, first, high - low, 0).astype(f32) for a in self.terms)
-
-    def hop(self):
+    def hop(self, after=()):
         n, half, size = self.left, self.half, self.size
+        spots = jnp.stack([(self.place + n) % CHIPS, (self.place - n) % CHIPS]) * size
         if n == 4:
-            ahead, behind = self.term(4, 0, half), self.term(-4, half, size)
-        elif n == 3:
-            ahead = jnp.concatenate([self.term(3, 0, half) + self.ahead.astype(f32), self.term(3, half, size)])
-            behind = jnp.concatenate([self.term(-3, 0, half), self.term(-3, half, size) + self.behind.astype(f32)])
+            spans, adds, came = [(0, half), (half, size)], [], []
         else:
-            ahead = self.term(n, 0, size) + self.ahead.astype(f32)
-            behind = self.term(-n, 0, size) + self.behind.astype(f32)
-        self.payload = [ahead.astype(bf16), behind.astype(bf16)]
+            spans, came = [(0, size)] * 2, [self.ahead, self.behind]
+            adds = [(0, 0, half, 0), (1, half, size, half)] if n == 3 else [(0, 0, size, 0), (1, 0, size, 0)]
+        ahead, behind = hop_sums(spots.astype(jnp.int32), self.terms, spans, adds, came, after)
+        self.ahead, self.behind = along(ahead, 1), along(behind, -1)
         self.left -= 1
-        self.send()
-
-    def send(self):
-        self.ahead, self.behind = along(self.payload[0], 1), along(self.payload[1], -1)
 
     def held(self, count=2):
         self.count = count
@@ -848,10 +899,10 @@
         self.terms = tuple(made[-self.count :]) + self.terms[self.count :]
         return made[: -self.count]
 
-    def finish(self):
-        while self.left:
-            self.hop()
-        return (self.term(0, 0, self.size) + self.ahead.astype(f32) + self.behind.astype(f32)).astype(bf16)
+    def finish(self, after=()):
+        spots = jnp.reshape(self.place * self.size, (1,)).astype(jnp.int32)
+        adds = [(0, 0, self.size, 0)] * 2
+        return hop_sums(spots, self.terms, [(0, self.size)], adds, [self.ahead, self.behind], after)[0]
 
 
 def time_features(steps_in):
@@ -871,7 +922,7 @@
     owner = owners[0]
     panels = owner.shape[0]
     moved = DOWN_END // panel_rows
-    cap = min(slots, max(4, (slots * 27 + 30) // 31))
+    cap = min(slots, max(4, (slots * 25 + 30) // 31))
     section = jnp.reshape(section_index, (1,)).astype(jnp.int32)
 
     number = jnp.arange(panels, dtype=jnp.int32)
@@ -948,8 +999,14 @@
 
     dmod = [jnp.concatenate([e[N_DMOD_ATT], e[N_DMOD_FFN]]) for e in every]
     dmod = jnp.stack(dmod).reshape(1, clips, 6 * D).astype(bf16)
-    dmod = lax.all_to_all(jnp.broadcast_to(dmod, (owner_total, clips, 6 * D)), BATCH, split_axis=0, concat_axis=0, tiled=True)
-    dmod = dmod.reshape(clip_total, 6 * D).T
+    dmod = lax.all_to_all(
+        jnp.broadcast_to(dmod, (owner_total, clips, 6 * D)), BATCH, split_axis=0, concat_axis=0, tiled=True
+    )
+    slot_code = jnp.where(kind == 1, slot_code + 2, jnp.where(kind == 2, 1, 0)).astype(jnp.int32)
+    update = run(
+        adam, code=slot_code, index=slot_index, row=grad_row, master=master[0], first=first_moment[0],
+        second=second_moment[0], dmod=dmod.reshape(clip_total, 6 * D).T, cond=cond,
+    )
     grads = run(weight_grads, code=code, index=index, every=every, length=length, panel_rows=panel_rows)
     if rings:
         place = me // 4 + (me // 2) % 2 * (CHIPS - 1 - 2 * (me // 4))
@@ -957,29 +1014,29 @@
         first_jobs = ((N_DA, N_O, QKV_END), (N_DQKV, N_H1, 0), (N_DU, N_H2, PROJ_END))
         made = grads(first_jobs, sizes=[sizes[0]] * 2 + wide, thread=[], after=[])
         first = Ring(place, *made[:2])
-        made = grads(((N_Z, N_DB, UP_END),), sizes=wide, thread=made[2:], after=[dmod], through=first.held(1))
+        made = grads(((N_Z, N_DB, UP_END),), sizes=wide, thread=made[2:], after=[], through=first.held(1))
         made = first.later(made)
         second = Ring(place, *made[:2])
-        sums = []
-        for ring in (first, second):
-            half = ring.finish()
-            sums += [half, swap_cores(half)]
-        sums.append(
-            lax.cond(
-                beyond,
-                lambda part: lax.psum_scatter(part, BATCH, scatter_dimension=0, tiled=True),
-                lambda part: jnp.zeros((slots, panel_rows, D), bf16),
-                made[2],
-            )
+        rest = lax.cond(
+            beyond,
+            lambda part: lax.psum_scatter(part, BATCH, scatter_dimension=0, tiled=True),
+            lambda part: jnp.zeros((slots, panel_rows, D), bf16),
+            made[2],
         )
+        for n in range(4):
+            first.hop(after=[[], [rest], [dmod], []][n])
+            second.hop()
+        half = first.finish()
+        sums = [half, swap_cores(half)]
+        results = update(0, 4, sums=sums, chain=[])
+        half = second.finish(after=results[3:])
+        sums += [half, swap_cores(half), rest]
+        results = update(4, 7, sums=sums, chain=results)
     else:
         jobs = ((N_Z, N_DB, UP_END), (N_DU, N_H2, PROJ_END), (N_DA, N_O, QKV_END), (N_DQKV, N_H1, 0))
         (made,) = grads(jobs, sizes=[sizes[0]], thread=[], after=[])
         sums = [lax.psum_scatter(made, BATCH, scatter_dimension=0, tiled=True)]
-    slot_code = jnp.where(kind == 1, slot_code, jnp.where(kind == 2, len(sums), len(sums) + 1))
-    results = adam(
-        slot_code, slot_index, grad_row, master[0], first_moment[0], second_moment[0], dmod, cond, sums
-    )
+        results = update(0, 3, sums=sums, chain=[])
     return (outs[None], gin[None], *(r[None] for r in results))
 
 

time: 495 us -> 481 us (0.972)
  Pallas kernels: 167 us -> 204 us
  waiting for transfers between devices: 165 us -> 131 us
  other arithmetic: 37 us -> 13 us
  local copies, waits for them, and re-layouts: 16.5 us -> 25.9 us
    pallas_call x1 -> x12, Pallas kernels: 10.9 us -> 47.9 us  [the longest x10 34.7 us: hop_sums(): pl.pallas_call(functools.partial(hop_kernel, spans, adds, len(after)), in...]
    ppermute x16, waiting for transfers between devices: 70.2 us -> 39.1 us  [along(): return lax.ppermute(value, BATCH, pairs)]
    convert_element_type x10 -> x0, other arithmetic: 15.6 us -> none  [the longest x8 12.5 us: hop(): self.payload = [ahead.astype(bf16), behind.astype(bf16)]]
    another operation x8 -> x4, other arithmetic: 9.15 us -> 0.02 us
    unnamed x48 -> x88, local copies, waits for them, and re-layouts: 5.01 us -> 13.9 us
    all_gather x1, waiting for transfers between devices: 48.4 us -> 41.1 us  [body(): gathered = lax.all_gather(low[:cap], BATCH, axis=0, tiled=True)]
  transfers between devices with their start and end apart: 27 -> 27, of which waited for: 14 -> 16; matrix products, arithmetic and copies ran while one was open for 8% -> 4% of each run, Pallas kernels for 22% -> 26%
where the time goes in v4:
time: 481 us; the launch traced here: 477 us
  Pallas kernels  204 us (42%)
  waiting for transfers between devices  131 us (27%)
  blocking collectives  42.5 us (9%)
  starting transfers between devices  40.9 us (9%)
  local copies, waits for them, and re-layouts  25.9 us (5%)
  between operations  18.2 us (4%)
  other arithmetic  13 us (3%)
    pallas_call x6, Pallas kernels, call_block(): pl.pallas_call(run, out_shape=[pltpu.HBM(*write[n]) for n in w_names], in...  118 us
    pmax x1, blocking collectives, body(): news = lax.pmax(jnp.concatenate(news), (SECTION, BATCH))  42.5 us
    all_gather x1, waiting for transfers between devices, body(): gathered = lax.all_gather(low[:cap], BATCH, axis=0, tiled=True)  41.1 us
    ppermute x2, waiting for transfers between devices, body(): received = [lax.ppermute(f[N_SENT], SECTION, [(1, 0)]) for f in seconds]  40.9 us
    ppermute x16, waiting for transfers between devices, along(): return lax.ppermute(value, BATCH, pairs)  39.1 us
    pallas_call x10, Pallas kernels, hop_sums(): pl.pallas_call(functools.partial(hop_kernel, spans, adds, len(after)), in...  34.7 us
    pallas_call x2, Pallas kernels, weight_grads(): pl.pallas_call(functools.partial(grads_kernel, jobs, clips, length, panel...  32.4 us
    ppermute x16, starting transfers between devices, along(): return lax.ppermute(value, BATCH, pairs)  14.4 us
  transfers between devices with their start and end apart: 27, of which 16 were waited for; matrix products, arithmetic and copies ran while one was open for 4% of the time, Pallas kernels for 26%

profile of v4, /device:TPU:1, one launch (start us, length us, event | category | flops | bytes accessed | tf_op | source)
XLA Modules:
  0.0 476.7 jit_solution(4708866626328070866)
XLA Ops:
  7.2 3.2 fusion.28
  10.5 1.1 slice.61
  14.2 1.2 multiply_add_fusion
  17.6 42.5 %pmax.7 = f32[34]{0:T(128)S(1)} all-reduce(f32[34]{0:T(128)S(1)} %pad_maximum_fusion.3), channel_id=1, replica_groups=mesh['section'=2,'batch'=16] {'section','batch'}, use_global_device_ids=true, to_apply=%region_5.6 | all-reduce | flops 34 | bytes 272 | tf_op jit(solution)/shard_map/pmax | solution.py:950
  62.1 5.9 %all-to-all-start = ((f32[16,2,992]{2,1,0:T(2,128)}), f32[16,2,992]{2,1,0:T(2,128)S(1)}, u32[]{:S(2)}, u32[]{:S(2)}) async-start(f32[16,2,992]{2,1,0:T(2,128)} %copy.63), calls=%async_computation.1 | async-start | bytes 262144 | tf_op jit(solution)/shard_map/all_to_all | solution.py:969
  69.3 8.0 %all-to-all-done = f32[16,2,992]{2,1,0:T(2,128)S(1)} async-done(((f32[16,2,992]{2,1,0:T(2,128)}), f32[16,2,992]{2,1,0:T(2,128)S(1)}, u32[]{:S(2)}, u32[]{:S(2)}) %all-to-all-start) | async-done | bytes 127008 | tf_op jit(solution)/shard_map/all_to_all | solution.py:969
  79.0 41.1 %all-gather.5.cloned.1.call-done.refs_0_ = bf16[400,32,768]{2,1,0:T(8,128)(2,1)} async-done(((bf16[25,32,768]{2,1,0:T(8,128)(2,1)}), bf16[400,32,768]{2,1,0:T(8,128)(2,1)}) %all-gather.5.cloned.1.call-update) | async-done | bytes 19660816 | tf_op jit(solution)/shard_map/all_gather | solution.py:945
  120.1 1.2 slice.63
  122.6 2.8 conditional.2
  122.6 2.7 broadcast.203
  125.4 5.8 %assemble.1.refs_1_.refs_2_ = bf16[9216,768]{1,0:T(8,128)(2,1)S(1)} custom-call(s32[288]{0:T(512)} %bitcast.70, bf16[400,32,768]{2,1,0:T(8,128)(2,1)} %all-gather.5.cloned.1.call-done.refs_0_, bf16[96,32,768]{2,1,0:T(8,128)(2,1)} %get-tuple-element.232.refs_1_), custom_call_target="tpu_custom_call" | custom-call | bytes 14155776 | tf_op jit(solution)/shard_map/assemble/pallas_call | solution.py:109
  131.2 18.1 %first_forward_0.1 = (bf16[512,768]{1,0:T(8,128)(2,1)}, bf16[512,2304]{1,0:T(8,128)(2,1)}, f32[16,512]{1,0:T(8,128)}, bf16[512,768]{1,0:T(8,128)(2,1)}, bf16[512...) custom-call(s32[1]{0:T(128)} %bitcast.refs_0_, ...), custom_call_target="tpu_custom_call" | custom-call | flops 16999999488 | bytes 31457280 | tf_op jit(solution)/shard_map/first_forward_0/pallas_call | solution.py:432
  149.3 1.3 collective-permute-start.1
  150.6 17.7 %first_forward_1.1 = (bf16[512,768]{1,0:T(8,128)(2,1)}, bf16[512,2304]{1,0:T(8,128)(2,1)}, f32[16,512]{1,0:T(8,128)}, bf16[512,768]{1,0:T(8,128)(2,1)}, bf16[512...) custom-call(s32[1]{0:T(128)} %bitcast.refs_0_, ...), custom_call_target="tpu_custom_call", output_to_operand_aliasing={{10}: (4, {})} | custom-call | flops 16999999488 | bytes 31457280 | tf_op jit(solution)/shard_map/first_forward_1/pallas_call | solution.py:432
  168.3 1.3 collective-permute-start
  170.6 15.0 %second_both_0.1 = (bf16[512,768]{1,0:T(8,128)(2,1)}, bf16[512,768]{1,0:T(8,128)(2,1)}, bf16[512,768]{1,0:T(8,128)(2,1)}, bf16[512,3072]{1,0:T(8,128)(2,1)}, bf1...) custom-call(s32[1]{0:T(128)} %bitcast.refs_0_, ...), custom_call_target="tpu_custom_call", output_to_operand_aliasing={{0}: (6, {}), {1}: (7, {}), {2}: (8, {}), {3}: (9, {}), {10... | custom-call | flops 40000000000 | bytes 41943040 | tf_op jit(solution)/shard_map/second_both_0/pallas_call | solution.py:432
  185.6 1.3 collective-permute-start.3
  187.0 0.9 copy-done.40
  187.9 15.0 %second_both_1.1 = (bf16[512,768]{1,0:T(8,128)(2,1)}, bf16[512,768]{1,0:T(8,128)(2,1)}, bf16[512,768]{1,0:T(8,128)(2,1)}, bf16[512,3072]{1,0:T(8,128)(2,1)}, bf1...) custom-call(s32[1]{0:T(128)} %bitcast.refs_0_, ...), custom_call_target="tpu_custom_call", output_to_operand_aliasing={{0}: (6, {}), {1}: (7, {}), {2}: (8, {}), {3}: (9, {}), {10... | custom-call | flops 40000000000 | bytes 41943040 | tf_op jit(solution)/shard_map/second_both_1/pallas_call | solution.py:432
  202.9 1.3 collective-permute-start.2
  204.2 25.3 %collective-permute-done.3.refs_4_ = bf16[512,768]{1,0:T(8,128)(2,1)S(1)} collective-permute-done((bf16[512,768]{1,0:T(8,128)(2,1)}, bf16[512,768]{1,0:T(8,128)(2,1)S(1)}, u32[]{:S(2)}, u32[]{:S(2)}) %collective-permute-start.3) | collective-permute-done | bytes 786464 | tf_op jit(solution)/shard_map/ppermute | solution.py:992
  230.4 25.7 %first_back_0.1 = (bf16[512,768]{1,0:T(8,128)(2,1)}, bf16[512,3072]{1,0:T(8,128)(2,1)}, bf16[512,768]{1,0:T(8,128)(2,1)}, bf16[512,2304]{1,0:T(8,128)(2,1)}, f32...) custom-call(s32[1]{0:T(128)} %bitcast.refs_0_, ...), custom_call_target="tpu_custom_call", output_to_operand_aliasing={{0}: (12, {}), {1}: (13, {}), {2}: (14, {}), {3}: (15, {}),... | custom-call | flops 24999999488 | bytes 31457280 | tf_op jit(solution)/shard_map/first_back_0/pallas_call | solution.py:432
  256.1 15.6 %collective-permute-done.2.refs_4_ = bf16[512,768]{1,0:T(8,128)(2,1)S(1)} collective-permute-done((bf16[512,768]{1,0:T(8,128)(2,1)}, bf16[512,768]{1,0:T(8,128)(2,1)S(1)}, u32[]{:S(2)}, u32[]{:S(2)}) %collective-permute-start.2) | collective-permute-done | bytes 786464 | tf_op jit(solution)/shard_map/ppermute | solution.py:992
  272.5 26.5 %first_back_1.1 = (bf16[512,768]{1,0:T(8,128)(2,1)}, bf16[512,3072]{1,0:T(8,128)(2,1)}, bf16[512,768]{1,0:T(8,128)(2,1)}, bf16[512,2304]{1,0:T(8,128)(2,1)}, f32...) custom-call(s32[1]{0:T(128)} %bitcast.refs_0_, ...), custom_call_target="tpu_custom_call", output_to_operand_aliasing={{0}: (12, {}), {1}: (13, {}), {2}: (14, {}), {3}: (15, {}),... | custom-call | flops 24999999488 | bytes 31457280 | tf_op jit(solution)/shard_map/first_back_1/pallas_call | solution.py:432
  299.1 20.5 %grads_2304.1 = (bf16[96,32,768]{2,1,0:T(8,128)(2,1)}, bf16[96,32,768]{2,1,0:T(8,128)(2,1)}, bf16[96,32,768]{2,1,0:T(8,128)(2,1)}, bf16[96,32,768]{2,1,0:T(8,128)(2,1)}, bf16[496,32,768]{2,1,0:T(8,128)(2,1)}) custom-call(s32[288]{0:T(512)} %get-tuple-element.216.code_ref, s32[288]{0:T(512)} %get-tuple-element.213.index_ref, ...), custom_call_target="tpu_custom_call" | custom-call | flops 19327352832 | bytes 12582912 | tf_op jit(solution)/shard_map/grads_2304/pallas_call | solution.py:694
  319.7 1.4 collective-permute-start.4
  321.0 11.8 %grads_6144.1 = (bf16[96,32,768]{2,1,0:T(8,128)(2,1)}, bf16[96,32,768]{2,1,0:T(8,128)(2,1)}, bf16[496,32,768]{2,1,0:T(8,128)(2,1)}, bf16[96,32,768]{2,1,0:T(8,128)(2,1)}) custom-call(s32[288]{0:T(512)} %get-tuple-element.216.code_ref, s32[288]{0:T(512)} %get-tuple-element.213.index_ref, ...), custom_call_target="tpu_custom_call", output_to_operand_aliasing={{0}: (6, {}), {1}: (7, {}), {2}: (8, {}), {3}: (9, {})} | custom-call | flops 9663676416 | bytes 12582912 | tf_op jit(solution)/shard_map/grads_6144/pallas_call | solution.py:694
  334.2 3.0 hop.10
  337.2 2.0 collective-permute-start.5
  340.0 1.3 conditional.3
  340.0 1.3 broadcast.204
  341.3 4.4 collective-permute-done.5.refs_2_
  345.7 1.6 collective-permute-done.6.refs_3_
  348.0 3.7 hop.11
  351.7 1.1 collective-permute-start.7
  354.1 5.8 %all-to-all-start.1 = ((bf16[16,2,4608]{2,1,0:T(2,128)(2,1)}), bf16[16,2,4608]{2,1,0:T(2,128)(2,1)S(1)}, u32[]{:S(2)}, u32[]{:S(2)}) async-start(bf16[16,2,4608]{2,1,0:T(2,128)(2,1)} %broadcast_in_dim.95), calls=%async_computation.2 | async-start | bytes 589824 | tf_op jit(solution)/shard_map/all_to_all | solution.py:1002
  359.9 2.9 hop.15
  362.8 1.4 collective-permute-start.15
  364.9 10.6 %collective-permute-done.15.refs_2_ = bf16[6,32,768]{2,1,0:T(8,128)(2,1)S(1)} collective-permute-done((bf16[6,32,768]{2,1,0:T(8,128)(2,1)}, bf16[6,32,768]{2,1,0:T(8,128)(2,1)S(1)}, u32[]{:S(2)}, u32[]{:S(2)}) %collective-permute-start.15) | collective-permute-done | bytes 294944 | tf_op jit(solution)/shard_map/ppermute | solution.py:820
  375.5 1.8 collective-permute-done.16.refs_3_
  378.1 3.7 hop.16
  381.8 2.0 collective-permute-start.17
  385.5 3.9 hop.12
  389.5 1.7 collective-permute-start.10
  391.9 2.6 collective-permute-done.17.refs_2_
  394.4 1.5 collective-permute-done.18.refs_3_
  396.8 4.0 hop.17
  400.8 1.3 collective-permute-start.19
  402.9 5.7 %collective-permute-done.10.refs_3_ = bf16[12,32,768]{2,1,0:T(8,128)(2,1)S(1)} collective-permute-done((bf16[12,32,768]{2,1,0:T(8,128)(2,1)}, bf16[12,32,768]{2,1,0:T(8,128)(2,1)S(1)}, u32[]{:S(2)}, u32[]{:S(2)}) %collective-permute-start.10) | collective-permute-done | bytes 589856 | tf_op jit(solution)/shard_map/ppermute | solution.py:820
  410.2 3.9 hop.13
  414.2 1.3 collective-permute-start.11
  416.1 3.6 collective-permute-done.19.refs_2_
  419.7 1.5 collective-permute-done.20.refs_3_
  422.1 4.0 hop.18
  426.0 1.3 collective-permute-start.21
  428.1 4.3 collective-permute-done.11.refs_2_
  432.4 1.5 collective-permute-done.12.refs_3_
  434.7 2.8 hop.14.refs_0_
  437.5 7.3 %collective-permute-start.13 = (bf16[12,32,768]{2,1,0:T(8,128)(2,1)}, bf16[12,32,768]{2,1,0:T(8,128)(2,1)S(1)}, u32[]{:S(2)}, u32[]{:S(2)}) collective-permute-start(bf16[12,32,768]{2,1,0:T(8,128)(2,1)} %hop.14.refs_0_), channel_id=1, source_target_pairs={{0,1},{1,0},{2,3},{3,2},{4,5},{5,4},{6,7},{7,6},{8,9},{9,8},{10,11... | collective-permute-start | bytes 1769480 | tf_op jit(solution)/shard_map/ppermute | solution.py:813
  446.9 1.4 copy.67
  449.1 8.1 %adam_0.1 = (f32[31,32,768]{2,1,0:T(8,128)}, f32[31,32,768]{2,1,0:T(8,128)}, f32[31,32,768]{2,1,0:T(8,128)}, bf16[31,32,768]{2,1,0:T(8,128)(2,1)}) custom-call(s32[31]{0:T(128)} %get-tuple-element.231.code_ref, s32[31]{0:T(128)} %get-tuple-element.209.index_ref, s32[31]{0:T(128)} %get-tuple-element.230.row_ref, f32[31,32,768]{2,1,0:T(8,128)} %bitcast.52, ...), custom_call_target="tpu_custom_call" | custom-call | bytes 11427840 | tf_op jit(solution)/shard_map/adam_0/pallas_call | solution.py:792
  458.3 2.8 hop.19.refs_2_
  461.9 1.8 collective-permute-done.23.refs_3_
  464.6 5.0 %adam_4.1 = (f32[31,32,768]{2,1,0:T(8,128)}, f32[31,32,768]{2,1,0:T(8,128)}, f32[31,32,768]{2,1,0:T(8,128)}, bf16[31,32,768]{2,1,0:T(8,128)(2,1)}) custom-call(s32[31]{0:T(128)} %get-tuple-element.231.code_ref, s32[31]{0:T(128)} %get-tuple-element.209.index_ref, ...), custom_call_target="tpu_custom_call", output_to_operand_aliasing={{0}: (13, {}), {1}: (14, {}), {2}: (15, {}), {3}: (16, {})} | custom-call | bytes 11427840 | tf_op jit(solution)/shard_map/adam_4/pallas_call | solution.py:792
  (163 shorter events, 30.1 us)
Async XLA Ops:
  7.2 112.9 %all-gather.5.cloned.1.call-start = ((), (), s32[]{:S(2)}) async-start(), calls=%async_computation.5 | async-start | bytes 20889600 | tf_op jit(solution)/shard_map/all_gather | solution.py:945
  10.4 1.7 copy-start.42
  10.5 1.8 copy-start.24
  12.5 110.1 %copy-start.22 = (s32[288]{0:T(512)}, s32[288]{0:T(512)S(1)}, u32[]{:S(2)}) copy-start(s32[288]{0:T(512)S(1)} %convert_reduce_fusion.2) | copy-start | bytes 3460
  13.0 109.6 %copy-start.20 = (s32[432]{0:T(512)}, s32[432]{0:T(512)S(1)}, u32[]{:S(2)}) copy-start(s32[432]{0:T(512)S(1)} %convert_reduce_fusion) | copy-start | bytes 5188
  13.6 109.0 %copy-start.35 = (pred[288]{0:T(512)(128)(4,1)}, pred[288]{0:T(512)(128)(4,1)S(1)}, u32[]{:S(2)}) copy-start(pred[288]{0:T(512)(128)(4,1)S(1)} %get-tuple-element.214) | copy-start | bytes 868
  60.1 62.5 %copy-start.30 = (f32[34]{0:T(128)}, f32[34]{0:T(128)S(1)}, u32[]{:S(2)}) copy-start(f32[34]{0:T(128)S(1)} %pmax.7) | copy-start | bytes 412
  62.1 15.2 %all-to-all-start = ((f32[16,2,992]{2,1,0:T(2,128)}), f32[16,2,992]{2,1,0:T(2,128)S(1)}, u32[]{:S(2)}, u32[]{:S(2)}) async-start(f32[16,2,992]{2,1,0:T(2,128)} %copy.63), calls=%async_computation.1 | async-start | bytes 262144 | tf_op jit(solution)/shard_map/all_to_all | solution.py:969
  149.3 20.4 %collective-permute-start.1 = (bf16[512,768]{1,0:T(8,128)(2,1)}, bf16[512,768]{1,0:T(8,128)(2,1)S(1)}, u32[]{:S(2)}, u32[]{:S(2)}) collective-permute-start(bf16[512,768]{1,0:T(8,128)(2,1)} %get-tuple-element.118), channel_id=1, source_target_pairs={{0,16},{1,17},{2,18},{3,19},{4,20},{5,21},{6,22},{7,23},{8,24},{9,... | collective-permute-start | bytes 2359304 | tf_op jit(solution)/shard_map/ppermute | solution.py:986
  168.3 18.6 %collective-permute-start = (bf16[512,768]{1,0:T(8,128)(2,1)}, bf16[512,768]{1,0:T(8,128)(2,1)S(1)}, u32[]{:S(2)}, u32[]{:S(2)}) collective-permute-start(bf16[512,768]{1,0:T(8,128)(2,1)} %get-tuple-element.113), channel_id=1, source_target_pairs={{0,16},{1,17},{2,18},{3,19},{4,20},{5,21},{6,22},{7,23},{8,24},{9,... | collective-permute-start | bytes 2359304 | tf_op jit(solution)/shard_map/ppermute | solution.py:986
  169.7 0.9 copy-start.41
  185.6 43.9 %collective-permute-start.3 = (bf16[512,768]{1,0:T(8,128)(2,1)}, bf16[512,768]{1,0:T(8,128)(2,1)S(1)}, u32[]{:S(2)}, u32[]{:S(2)}) collective-permute-start(bf16[512,768]{1,0:T(8,128)(2,1)} %get-tuple-element.134), channel_id=1, source_target_pairs={{16,0},{17,1},{18,2},{19,3},{20,4},{21,5},{22,6},{23,7},{24,8},{25... | collective-permute-start | bytes 2359304 | tf_op jit(solution)/shard_map/ppermute | solution.py:992
  186.9 0.9 copy-start.40
  202.9 68.8 %collective-permute-start.2 = (bf16[512,768]{1,0:T(8,128)(2,1)}, bf16[512,768]{1,0:T(8,128)(2,1)S(1)}, u32[]{:S(2)}, u32[]{:S(2)}) collective-permute-start(bf16[512,768]{1,0:T(8,128)(2,1)} %get-tuple-element.127), channel_id=1, source_target_pairs={{16,0},{17,1},{18,2},{19,3},{20,4},{21,5},{22,6},{23,7},{24,8},{25... | collective-permute-start | bytes 2359304 | tf_op jit(solution)/shard_map/ppermute | solution.py:992
  229.5 0.9 copy-start.39
  271.7 0.9 copy-start.38
  319.7 14.6 %collective-permute-start.4 = (bf16[96,32,768]{2,1,0:T(8,128)(2,1)}, bf16[96,32,768]{2,1,0:T(8,128)(2,1)}, u32[]{:S(2)}, u32[]{:S(2)}) collective-permute-start(bf16[96,32,768]{2,1,0:T(8,128)(2,1)} %get-tuple-element.181), channel_id=1, source_target_pairs={{0,1},{1,0},{2,3},{3,2},{4,5},{5,4},{6,7},{7,6},{8,9},{9,8},{10,11... | collective-permute-start | bytes 14155784 | tf_op jit(solution)/shard_map/ppermute | solution.py:813
  332.9 27.1 %collective-permute-start.14 = (bf16[96,32,768]{2,1,0:T(8,128)(2,1)}, bf16[96,32,768]{2,1,0:T(8,128)(2,1)}, u32[]{:S(2)}, u32[]{:S(2)}) collective-permute-start(bf16[96,32,768]{2,1,0:T(8,128)(2,1)} %get-tuple-element.192), channel_id=1, source_target_pairs={{0,1},{1,0},{2,3},{3,2},{4,5},{5,4},{6,7},{7,6},{8,9},{9,8},{10,11... | collective-permute-start | bytes 14155784 | tf_op jit(solution)/shard_map/ppermute | solution.py:813
  334.2 5.6 %copy-start.34 = (f32[2,768]{1,0:T(2,128)S(1)}, f32[2,768]{1,0:T(2,128)}, u32[]{:S(2)}) copy-start(f32[2,768]{1,0:T(2,128)} %get-tuple-element.148.refs_11_) | copy-start | bytes 18436
  334.2 5.6 %copy-start.29 = (f32[4,768]{1,0:T(4,128)S(1)}, f32[4,768]{1,0:T(4,128)}, u32[]{:S(2)}) copy-start(f32[4,768]{1,0:T(4,128)} %get-tuple-element.157) | copy-start | bytes 36868
  334.2 5.7 %copy-start.28 = (f32[4,768]{1,0:T(4,128)S(1)}, f32[4,768]{1,0:T(4,128)}, u32[]{:S(2)}) copy-start(f32[4,768]{1,0:T(4,128)} %get-tuple-element.159) | copy-start | bytes 36868
  334.2 5.7 %copy-start.33 = (f32[2,768]{1,0:T(2,128)S(1)}, f32[2,768]{1,0:T(2,128)}, u32[]{:S(2)}) copy-start(f32[2,768]{1,0:T(2,128)} %get-tuple-element.158) | copy-start | bytes 18436
  337.2 8.4 %collective-permute-start.5 = (bf16[6,32,768]{2,1,0:T(8,128)(2,1)}, bf16[6,32,768]{2,1,0:T(8,128)(2,1)S(1)}, u32[]{:S(2)}, u32[]{:S(2)}) collective-permute-start(bf16[6,32,768]{2,1,0:T(8,128)(2,1)} %get-tuple-element.182), channel_id=1, source_target_pairs={{0,4},{1,5},{4,8},{5,9},{8,12},{9,13},{12,14},{13,15},{14,10},{15,... | collective-permute-start | bytes 884744 | tf_op jit(solution)/shard_map/ppermute | solution.py:820
  339.2 8.1 %collective-permute-start.6 = (bf16[6,32,768]{2,1,0:T(8,128)(2,1)}, bf16[6,32,768]{2,1,0:T(8,128)(2,1)S(1)}, u32[]{:S(2)}, u32[]{:S(2)}) collective-permute-start(bf16[6,32,768]{2,1,0:T(8,128)(2,1)} %get-tuple-element.183), channel_id=1, source_target_pairs={{0,2},{1,3},{4,0},{5,1},{8,4},{9,5},{12,8},{13,9},{14,12},{15,13},... | collective-permute-start | bytes 884744 | tf_op jit(solution)/shard_map/ppermute | solution.py:820
  345.7 1.6 copy-start.17
  351.7 32.1 %collective-permute-start.7 = (bf16[12,32,768]{2,1,0:T(8,128)(2,1)}, bf16[12,32,768]{2,1,0:T(8,128)(2,1)S(1)}, u32[]{:S(2)}, u32[]{:S(2)}) collective-permute-start(bf16[12,32,768]{2,1,0:T(8,128)(2,1)} %get-tuple-element.185), channel_id=1, source_target_pairs={{0,4},{1,5},{4,8},{5,9},{8,12},{9,13},{12,14},{13,15},{14,10},{15,... | collective-permute-start | bytes 1769480 | tf_op jit(solution)/shard_map/ppermute | solution.py:820
  352.8 31.1 %collective-permute-start.8 = (bf16[12,32,768]{2,1,0:T(8,128)(2,1)}, bf16[12,32,768]{2,1,0:T(8,128)(2,1)S(1)}, u32[]{:S(2)}, u32[]{:S(2)}) collective-permute-start(bf16[12,32,768]{2,1,0:T(8,128)(2,1)} %get-tuple-element.186), channel_id=1, source_target_pairs={{0,2},{1,3},{4,0},{5,1},{8,4},{9,5},{12,8},{13,9},{14,12},{15,13},... | collective-permute-start | bytes 1769480 | tf_op jit(solution)/shard_map/ppermute | solution.py:820
  354.1 29.7 %all-to-all-start.1 = ((bf16[16,2,4608]{2,1,0:T(2,128)(2,1)}), bf16[16,2,4608]{2,1,0:T(2,128)(2,1)S(1)}, u32[]{:S(2)}, u32[]{:S(2)}) async-start(bf16[16,2,4608]{2,1,0:T(2,128)(2,1)} %broadcast_in_dim.95), calls=%async_computation.2 | async-start | bytes 589824 | tf_op jit(solution)/shard_map/all_to_all | solution.py:1002
  362.8 12.7 %collective-permute-start.15 = (bf16[6,32,768]{2,1,0:T(8,128)(2,1)}, bf16[6,32,768]{2,1,0:T(8,128)(2,1)S(1)}, u32[]{:S(2)}, u32[]{:S(2)}) collective-permute-start(bf16[6,32,768]{2,1,0:T(8,128)(2,1)} %get-tuple-element.193), channel_id=1, source_target_pairs={{0,4},{1,5},{4,8},{5,9},{8,12},{9,13},{12,14},{13,15},{14,10},{15,... | collective-permute-start | bytes 884744 | tf_op jit(solution)/shard_map/ppermute | solution.py:820
  364.2 13.1 %collective-permute-start.16 = (bf16[6,32,768]{2,1,0:T(8,128)(2,1)}, bf16[6,32,768]{2,1,0:T(8,128)(2,1)S(1)}, u32[]{:S(2)}, u32[]{:S(2)}) collective-permute-start(bf16[6,32,768]{2,1,0:T(8,128)(2,1)} %get-tuple-element.194), channel_id=1, source_target_pairs={{0,2},{1,3},{4,0},{5,1},{8,4},{9,5},{12,8},{13,9},{14,12},{15,13},... | collective-permute-start | bytes 884744 | tf_op jit(solution)/shard_map/ppermute | solution.py:820
  375.5 1.8 copy-start.16
  381.8 12.6 %collective-permute-start.17 = (bf16[12,32,768]{2,1,0:T(8,128)(2,1)}, bf16[12,32,768]{2,1,0:T(8,128)(2,1)S(1)}, u32[]{:S(2)}, u32[]{:S(2)}) collective-permute-start(bf16[12,32,768]{2,1,0:T(8,128)(2,1)} %get-tuple-element.195), channel_id=1, source_target_pairs={{0,4},{1,5},{4,8},{5,9},{8,12},{9,13},{12,14},{13,15},{14,10},{15,... | collective-permute-start | bytes 1769480 | tf_op jit(solution)/shard_map/ppermute | solution.py:820
  383.8 8.0 %copy-start.25 = (s32[1,432]{1,0:T(1,128)S(1)}, s32[1,432]{1,0:T(1,128)}, u32[]{:S(2)}) copy-start(s32[1,432]{1,0:T(1,128)} %param.16) | copy-start | bytes 5188
  383.8 12.2 %collective-permute-start.18 = (bf16[12,32,768]{2,1,0:T(8,128)(2,1)}, bf16[12,32,768]{2,1,0:T(8,128)(2,1)S(1)}, u32[]{:S(2)}, u32[]{:S(2)}) collective-permute-start(bf16[12,32,768]{2,1,0:T(8,128)(2,1)} %get-tuple-element.196), channel_id=1, source_target_pairs={{0,2},{1,3},{4,0},{5,1},{8,4},{9,5},{12,8},{13,9},{14,12},{15,13},... | collective-permute-start | bytes 1769480 | tf_op jit(solution)/shard_map/ppermute | solution.py:820
  383.8 0.9 copy-start.3
  389.5 19.1 %collective-permute-start.10 = (bf16[12,32,768]{2,1,0:T(8,128)(2,1)}, bf16[12,32,768]{2,1,0:T(8,128)(2,1)S(1)}, u32[]{:S(2)}, u32[]{:S(2)}) collective-permute-start(bf16[12,32,768]{2,1,0:T(8,128)(2,1)} %get-tuple-element.188), channel_id=1, source_target_pairs={{0,2},{1,3},{4,0},{5,1},{8,4},{9,5},{12,8},{13,9},{14,12},{15,13},... | collective-permute-start | bytes 1769480 | tf_op jit(solution)/shard_map/ppermute | solution.py:820
  391.2 17.4 %collective-permute-start.9 = (bf16[12,32,768]{2,1,0:T(8,128)(2,1)}, bf16[12,32,768]{2,1,0:T(8,128)(2,1)S(1)}, u32[]{:S(2)}, u32[]{:S(2)}) collective-permute-start(bf16[12,32,768]{2,1,0:T(8,128)(2,1)} %get-tuple-element.187), channel_id=1, source_target_pairs={{0,4},{1,5},{4,8},{5,9},{8,12},{9,13},{12,14},{13,15},{14,10},{15,... | collective-permute-start | bytes 1769480 | tf_op jit(solution)/shard_map/ppermute | solution.py:820
  394.4 1.5 copy-start.10
  396.0 0.8 copy-start.11
  400.8 19.0 %collective-permute-start.19 = (bf16[12,32,768]{2,1,0:T(8,128)(2,1)}, bf16[12,32,768]{2,1,0:T(8,128)(2,1)S(1)}, u32[]{:S(2)}, u32[]{:S(2)}) collective-permute-start(bf16[12,32,768]{2,1,0:T(8,128)(2,1)} %get-tuple-element.197), channel_id=1, source_target_pairs={{0,4},{1,5},{4,8},{5,9},{8,12},{9,13},{12,14},{13,15},{14,10},{15,... | collective-permute-start | bytes 1769480 | tf_op jit(solution)/shard_map/ppermute | solution.py:820
  402.1 13.6 %copy-start.21 = (s32[432]{0:T(512)S(1)}, s32[432]{0:T(512)}, u32[]{:S(2)}) copy-start(s32[432]{0:T(512)} %copy-done.20) | copy-start | bytes 5188
  402.1 13.7 %copy-start.23 = (s32[288]{0:T(512)S(1)}, s32[288]{0:T(512)}, u32[]{:S(2)}) copy-start(s32[288]{0:T(512)} %copy-done.22) | copy-start | bytes 3460
  402.1 13.7 %copy-start.36 = (pred[288]{0:T(512)(128)(4,1)S(1)}, pred[288]{0:T(512)(128)(4,1)}, u32[]{:S(2)}) copy-start(pred[288]{0:T(512)(128)(4,1)} %copy-done.35) | copy-start | bytes 868
  402.1 13.8 %copy-start.37 = (pred[288]{0:T(512)(128)(4,1)S(1)}, pred[288]{0:T(512)(128)(4,1)}, u32[]{:S(2)}) copy-start(pred[288]{0:T(512)(128)(4,1)} %get-tuple-element.217) | copy-start | bytes 868
  402.1 13.8 %copy-start.27 = (f32[384]{0:T(512)S(1)}, f32[384]{0:T(512)}, u32[]{:S(2)}) copy-start(f32[384]{0:T(512)} %copy-done.26) | copy-start | bytes 4612
  402.1 13.8 %copy-start.31 = (f32[34]{0:T(128)S(1)}, f32[34]{0:T(128)}, u32[]{:S(2)}) copy-start(f32[34]{0:T(128)} %copy-done.30) | copy-start | bytes 412
  402.1 19.1 %collective-permute-start.20 = (bf16[12,32,768]{2,1,0:T(8,128)(2,1)}, bf16[12,32,768]{2,1,0:T(8,128)(2,1)S(1)}, u32[]{:S(2)}, u32[]{:S(2)}) collective-permute-start(bf16[12,32,768]{2,1,0:T(8,128)(2,1)} %get-tuple-element.198), channel_id=1, source_target_pairs={{0,2},{1,3},{4,0},{5,1},{8,4},{9,5},{12,8},{13,9},{14,12},{15,13},... | collective-permute-start | bytes 1769480 | tf_op jit(solution)/shard_map/ppermute | solution.py:820
  408.6 0.8 copy-start.12
  414.2 18.2 %collective-permute-start.11 = (bf16[12,32,768]{2,1,0:T(8,128)(2,1)}, bf16[12,32,768]{2,1,0:T(8,128)(2,1)S(1)}, u32[]{:S(2)}, u32[]{:S(2)}) collective-permute-start(bf16[12,32,768]{2,1,0:T(8,128)(2,1)} %get-tuple-element.189), channel_id=1, source_target_pairs={{0,4},{1,5},{4,8},{5,9},{8,12},{9,13},{12,14},{13,15},{14,10},{15,... | collective-permute-start | bytes 1769480 | tf_op jit(solution)/shard_map/ppermute | solution.py:820
  415.5 18.4 %collective-permute-start.12 = (bf16[12,32,768]{2,1,0:T(8,128)(2,1)}, bf16[12,32,768]{2,1,0:T(8,128)(2,1)S(1)}, u32[]{:S(2)}, u32[]{:S(2)}) collective-permute-start(bf16[12,32,768]{2,1,0:T(8,128)(2,1)} %get-tuple-element.190), channel_id=1, source_target_pairs={{0,2},{1,3},{4,0},{5,1},{8,4},{9,5},{12,8},{13,9},{14,12},{15,13},... | collective-permute-start | bytes 1769480 | tf_op jit(solution)/shard_map/ppermute | solution.py:820
  419.7 1.5 copy-start.14
  421.2 0.8 copy-start.15
  426.0 31.2 %collective-permute-start.21 = (bf16[12,32,768]{2,1,0:T(8,128)(2,1)}, bf16[12,32,768]{2,1,0:T(8,128)(2,1)S(1)}, u32[]{:S(2)}, u32[]{:S(2)}) collective-permute-start(bf16[12,32,768]{2,1,0:T(8,128)(2,1)} %get-tuple-element.199), channel_id=1, source_target_pairs={{0,4},{1,5},{4,8},{5,9},{8,12},{9,13},{12,14},{13,15},{14,10},{15,... | collective-permute-start | bytes 1769480 | tf_op jit(solution)/shard_map/ppermute | solution.py:820
  427.4 29.9 %collective-permute-start.22 = (bf16[12,32,768]{2,1,0:T(8,128)(2,1)}, bf16[12,32,768]{2,1,0:T(8,128)(2,1)S(1)}, u32[]{:S(2)}, u32[]{:S(2)}) collective-permute-start(bf16[12,32,768]{2,1,0:T(8,128)(2,1)} %get-tuple-element.200), channel_id=1, source_target_pairs={{0,2},{1,3},{4,0},{5,1},{8,4},{9,5},{12,8},{13,9},{14,12},{15,13},... | collective-permute-start | bytes 1769480 | tf_op jit(solution)/shard_map/ppermute | solution.py:820
  432.4 1.5 copy-start.7
  433.9 0.8 copy-start.8
  434.7 10.8 %copy-start.32 = (s32[288]{0:T(512)S(1)}, s32[288]{0:T(512)}, u32[]{:S(2)}) copy-start(s32[288]{0:T(512)} %get-tuple-element.226) | copy-start | bytes 3460
  434.7 12.0 %copy-start.1 = (bf16[16,2,4608]{2,1,0:T(2,128)(2,1)S(1)}, bf16[16,2,4608]{2,1,0:T(2,128)(2,1)}, u32[]{:S(2)}) copy-start(bf16[16,2,4608]{2,1,0:T(2,128)(2,1)} %copy-done) | copy-start | bytes 884740
  437.5 10.7 %collective-permute-start.13 = (bf16[12,32,768]{2,1,0:T(8,128)(2,1)}, bf16[12,32,768]{2,1,0:T(8,128)(2,1)S(1)}, u32[]{:S(2)}, u32[]{:S(2)}) collective-permute-start(bf16[12,32,768]{2,1,0:T(8,128)(2,1)} %hop.14.refs_0_), channel_id=1, source_target_pairs={{0,1},{1,0},{2,3},{3,2},{4,5},{5,4},{6,7},{7,6},{8,9},{9,8},{10,11... | collective-permute-start | bytes 1769480 | tf_op jit(solution)/shard_map/ppermute | solution.py:813
  448.3 0.8 copy-start.2
  457.2 0.9 copy-start.5
  457.2 1.0 copy-start.6
  461.1 2.6 collective-permute-start.23
  463.7 0.9 copy-start.9
  (6 other events, 4.3 us)
Sparse Core Ops, SparseCore 0:
  11.7 108.3 all-gather.4

commit v5 on v4

--- a/solution.py
+++ b/solution.py
@@ -599,18 +599,19 @@
     )
 
 
-def grads_kernel(jobs, clips, length, panel_rows, own, passed, others, code_ref, index_ref, *refs):
+def grads_kernel(jobs, clips, length, panel_rows, plain, added, own, passed, others, code_ref, index_ref, *refs):
     count = 2 * len(jobs) * clips
-    sources = refs[:count]
+    sources, partial = refs[:count], refs[count + others - 1]
     refs = refs[count + others :]
     outs = refs[:own]
     scratch = refs[own + passed :]
     values = scratch[: 2 * len(jobs)]
-    tile_v, in_sem, out_sem = scratch[2 * len(jobs) :]
+    tile_v, add_v, in_sem, add_sem, out_sem = scratch[2 * len(jobs) :]
+    per_tile = D // panel_rows
     tiles = []
     for n, (left, right, base) in enumerate(jobs):
         tiles += [(n, column, base + column) for column in range(0, values[2 * n].shape[1], D)]
-    get = {}
+    get, more = {}, {}
 
     def fetch(n, column):
         get[n, column] = [
@@ -628,11 +629,12 @@
             if column == 0:
                 fetch(2 * n + 1, 0)
             fetch(2 * n, column)
+            if added:
+                first_panel = tiles[t][2] // panel_rows
+                more[t] = start(partial.at[pl.ds(first_panel, per_tile)], add_v.at[t % 4], add_sem.at[t % 4])
 
     for t in range(3):
         fetch_tile(t)
-    per_tile = D // panel_rows
-
     def drain(slot):
         pltpu.make_async_copy(outs[-1].at[pl.ds(0, per_tile)], tile_v.at[slot], out_sem.at[slot]).wait()
 
@@ -647,7 +649,14 @@
         if t >= 2:
             drain(slot)
         part = dot_tn(values[2 * n][:, column : column + D], values[2 * n + 1][...])
+        if added:
+            more[t].wait()
+            part = part + add_v[t % 4].reshape(D, D).astype(f32)
         tile_v[slot, :, :, :] = part.astype(bf16).reshape(per_tile, panel_rows, D)
+        if plain:
+            first_panel = first_row // panel_rows
+            pltpu.make_async_copy(tile_v.at[slot], outs[0].at[pl.ds(first_panel, per_tile)], out_sem.at[slot]).start()
+            continue
 
         @pl.loop(0, per_tile)
         def _(p):
@@ -672,7 +681,7 @@
         drain(slot)
 
 
-def weight_grads(jobs, code, index, every, length, panel_rows, sizes, thread, after, through=()):
+def weight_grads(jobs, code, index, every, length, panel_rows, sizes, thread=(), after=(), through=(), partial=None, plain=False):
     clips = len(every)
     any_spec = pl.BlockSpec(memory_space=pltpu.HBM)
     operands, scratch = [code, index], []
@@ -690,24 +699,31 @@
         aliases[len(operands)] = len(sizes) + n
         operands.append(array)
     operands += after
+    if partial is not None:
+        operands.append(partial)
+    others = len(operands) - 2 - 2 * len(jobs) * clips
     width = sum(s.shape[1] for s in scratch[0::2])
     return pl.pallas_call(
-        functools.partial(grads_kernel, jobs, clips, length, panel_rows, len(sizes), len(passed), len(thread) + len(through) + len(after)),
+        functools.partial(
+            grads_kernel, jobs, clips, length, panel_rows, plain, partial is not None, len(sizes), len(passed), others
+        ),
         out_shape=[pltpu.HBM((size, panel_rows, D), bf16) for size in sizes] + passed,
         in_specs=[pl.BlockSpec(memory_space=pltpu.SMEM)] * 2 + [any_spec] * (len(operands) - 2),
         out_specs=[any_spec] * (len(sizes) + len(passed)),
         scratch_shapes=scratch
         + [
             pltpu.VMEM((2, D // panel_rows, panel_rows, D), bf16),
+            pltpu.VMEM((4 if partial is not None else 1, D // panel_rows, panel_rows, D), bf16),
             pltpu.SemaphoreType.DMA((width // D + len(jobs), clips)),
+            pltpu.SemaphoreType.DMA((4,)),
             pltpu.SemaphoreType.DMA((2,)),
         ],
         input_output_aliases=aliases,
-        compiler_params=pltpu.CompilerParams(vmem_limit_bytes=VMEM_ALL),
+        compiler_params=pltpu.CompilerParams(vmem_limit_bytes=26 * 1024 * 1024 if plain else VMEM_ALL),
         cost_estimate=pl.CostEstimate(
             flops=4 * clips * length * width * D, bytes_accessed=12 << 20, transcendentals=0
         ),
-        name=f"grads_{jobs[0][2]}",
+        name=f"grads_{jobs[0][2]}_{plain:d}",
     )(*operands[:2], *in_hbm(operands[2:]))
 
 
@@ -888,6 +904,7 @@
             spans, came = [(0, size)] * 2, [self.ahead, self.behind]
             adds = [(0, 0, half, 0), (1, half, size, half)] if n == 3 else [(0, 0, size, 0), (1, 0, size, 0)]
         ahead, behind = hop_sums(spots.astype(jnp.int32), self.terms, spans, adds, came, after)
+        self.sent = [ahead, behind]
         self.ahead, self.behind = along(ahead, 1), along(behind, -1)
         self.left -= 1
 
@@ -919,7 +936,8 @@
     slots, panel_rows = master.shape[1], master.shape[2]
     clips = timesteps.shape[0]
     length = tokens.shape[0] // clips
-    owner = owners[0]
+    low = master[0].astype(bf16)
+    owner = owners[0] + (0.0 * low[0, 0, 0].astype(f32)).astype(jnp.int32)
     panels = owner.shape[0]
     moved = DOWN_END // panel_rows
     cap = min(slots, max(4, (slots * 25 + 30) // 31))
@@ -941,7 +959,6 @@
 
     rings = owner_total == 2 * CHIPS
     code, index, slot_code, slot_index, sizes, beyond = routes(owner, rank, mine, me, owner_total, slots, moved)
-    low = master[0].astype(bf16)
     gathered = lax.all_gather(low[:cap], BATCH, axis=0, tiled=True)
     spot = jnp.arange(owner_total * clips, dtype=jnp.int32) // clips == me
     news = [jnp.where(spot, jnp.tile(timesteps.astype(f32), owner_total), 0.0)]
@@ -992,10 +1009,16 @@
     received = [lax.ppermute(f[N_SENT], SECTION, [(1, 0)]) for f in seconds]
     every = [dict(f) for f in seconds]
 
+    all_jobs = ((N_Z, N_DB, UP_END), (N_DU, N_H2, PROJ_END), (N_DA, N_O, QKV_END), (N_DQKV, N_H1, 0))
+    grads = run(weight_grads, code=code, index=index, length=length, panel_rows=panel_rows)
+    partial, after = None, mod
     for c in range(clips):
         chain = {n: every[c][n] for n in BACK_MAKES} | {N_GIN: gin}
-        every[c] |= first_back(c, x=tokens, g=received[c], kept=firsts[c], chain=chain, after=every[0][N_DMOD_ATT] if c else mod, **base)
-        gin = every[c][N_GIN]
+        every[c] |= first_back(c, x=tokens, g=received[c], kept=firsts[c], chain=chain, after=after, **base)
+        gin, after = every[c][N_GIN], every[c][N_DMOD_ATT]
+        if rings and c == clips - 2:
+            (partial,) = grads(all_jobs, every=every[:-1], sizes=[moved], plain=True)
+            after = partial
 
     dmod = [jnp.concatenate([e[N_DMOD_ATT], e[N_DMOD_FFN]]) for e in every]
     dmod = jnp.stack(dmod).reshape(1, clips, 6 * D).astype(bf16)
@@ -1007,14 +1030,16 @@
         adam, code=slot_code, index=slot_index, row=grad_row, master=master[0], first=first_moment[0],
         second=second_moment[0], dmod=dmod.reshape(clip_total, 6 * D).T, cond=cond,
     )
-    grads = run(weight_grads, code=code, index=index, every=every, length=length, panel_rows=panel_rows)
     if rings:
         place = me // 4 + (me // 2) % 2 * (CHIPS - 1 - 2 * (me // 4))
         wide = [sizes[1]] * 2 + [sizes[2]]
         first_jobs = ((N_DA, N_O, QKV_END), (N_DQKV, N_H1, 0), (N_DU, N_H2, PROJ_END))
-        made = grads(first_jobs, sizes=[sizes[0]] * 2 + wide, thread=[], after=[])
+        now = every[-1:] if partial is not None else every
+        made = grads(first_jobs, every=now, sizes=[sizes[0]] * 2 + wide, partial=partial)
         first = Ring(place, *made[:2])
-        made = grads(((N_Z, N_DB, UP_END),), sizes=wide, thread=made[2:], after=[], through=first.held(1))
+        made = grads(
+            ((N_Z, N_DB, UP_END),), every=now, sizes=wide, thread=made[2:], through=first.held(1), partial=partial
+        )
         made = first.later(made)
         second = Ring(place, *made[:2])
         rest = lax.cond(
@@ -1023,18 +1048,23 @@
             lambda part: jnp.zeros((slots, panel_rows, D), bf16),
             made[2],
         )
-        for n in range(4):
-            first.hop(after=[[], [rest], [dmod], []][n])
-            second.hop()
+        first.hop()
+        second.hop()
+        first.hop(after=[rest, *second.sent])
+        second.hop(after=[dmod])
+        results = update(0, 2, sums=[], chain=[])
+        first.hop()
+        second.hop(after=results[3:])
+        first.hop()
+        second.hop()
         half = first.finish()
         sums = [half, swap_cores(half)]
-        results = update(0, 4, sums=sums, chain=[])
+        results = update(2, 4, sums=sums, chain=results)
         half = second.finish(after=results[3:])
         sums += [half, swap_cores(half), rest]
         results = update(4, 7, sums=sums, chain=results)
     else:
-        jobs = ((N_Z, N_DB, UP_END), (N_DU, N_H2, PROJ_END), (N_DA, N_O, QKV_END), (N_DQKV, N_H1, 0))
-        (made,) = grads(jobs, sizes=[sizes[0]], thread=[], after=[])
+        (made,) = grads(all_jobs, every=every, sizes=[sizes[0]])
         sums = [lax.psum_scatter(made, BATCH, scatter_dimension=0, tiled=True)]
         results = update(0, 3, sums=sums, chain=[])
     return (outs[None], gin[None], *(r[None] for r in results))

time: 481 us -> 480 us (level); the launches traced: 477 us -> 470 us
  waiting for transfers between devices: 131 us -> 109 us
  Pallas kernels: 204 us -> 213 us
  starting transfers between devices: 40.9 us -> 46.9 us
    ppermute x16, waiting for transfers between devices: 39.1 us -> 20.5 us  [along(): return lax.ppermute(value, BATCH, pairs)]
    ppermute x2, waiting for transfers between devices: 40.9 us -> 25.6 us  [body(): received = [lax.ppermute(f[N_SENT], SECTION, [(1, 0)]) for f in seconds]]
    all_to_all x1, waiting for transfers between devices: 0.01 us -> 12.4 us  [body(): lax.all_to_all(jnp.broadcast_to(dmod, (owner_total, clips, 6 * D)), BATCH...]
    ppermute x4, starting transfers between devices: 9.52 us -> 16 us  [swap_cores(): return lax.ppermute(value, BATCH, [(d, d ^ 1) for d in range(2 * CHIPS)])]
    pallas_call x2 -> x3, Pallas kernels: 32.4 us -> 38.6 us  [weight_grads(): pl.pallas_call(functools.partial(grads_kernel, jobs, clips, length, panel...]
    pallas_call x2 -> x3, Pallas kernels: 13.2 us -> 16.6 us  [adam(): pl.pallas_call(functools.partial(adam_kernel, low, high, len(sums), bool(...]
  transfers between devices with their start and end apart: 27 -> 27, of which waited for: 16 -> 15; matrix products, arithmetic and copies ran while one was open for 4% -> 4% of each run, Pallas kernels for 26% -> 29%
where the time goes in v5:
time: 480 us; the launch traced here: 470 us
  Pallas kernels  213 us (44%)
  waiting for transfers between devices  109 us (23%)
  starting transfers between devices  46.9 us (10%)
  blocking collectives  42.5 us (9%)
  local copies, waits for them, and re-layouts  25.8 us (5%)
  between operations  18.3 us (4%)
  other arithmetic  13.4 us (3%)
    pallas_call x6, Pallas kernels, call_block(): pl.pallas_call(run, out_shape=[pltpu.HBM(*write[n]) for n in w_names], in...  117 us
    pmax x1, blocking collectives, body(): news = lax.pmax(jnp.concatenate(news), (SECTION, BATCH))  42.5 us
    all_gather x1, waiting for transfers between devices, body(): gathered = lax.all_gather(low[:cap], BATCH, axis=0, tiled=True)  40.8 us
    pallas_call x3, Pallas kernels, weight_grads(): pl.pallas_call(functools.partial(grads_kernel, jobs, clips, length, panel...  38.6 us
    pallas_call x10, Pallas kernels, hop_sums(): pl.pallas_call(functools.partial(hop_kernel, spans, adds, len(after)), in...  34.8 us
    ppermute x2, waiting for transfers between devices, body(): received = [lax.ppermute(f[N_SENT], SECTION, [(1, 0)]) for f in seconds]  25.6 us
    ppermute x16, waiting for transfers between devices, along(): return lax.ppermute(value, BATCH, pairs)  20.5 us
    pallas_call x3, Pallas kernels, adam(): pl.pallas_call(functools.partial(adam_kernel, low, high, len(sums), bool(...  16.6 us
  transfers between devices with their start and end apart: 27, of which 15 were waited for; matrix products, arithmetic and copies ran while one was open for 4% of the time, Pallas kernels for 29%

profile of v5, /device:TPU:1, one launch (start us, length us, event | category | flops | bytes accessed | tf_op | source)
XLA Modules:
  0.0 470.3 jit_solution(1391791144964991901)
XLA Ops:
  7.2 3.2 fusion.27
  10.5 1.1 slice.63
  15.4 1.2 multiply_add_fusion
  18.1 42.5 %pmax.7 = f32[34]{0:T(128)S(1)} all-reduce(f32[34]{0:T(128)S(1)} %pad_maximum_fusion.3), channel_id=1, replica_groups=mesh['section'=2,'batch'=16] {'section','batch'}, use_global_device_ids=true, to_apply=%region_5.6 | all-reduce | flops 34 | bytes 272 | tf_op jit(solution)/shard_map/pmax | solution.py:967
  62.4 5.9 %all-to-all-start = ((f32[16,2,992]{2,1,0:T(2,128)}), f32[16,2,992]{2,1,0:T(2,128)S(1)}, u32[]{:S(2)}, u32[]{:S(2)}) async-start(f32[16,2,992]{2,1,0:T(2,128)} %copy.67), calls=%async_computation.1 | async-start | bytes 262144 | tf_op jit(solution)/shard_map/all_to_all | solution.py:986
  69.6 8.0 %all-to-all-done = f32[16,2,992]{2,1,0:T(2,128)S(1)} async-done(((f32[16,2,992]{2,1,0:T(2,128)}), f32[16,2,992]{2,1,0:T(2,128)S(1)}, u32[]{:S(2)}, u32[]{:S(2)}) %all-to-all-start) | async-done | bytes 127008 | tf_op jit(solution)/shard_map/all_to_all | solution.py:986
  79.3 40.8 %all-gather.5.cloned.1.call-done.refs_0_ = bf16[400,32,768]{2,1,0:T(8,128)(2,1)} async-done(((bf16[25,32,768]{2,1,0:T(8,128)(2,1)}), bf16[400,32,768]{2,1,0:T(8,128)(2,1)}) %all-gather.5.cloned.1.call-update) | async-done | bytes 19660816 | tf_op jit(solution)/shard_map/all_gather | solution.py:962
  120.1 1.2 slice.65
  122.6 2.8 conditional.2
  122.6 2.8 broadcast.181
  125.4 5.8 %assemble.1.refs_1_.refs_2_ = bf16[9216,768]{1,0:T(8,128)(2,1)S(1)} custom-call(s32[288]{0:T(512)} %bitcast.74, bf16[400,32,768]{2,1,0:T(8,128)(2,1)} %all-gather.5.cloned.1.call-done.refs_0_, bf16[96,32,768]{2,1,0:T(8,128)(2,1)} %get-tuple-element.241.refs_1_), custom_call_target="tpu_custom_call" | custom-call | bytes 14155776 | tf_op jit(solution)/shard_map/assemble/pallas_call | solution.py:109
  131.2 18.1 %first_forward_0.1 = (bf16[512,768]{1,0:T(8,128)(2,1)}, bf16[512,2304]{1,0:T(8,128)(2,1)}, f32[16,512]{1,0:T(8,128)}, bf16[512,768]{1,0:T(8,128)(2,1)}, bf16[512...) custom-call(s32[1]{0:T(128)} %bitcast.refs_0_, ...), custom_call_target="tpu_custom_call" | custom-call | flops 16999999488 | bytes 31457280 | tf_op jit(solution)/shard_map/first_forward_0/pallas_call | solution.py:432
  149.3 1.3 collective-permute-start.1
  150.7 17.7 %first_forward_1.1 = (bf16[512,768]{1,0:T(8,128)(2,1)}, bf16[512,2304]{1,0:T(8,128)(2,1)}, f32[16,512]{1,0:T(8,128)}, bf16[512,768]{1,0:T(8,128)(2,1)}, bf16[512...) custom-call(s32[1]{0:T(128)} %bitcast.refs_0_, ...), custom_call_target="tpu_custom_call", output_to_operand_aliasing={{10}: (4, {})} | custom-call | flops 16999999488 | bytes 31457280 | tf_op jit(solution)/shard_map/first_forward_1/pallas_call | solution.py:432
  168.4 1.3 collective-permute-start
  169.7 0.9 copy-done.41
  170.6 15.0 %second_both_0.1 = (bf16[512,768]{1,0:T(8,128)(2,1)}, bf16[512,768]{1,0:T(8,128)(2,1)}, bf16[512,768]{1,0:T(8,128)(2,1)}, bf16[512,3072]{1,0:T(8,128)(2,1)}, bf1...) custom-call(s32[1]{0:T(128)} %bitcast.refs_0_, ...), custom_call_target="tpu_custom_call", output_to_operand_aliasing={{0}: (6, {}), {1}: (7, {}), {2}: (8, {}), {3}: (9, {}), {10... | custom-call | flops 40000000000 | bytes 41943040 | tf_op jit(solution)/shard_map/second_both_0/pallas_call | solution.py:432
  185.6 1.3 collective-permute-start.3
  187.0 0.9 copy-done.40
  187.9 15.0 %second_both_1.1 = (bf16[512,768]{1,0:T(8,128)(2,1)}, bf16[512,768]{1,0:T(8,128)(2,1)}, bf16[512,768]{1,0:T(8,128)(2,1)}, bf16[512,3072]{1,0:T(8,128)(2,1)}, bf1...) custom-call(s32[1]{0:T(128)} %bitcast.refs_0_, ...), custom_call_target="tpu_custom_call", output_to_operand_aliasing={{0}: (6, {}), {1}: (7, {}), {2}: (8, {}), {3}: (9, {}), {10... | custom-call | flops 40000000000 | bytes 41943040 | tf_op jit(solution)/shard_map/second_both_1/pallas_call | solution.py:432
  202.9 1.3 collective-permute-start.2
  204.2 25.3 %collective-permute-done.3.refs_4_ = bf16[512,768]{1,0:T(8,128)(2,1)S(1)} collective-permute-done((bf16[512,768]{1,0:T(8,128)(2,1)}, bf16[512,768]{1,0:T(8,128)(2,1)S(1)}, u32[]{:S(2)}, u32[]{:S(2)}) %collective-permute-start.3) | collective-permute-done | bytes 786464 | tf_op jit(solution)/shard_map/ppermute | solution.py:1009
  229.5 0.9 copy-done.39
  230.4 25.5 %first_back_0.1 = (bf16[512,768]{1,0:T(8,128)(2,1)}, bf16[512,3072]{1,0:T(8,128)(2,1)}, bf16[512,768]{1,0:T(8,128)(2,1)}, bf16[512,2304]{1,0:T(8,128)(2,1)}, f32...) custom-call(s32[1]{0:T(128)} %bitcast.refs_0_, ...), custom_call_target="tpu_custom_call", output_to_operand_aliasing={{0}: (12, {}), {1}: (13, {}), {2}: (14, {}), {3}: (15, {}),... | custom-call | flops 24999999488 | bytes 31457280 | tf_op jit(solution)/shard_map/first_back_0/pallas_call | solution.py:432
  255.9 15.4 %grads_6144_1.1.refs_11_.refs_6_ = bf16[288,32,768]{2,1,0:T(8,128)(2,1)} custom-call(s32[288]{0:T(512)S(1)} %get-tuple-element.240.code_ref, s32[288]{0:T(512)S(1)} %get-tuple-element.228.index_ref, bf16[512,3072]{1,0:T(8,128)(2,1)} %get-tuple-element.138.refs_0_, bf16[512,768]{1,0:T(8,128)(2,1)} %get-tuple-element.153.refs_1_, ...), custom_call_target="tpu_custom_call" | custom-call | flops 14495514624 | bytes 12582912 | tf_op jit(solution)/shard_map/grads_6144_1/pallas_call | solution.py:706
  272.6 25.8 %first_back_1.1 = (bf16[512,768]{1,0:T(8,128)(2,1)}, bf16[512,3072]{1,0:T(8,128)(2,1)}, bf16[512,768]{1,0:T(8,128)(2,1)}, bf16[512,2304]{1,0:T(8,128)(2,1)}, f32...) custom-call(s32[1]{0:T(128)} %bitcast.refs_0_, ...), custom_call_target="tpu_custom_call", output_to_operand_aliasing={{0}: (12, {}), {1}: (13, {}), {2}: (14, {}), {3}: (15, {}),... | custom-call | flops 24999999488 | bytes 31457280 | tf_op jit(solution)/shard_map/first_back_1/pallas_call | solution.py:432
  298.4 14.6 %grads_2304_0.1 = (bf16[96,32,768]{2,1,0:T(8,128)(2,1)}, bf16[96,32,768]{2,1,0:T(8,128)(2,1)}, bf16[96,32,768]{2,1,0:T(8,128)(2,1)}, bf16[96,32,768]{2,1,0:T(8,128)(2,1)}, bf16[496,32,768]{2,1,0:T(8,128)(2,1)}) custom-call(s32[288]{0:T(512)} %copy-done.1, s32[288]{0:T(512)} %copy-done, bf16[512,768]{1,0:T(8,128)(2,1)} %get-tuple-element.174.refs_0_, ...), custom_call_target="tpu_custom_call" | custom-call | flops 9663676416 | bytes 12582912 | tf_op jit(solution)/shard_map/grads_2304_0/pallas_call | solution.py:706
  313.0 1.3 collective-permute-start.4
  314.4 8.5 %grads_6144_0.1 = (bf16[96,32,768]{2,1,0:T(8,128)(2,1)}, bf16[96,32,768]{2,1,0:T(8,128)(2,1)}, bf16[496,32,768]{2,1,0:T(8,128)(2,1)}, bf16[96,32,768]{2,1,0:T(8,128)(2,1)}) custom-call(s32[288]{0:T(512)} %copy-done.1, s32[288]{0:T(512)} %copy-done, ...), custom_call_target="tpu_custom_call", output_to_operand_aliasing={{0}: (4, {}), {1}: (5, {}), {2}: (6, {}), {3}: (7, {})} | custom-call | flops 4831838208 | bytes 12582912 | tf_op jit(solution)/shard_map/grads_6144_0/pallas_call | solution.py:706
  324.4 3.0 hop.10
  327.4 2.0 collective-permute-start.5
  330.0 1.3 conditional.3
  330.1 1.3 broadcast.182
  331.4 2.9 hop.11
  334.2 1.6 collective-permute-done.5.refs_2_
  335.9 1.6 collective-permute-done.6.refs_3_
  338.2 3.8 hop.12
  342.6 1.1 collective-permute-start.9
  344.6 5.7 %all-to-all-start.1 = ((bf16[16,2,4608]{2,1,0:T(2,128)(2,1)}), bf16[16,2,4608]{2,1,0:T(2,128)(2,1)S(1)}, u32[]{:S(2)}, u32[]{:S(2)}) async-start(bf16[16,2,4608]{2,1,0:T(2,128)(2,1)} %broadcast_in_dim.99), calls=%async_computation.2 | async-start | bytes 589824 | tf_op jit(solution)/shard_map/all_to_all | solution.py:1025
  350.6 1.4 collective-permute-start.15
  353.6 12.4 %all-to-all-done.1.refs_4_ = bf16[16,2,4608]{2,1,0:T(2,128)(2,1)S(1)} async-done(((bf16[16,2,4608]{2,1,0:T(2,128)(2,1)}), bf16[16,2,4608]{2,1,0:T(2,128)(2,1)S(1)}, u32[]{:S(2)}, u32[]{:S(2)}) %all-to-all-start.1) | async-done | bytes 294944 | tf_op jit(solution)/shard_map/all_to_all | solution.py:1025
  366.0 1.0 collective-permute-done.16.refs_3_
  367.8 3.7 hop.16
  371.5 2.5 collective-permute-start.17
  375.6 3.9 hop.13
  379.6 1.5 collective-permute-start.10
  383.2 1.4 copy.71
  384.6 5.3 %adam_0.1 = (f32[31,32,768]{2,1,0:T(8,128)}, f32[31,32,768]{2,1,0:T(8,128)}, f32[31,32,768]{2,1,0:T(8,128)}, bf16[31,32,768]{2,1,0:T(8,128)(2,1)}) custom-call(s32[31]{0:T(128)} %get-tuple-element.239.code_ref, s32[31]{0:T(128)} %get-tuple-element.217.index_ref, s32[31]{0:T(128)} %get-tuple-element.238.row_ref, f32[31,32,768]{2,1,0:T(8,128)} %bitcast.52, ...), custom_call_target="tpu_custom_call" | custom-call | bytes 11427840 | tf_op jit(solution)/shard_map/adam_0/pallas_call | solution.py:808
  389.8 7.0 %collective-permute-done.10.refs_2_ = bf16[12,32,768]{2,1,0:T(8,128)(2,1)S(1)} collective-permute-done((bf16[12,32,768]{2,1,0:T(8,128)(2,1)}, bf16[12,32,768]{2,1,0:T(8,128)(2,1)S(1)}, u32[]{:S(2)}, u32[]{:S(2)}) %collective-permute-start.10) | collective-permute-done | bytes 589856 | tf_op jit(solution)/shard_map/ppermute | solution.py:836
  396.8 1.8 collective-permute-done.11.refs_3_
  399.5 3.9 hop.14
  403.4 1.2 collective-permute-start.12
  406.3 4.0 hop.17
  410.2 0.9 collective-permute-start.19
  411.8 3.3 collective-permute-done.12.refs_2_
  416.5 2.8 hop.15.refs_0_
  419.4 9.4 %collective-permute-start.14 = (bf16[12,32,768]{2,1,0:T(8,128)(2,1)}, bf16[12,32,768]{2,1,0:T(8,128)(2,1)S(1)}, u32[]{:S(2)}, u32[]{:S(2)}) collective-permute-start(bf16[12,32,768]{2,1,0:T(8,128)(2,1)} %hop.15.refs_0_), channel_id=1, source_target_pairs={{0,1},{1,0},{2,3},{3,2},{4,5},{5,4},{6,7},{7,6},{8,9},{9,8},{10,11... | collective-permute-start | bytes 1769480 | tf_op jit(solution)/shard_map/ppermute | solution.py:829
  430.4 4.0 hop.18
  436.7 5.7 %adam_2.1 = (f32[31,32,768]{2,1,0:T(8,128)}, f32[31,32,768]{2,1,0:T(8,128)}, f32[31,32,768]{2,1,0:T(8,128)}, bf16[31,32,768]{2,1,0:T(8,128)(2,1)}) custom-call(s32[31]{0:T(128)} %get-tuple-element.239.code_ref, s32[31]{0:T(128)} %get-tuple-element.217.index_ref, ...), custom_call_target="tpu_custom_call", output_to_operand_aliasing={{0}: (10, {}), {1}: (11, {}), {2}: (12, {}), {3}: (13, {})} | custom-call | bytes 11427840 | tf_op jit(solution)/shard_map/adam_2/pallas_call | solution.py:808
  442.4 3.3 collective-permute-done.21.refs_2_
  446.9 2.8 hop.19.refs_2_
  449.7 5.2 %collective-permute-start.23 = (bf16[12,32,768]{2,1,0:T(8,128)(2,1)}, bf16[12,32,768]{2,1,0:T(8,128)(2,1)S(1)}, u32[]{:S(2)}, u32[]{:S(2)}) collective-permute-start(bf16[12,32,768]{2,1,0:T(8,128)(2,1)} %hop.19.refs_2_), channel_id=1, source_target_pairs={{0,1},{1,0},{2,3},{3,2},{4,5},{5,4},{6,7},{7,6},{8,9},{9,8},{10,11... | collective-permute-start | bytes 1769480 | tf_op jit(solution)/shard_map/ppermute | solution.py:829
  454.9 1.8 collective-permute-done.23.refs_3_
  457.6 5.6 %adam_4.1 = (f32[31,32,768]{2,1,0:T(8,128)}, f32[31,32,768]{2,1,0:T(8,128)}, f32[31,32,768]{2,1,0:T(8,128)}, bf16[31,32,768]{2,1,0:T(8,128)(2,1)}) custom-call(s32[31]{0:T(128)} %get-tuple-element.239.code_ref, s32[31]{0:T(128)} %get-tuple-element.217.index_ref, ...), custom_call_target="tpu_custom_call", output_to_operand_aliasing={{0}: (13, {}), {1}: (14, {}), {2}: (15, {}), {3}: (16, {})} | custom-call | bytes 11427840 | tf_op jit(solution)/shard_map/adam_4/pallas_call | solution.py:808
  (164 shorter events, 30.2 us)
Async XLA Ops:
  7.2 112.9 %all-gather.5.cloned.1.call-start = ((), (), s32[]{:S(2)}) async-start(), calls=%async_computation.5 | async-start | bytes 20889600 | tf_op jit(solution)/shard_map/all_gather | solution.py:962
  10.4 2.3 copy-start.42
  10.5 2.5 copy-start.37
  15.4 107.2 %copy-start.24 = (s32[432]{0:T(512)}, s32[432]{0:T(512)S(1)}, u32[]{:S(2)}) copy-start(s32[432]{0:T(512)S(1)} %convert_reduce_fusion) | copy-start | bytes 5188
  60.6 62.0 %copy-start.30 = (f32[34]{0:T(128)}, f32[34]{0:T(128)S(1)}, u32[]{:S(2)}) copy-start(f32[34]{0:T(128)S(1)} %pmax.7) | copy-start | bytes 412
  60.8 61.8 %copy-start.26 = (f32[384]{0:T(512)}, f32[384]{0:T(512)S(1)}, u32[]{:S(2)}) copy-start(f32[384]{0:T(512)S(1)} %multiply_exponential_fusion) | copy-start | bytes 4612
  62.4 15.2 %all-to-all-start = ((f32[16,2,992]{2,1,0:T(2,128)}), f32[16,2,992]{2,1,0:T(2,128)S(1)}, u32[]{:S(2)}, u32[]{:S(2)}) async-start(f32[16,2,992]{2,1,0:T(2,128)} %copy.67), calls=%async_computation.1 | async-start | bytes 262144 | tf_op jit(solution)/shard_map/all_to_all | solution.py:986
  69.6 186.3 %copy-start = (s32[288]{0:T(512)}, s32[288]{0:T(512)S(1)}, u32[]{:S(2)}) copy-start(s32[288]{0:T(512)S(1)} %get-tuple-element.228.index_ref) | copy-start | bytes 3460
  69.6 186.3 %copy-start.1 = (s32[288]{0:T(512)}, s32[288]{0:T(512)S(1)}, u32[]{:S(2)}) copy-start(s32[288]{0:T(512)S(1)} %get-tuple-element.240.code_ref) | copy-start | bytes 3460
  149.3 20.4 %collective-permute-start.1 = (bf16[512,768]{1,0:T(8,128)(2,1)}, bf16[512,768]{1,0:T(8,128)(2,1)S(1)}, u32[]{:S(2)}, u32[]{:S(2)}) collective-permute-start(bf16[512,768]{1,0:T(8,128)(2,1)} %get-tuple-element.122), channel_id=1, source_target_pairs={{0,16},{1,17},{2,18},{3,19},{4,20},{5,21},{6,22},{7,23},{8,24},{9,... | collective-permute-start | bytes 2359304 | tf_op jit(solution)/shard_map/ppermute | solution.py:1003
  168.4 18.6 %collective-permute-start = (bf16[512,768]{1,0:T(8,128)(2,1)}, bf16[512,768]{1,0:T(8,128)(2,1)S(1)}, u32[]{:S(2)}, u32[]{:S(2)}) collective-permute-start(bf16[512,768]{1,0:T(8,128)(2,1)} %get-tuple-element.117), channel_id=1, source_target_pairs={{0,16},{1,17},{2,18},{3,19},{4,20},{5,21},{6,22},{7,23},{8,24},{9,... | collective-permute-start | bytes 2359304 | tf_op jit(solution)/shard_map/ppermute | solution.py:1003
  169.7 0.9 copy-start.41
  185.6 43.9 %collective-permute-start.3 = (bf16[512,768]{1,0:T(8,128)(2,1)}, bf16[512,768]{1,0:T(8,128)(2,1)S(1)}, u32[]{:S(2)}, u32[]{:S(2)}) collective-permute-start(bf16[512,768]{1,0:T(8,128)(2,1)} %get-tuple-element.139), channel_id=1, source_target_pairs={{16,0},{17,1},{18,2},{19,3},{20,4},{21,5},{22,6},{23,7},{24,8},{25... | collective-permute-start | bytes 2359304 | tf_op jit(solution)/shard_map/ppermute | solution.py:1009
  187.0 0.9 copy-start.40
  202.9 68.8 %collective-permute-start.2 = (bf16[512,768]{1,0:T(8,128)(2,1)}, bf16[512,768]{1,0:T(8,128)(2,1)S(1)}, u32[]{:S(2)}, u32[]{:S(2)}) collective-permute-start(bf16[512,768]{1,0:T(8,128)(2,1)} %get-tuple-element.131), channel_id=1, source_target_pairs={{16,0},{17,1},{18,2},{19,3},{20,4},{21,5},{22,6},{23,7},{24,8},{25... | collective-permute-start | bytes 2359304 | tf_op jit(solution)/shard_map/ppermute | solution.py:1009
  229.5 0.9 copy-start.39
  271.7 0.9 copy-start.38
  313.0 11.3 %collective-permute-start.4 = (bf16[96,32,768]{2,1,0:T(8,128)(2,1)}, bf16[96,32,768]{2,1,0:T(8,128)(2,1)}, u32[]{:S(2)}, u32[]{:S(2)}) collective-permute-start(bf16[96,32,768]{2,1,0:T(8,128)(2,1)} %get-tuple-element.185), channel_id=1, source_target_pairs={{0,1},{1,0},{2,3},{3,2},{4,5},{5,4},{6,7},{7,6},{8,9},{9,8},{10,11... | collective-permute-start | bytes 14155784 | tf_op jit(solution)/shard_map/ppermute | solution.py:829
  322.9 8.5 %collective-permute-start.7 = (bf16[96,32,768]{2,1,0:T(8,128)(2,1)}, bf16[96,32,768]{2,1,0:T(8,128)(2,1)}, u32[]{:S(2)}, u32[]{:S(2)}) collective-permute-start(bf16[96,32,768]{2,1,0:T(8,128)(2,1)} %get-tuple-element.190), channel_id=1, source_target_pairs={{0,1},{1,0},{2,3},{3,2},{4,5},{5,4},{6,7},{7,6},{8,9},{9,8},{10,11... | collective-permute-start | bytes 14155784 | tf_op jit(solution)/shard_map/ppermute | solution.py:829
  324.3 5.5 %copy-start.28 = (f32[4,768]{1,0:T(4,128)S(1)}, f32[4,768]{1,0:T(4,128)}, u32[]{:S(2)}) copy-start(f32[4,768]{1,0:T(4,128)} %get-tuple-element.171) | copy-start | bytes 36868
  324.3 5.6 %copy-start.34 = (f32[2,768]{1,0:T(2,128)S(1)}, f32[2,768]{1,0:T(2,128)}, u32[]{:S(2)}) copy-start(f32[2,768]{1,0:T(2,128)} %get-tuple-element.170) | copy-start | bytes 18436
  324.3 5.6 %copy-start.29 = (f32[4,768]{1,0:T(4,128)S(1)}, f32[4,768]{1,0:T(4,128)}, u32[]{:S(2)}) copy-start(f32[4,768]{1,0:T(4,128)} %get-tuple-element.169) | copy-start | bytes 36868
  324.4 5.6 %copy-start.35 = (f32[2,768]{1,0:T(2,128)S(1)}, f32[2,768]{1,0:T(2,128)}, u32[]{:S(2)}) copy-start(f32[2,768]{1,0:T(2,128)} %get-tuple-element.168) | copy-start | bytes 18436
  327.4 8.5 %collective-permute-start.5 = (bf16[6,32,768]{2,1,0:T(8,128)(2,1)}, bf16[6,32,768]{2,1,0:T(8,128)(2,1)S(1)}, u32[]{:S(2)}, u32[]{:S(2)}) collective-permute-start(bf16[6,32,768]{2,1,0:T(8,128)(2,1)} %get-tuple-element.186), channel_id=1, source_target_pairs={{0,4},{1,5},{4,8},{5,9},{8,12},{9,13},{12,14},{13,15},{14,10},{15,... | collective-permute-start | bytes 884744 | tf_op jit(solution)/shard_map/ppermute | solution.py:836
  329.3 8.1 %collective-permute-start.6 = (bf16[6,32,768]{2,1,0:T(8,128)(2,1)}, bf16[6,32,768]{2,1,0:T(8,128)(2,1)S(1)}, u32[]{:S(2)}, u32[]{:S(2)}) collective-permute-start(bf16[6,32,768]{2,1,0:T(8,128)(2,1)} %get-tuple-element.187), channel_id=1, source_target_pairs={{0,2},{1,3},{4,0},{5,1},{8,4},{9,5},{12,8},{13,9},{14,12},{15,13},... | collective-permute-start | bytes 884744 | tf_op jit(solution)/shard_map/ppermute | solution.py:836
  335.8 1.6 copy-start.18
  338.1 12.2 %copy-start.27 = (f32[384]{0:T(512)S(1)}, f32[384]{0:T(512)}, u32[]{:S(2)}) copy-start(f32[384]{0:T(512)} %copy-done.26) | copy-start | bytes 4612
  338.2 12.2 %copy-start.31 = (f32[34]{0:T(128)S(1)}, f32[34]{0:T(128)}, u32[]{:S(2)}) copy-start(f32[34]{0:T(128)} %copy-done.30) | copy-start | bytes 412
  338.2 12.5 %copy-start.21 = (bf16[6,32,768]{2,1,0:T(8,128)(2,1)S(1)}, bf16[6,32,768]{2,1,0:T(8,128)(2,1)}, u32[]{:S(2)}) copy-start(bf16[6,32,768]{2,1,0:T(8,128)(2,1)} %get-tuple-element.191.refs_5_) | copy-start | bytes 884740
  338.2 13.9 %copy-start.20 = (bf16[6,32,768]{2,1,0:T(8,128)(2,1)S(1)}, bf16[6,32,768]{2,1,0:T(8,128)(2,1)}, u32[]{:S(2)}) copy-start(bf16[6,32,768]{2,1,0:T(8,128)(2,1)} %get-tuple-element.192.refs_6_) | copy-start | bytes 884740
  338.2 15.3 %copy-start.25 = (s32[432]{0:T(512)S(1)}, s32[432]{0:T(512)}, u32[]{:S(2)}) copy-start(s32[432]{0:T(512)} %copy-done.24) | copy-start | bytes 5188
  338.2 15.3 %copy-start.36 = (pred[432]{0:T(512)(128)(4,1)S(1)}, pred[432]{0:T(512)(128)(4,1)}, u32[]{:S(2)}) copy-start(pred[432]{0:T(512)(128)(4,1)} %get-tuple-element.223) | copy-start | bytes 1300
  342.0 32.0 %collective-permute-start.8 = (bf16[12,32,768]{2,1,0:T(8,128)(2,1)}, bf16[12,32,768]{2,1,0:T(8,128)(2,1)S(1)}, u32[]{:S(2)}, u32[]{:S(2)}) collective-permute-start(bf16[12,32,768]{2,1,0:T(8,128)(2,1)} %get-tuple-element.193), channel_id=1, source_target_pairs={{0,4},{1,5},{4,8},{5,9},{8,12},{9,13},{12,14},{13,15},{14,10},{15,... | collective-permute-start | bytes 1769480 | tf_op jit(solution)/shard_map/ppermute | solution.py:836
  342.6 31.4 %collective-permute-start.9 = (bf16[12,32,768]{2,1,0:T(8,128)(2,1)}, bf16[12,32,768]{2,1,0:T(8,128)(2,1)S(1)}, u32[]{:S(2)}, u32[]{:S(2)}) collective-permute-start(bf16[12,32,768]{2,1,0:T(8,128)(2,1)} %get-tuple-element.194), channel_id=1, source_target_pairs={{0,2},{1,3},{4,0},{5,1},{8,4},{9,5},{12,8},{13,9},{14,12},{15,13},... | collective-permute-start | bytes 1769480 | tf_op jit(solution)/shard_map/ppermute | solution.py:836
  344.6 21.4 %all-to-all-start.1 = ((bf16[16,2,4608]{2,1,0:T(2,128)(2,1)}), bf16[16,2,4608]{2,1,0:T(2,128)(2,1)S(1)}, u32[]{:S(2)}, u32[]{:S(2)}) async-start(bf16[16,2,4608]{2,1,0:T(2,128)(2,1)} %broadcast_in_dim.99), calls=%async_computation.2 | async-start | bytes 589824 | tf_op jit(solution)/shard_map/all_to_all | solution.py:1025
  350.6 15.4 %collective-permute-start.15 = (bf16[6,32,768]{2,1,0:T(8,128)(2,1)S(1)}, bf16[6,32,768]{2,1,0:T(8,128)(2,1)S(1)}, u32[]{:S(2)}, u32[]{:S(2)}) collective-permute-start(bf16[6,32,768]{2,1,0:T(8,128)(2,1)S(1)} %copy-done.21), channel_id=1, source_target_pairs={{0,4},{1,5},{4,8},{5,9},{8,12},{9,13},{12,14},{13,15},{14,10},{15,... | collective-permute-start | bytes 884744 | tf_op jit(solution)/shard_map/ppermute | solution.py:836
  352.1 14.9 %collective-permute-start.16 = (bf16[6,32,768]{2,1,0:T(8,128)(2,1)S(1)}, bf16[6,32,768]{2,1,0:T(8,128)(2,1)S(1)}, u32[]{:S(2)}, u32[]{:S(2)}) collective-permute-start(bf16[6,32,768]{2,1,0:T(8,128)(2,1)S(1)} %copy-done.20), channel_id=1, source_target_pairs={{0,2},{1,3},{4,0},{5,1},{8,4},{9,5},{12,8},{13,9},{14,12},{15,13},... | collective-permute-start | bytes 884744 | tf_op jit(solution)/shard_map/ppermute | solution.py:836
  366.0 1.0 copy-start.2
  366.0 1.0 copy-start.22
  371.5 33.7 %collective-permute-start.17 = (bf16[12,32,768]{2,1,0:T(8,128)(2,1)}, bf16[12,32,768]{2,1,0:T(8,128)(2,1)S(1)}, u32[]{:S(2)}, u32[]{:S(2)}) collective-permute-start(bf16[12,32,768]{2,1,0:T(8,128)(2,1)} %get-tuple-element.199), channel_id=1, source_target_pairs={{0,4},{1,5},{4,8},{5,9},{8,12},{9,13},{12,14},{13,15},{14,10},{15,... | collective-permute-start | bytes 1769480 | tf_op jit(solution)/shard_map/ppermute | solution.py:836
  374.0 7.8 %copy-start.32 = (s32[288]{0:T(512)S(1)}, s32[288]{0:T(512)}, u32[]{:S(2)}) copy-start(s32[288]{0:T(512)} %get-tuple-element.219) | copy-start | bytes 3460
  374.0 7.8 %copy-start.33 = (s32[288]{0:T(512)S(1)}, s32[288]{0:T(512)}, u32[]{:S(2)}) copy-start(s32[288]{0:T(512)} %get-tuple-element.227) | copy-start | bytes 3460
  374.0 9.1 %copy-start.3 = (bf16[16,2,4608]{2,1,0:T(2,128)(2,1)S(1)}, bf16[16,2,4608]{2,1,0:T(2,128)(2,1)}, u32[]{:S(2)}) copy-start(bf16[16,2,4608]{2,1,0:T(2,128)(2,1)} %copy-done.2) | copy-start | bytes 884740
  374.0 31.3 %collective-permute-start.18 = (bf16[12,32,768]{2,1,0:T(8,128)(2,1)}, bf16[12,32,768]{2,1,0:T(8,128)(2,1)S(1)}, u32[]{:S(2)}, u32[]{:S(2)}) collective-permute-start(bf16[12,32,768]{2,1,0:T(8,128)(2,1)} %get-tuple-element.200), channel_id=1, source_target_pairs={{0,2},{1,3},{4,0},{5,1},{8,4},{9,5},{12,8},{13,9},{14,12},{15,13},... | collective-permute-start | bytes 1769480 | tf_op jit(solution)/shard_map/ppermute | solution.py:836
  379.6 17.2 %collective-permute-start.10 = (bf16[12,32,768]{2,1,0:T(8,128)(2,1)}, bf16[12,32,768]{2,1,0:T(8,128)(2,1)S(1)}, u32[]{:S(2)}, u32[]{:S(2)}) collective-permute-start(bf16[12,32,768]{2,1,0:T(8,128)(2,1)} %get-tuple-element.195), channel_id=1, source_target_pairs={{0,4},{1,5},{4,8},{5,9},{8,12},{9,13},{12,14},{13,15},{14,10},{15,... | collective-permute-start | bytes 1769480 | tf_op jit(solution)/shard_map/ppermute | solution.py:836
  381.1 17.6 %collective-permute-start.11 = (bf16[12,32,768]{2,1,0:T(8,128)(2,1)}, bf16[12,32,768]{2,1,0:T(8,128)(2,1)S(1)}, u32[]{:S(2)}, u32[]{:S(2)}) collective-permute-start(bf16[12,32,768]{2,1,0:T(8,128)(2,1)} %get-tuple-element.196), channel_id=1, source_target_pairs={{0,2},{1,3},{4,0},{5,1},{8,4},{9,5},{12,8},{13,9},{14,12},{15,13},... | collective-permute-start | bytes 1769480 | tf_op jit(solution)/shard_map/ppermute | solution.py:836
  396.8 1.8 copy-start.14
  398.6 0.8 copy-start.15
  403.4 11.6 %collective-permute-start.12 = (bf16[12,32,768]{2,1,0:T(8,128)(2,1)}, bf16[12,32,768]{2,1,0:T(8,128)(2,1)S(1)}, u32[]{:S(2)}, u32[]{:S(2)}) collective-permute-start(bf16[12,32,768]{2,1,0:T(8,128)(2,1)} %get-tuple-element.197), channel_id=1, source_target_pairs={{0,4},{1,5},{4,8},{5,9},{8,12},{9,13},{12,14},{13,15},{14,10},{15,... | collective-permute-start | bytes 1769480 | tf_op jit(solution)/shard_map/ppermute | solution.py:836
  404.6 11.1 %collective-permute-start.13 = (bf16[12,32,768]{2,1,0:T(8,128)(2,1)}, bf16[12,32,768]{2,1,0:T(8,128)(2,1)S(1)}, u32[]{:S(2)}, u32[]{:S(2)}) collective-permute-start(bf16[12,32,768]{2,1,0:T(8,128)(2,1)} %get-tuple-element.198), channel_id=1, source_target_pairs={{0,2},{1,3},{4,0},{5,1},{8,4},{9,5},{12,8},{13,9},{14,12},{15,13},... | collective-permute-start | bytes 1769480 | tf_op jit(solution)/shard_map/ppermute | solution.py:836
  405.2 0.8 copy-start.5
  405.2 1.0 copy-start.6
  410.2 18.5 %collective-permute-start.19 = (bf16[12,32,768]{2,1,0:T(8,128)(2,1)}, bf16[12,32,768]{2,1,0:T(8,128)(2,1)S(1)}, u32[]{:S(2)}, u32[]{:S(2)}) collective-permute-start(bf16[12,32,768]{2,1,0:T(8,128)(2,1)} %get-tuple-element.202), channel_id=1, source_target_pairs={{0,4},{1,5},{4,8},{5,9},{8,12},{9,13},{12,14},{13,15},{14,10},{15,... | collective-permute-start | bytes 1769480 | tf_op jit(solution)/shard_map/ppermute | solution.py:836
  411.1 17.6 %collective-permute-start.20 = (bf16[12,32,768]{2,1,0:T(8,128)(2,1)}, bf16[12,32,768]{2,1,0:T(8,128)(2,1)S(1)}, u32[]{:S(2)}, u32[]{:S(2)}) collective-permute-start(bf16[12,32,768]{2,1,0:T(8,128)(2,1)} %get-tuple-element.203), channel_id=1, source_target_pairs={{0,2},{1,3},{4,0},{5,1},{8,4},{9,5},{12,8},{13,9},{14,12},{15,13},... | collective-permute-start | bytes 1769480 | tf_op jit(solution)/shard_map/ppermute | solution.py:836
  419.4 16.5 %collective-permute-start.14 = (bf16[12,32,768]{2,1,0:T(8,128)(2,1)}, bf16[12,32,768]{2,1,0:T(8,128)(2,1)S(1)}, u32[]{:S(2)}, u32[]{:S(2)}) collective-permute-start(bf16[12,32,768]{2,1,0:T(8,128)(2,1)} %hop.15.refs_0_), channel_id=1, source_target_pairs={{0,1},{1,0},{2,3},{3,2},{4,5},{5,4},{6,7},{7,6},{8,9},{9,8},{10,11... | collective-permute-start | bytes 1769480 | tf_op jit(solution)/shard_map/ppermute | solution.py:829
  428.7 0.8 copy-start.16
  429.5 0.8 copy-start.17
  434.3 11.4 %collective-permute-start.21 = (bf16[12,32,768]{2,1,0:T(8,128)(2,1)}, bf16[12,32,768]{2,1,0:T(8,128)(2,1)S(1)}, u32[]{:S(2)}, u32[]{:S(2)}) collective-permute-start(bf16[12,32,768]{2,1,0:T(8,128)(2,1)} %get-tuple-element.204), channel_id=1, source_target_pairs={{0,4},{1,5},{4,8},{5,9},{8,12},{9,13},{12,14},{13,15},{14,10},{15,... | collective-permute-start | bytes 1769480 | tf_op jit(solution)/shard_map/ppermute | solution.py:836
  435.2 10.8 %collective-permute-start.22 = (bf16[12,32,768]{2,1,0:T(8,128)(2,1)}, bf16[12,32,768]{2,1,0:T(8,128)(2,1)S(1)}, u32[]{:S(2)}, u32[]{:S(2)}) collective-permute-start(bf16[12,32,768]{2,1,0:T(8,128)(2,1)} %get-tuple-element.205), channel_id=1, source_target_pairs={{0,2},{1,3},{4,0},{5,1},{8,4},{9,5},{12,8},{13,9},{14,12},{15,13},... | collective-permute-start | bytes 1769480 | tf_op jit(solution)/shard_map/ppermute | solution.py:836
  435.9 0.8 copy-start.4
  445.8 0.8 copy-start.9
  446.0 0.9 copy-start.10
  449.7 7.0 %collective-permute-start.23 = (bf16[12,32,768]{2,1,0:T(8,128)(2,1)}, bf16[12,32,768]{2,1,0:T(8,128)(2,1)S(1)}, u32[]{:S(2)}, u32[]{:S(2)}) collective-permute-start(bf16[12,32,768]{2,1,0:T(8,128)(2,1)} %hop.19.refs_2_), channel_id=1, source_target_pairs={{0,1},{1,0},{2,3},{3,2},{4,5},{5,4},{6,7},{7,6},{8,9},{9,8},{10,11... | collective-permute-start | bytes 1769480 | tf_op jit(solution)/shard_map/ppermute | solution.py:829
  456.7 0.9 copy-start.11
  (6 other events, 4.7 us)
Sparse Core Ops, SparseCore 0:
  11.7 108.3 all-gather.4
